TPU v7x, 32 devices: a whole 2x2x4 slice. The times are simulated.
32 devices in a mesh: member: 2 (over y), tile: 4 (over z), nest: 2 (over x), lev: 2 (over core).
Axes of the slice: x: 2, y: 2, z: 4, core: 2. Of those that a mesh axis runs over, the one named last changes fastest.
Arguments:
- parent_field: float32 [10, 2, 256, 512], P('member', None, 'tile', ('nest', 'lev')), parts along dimension 0, may hold values from -6 to 6
- nest_fields: float32 [12, 5, 2, 384, 384], P(('member', 'nest'), None, None, 'tile', 'lev'), parts along dimension 0, may hold values from -6 to 6
- lateral_rate: float32 [5], replicated, may hold values from 0.02 to 0.12
- vertical_rate: float32 [5], replicated, may hold values from 0.02 to 0.12
- centres: int32 [6, 6, 2], P('member'), parts along dimension 0, may hold values from 64 to 448, as said below
- slot_storm: int32 [12], P('member'), parts along dimension 0, may hold values from 0 to 5, each once
Outputs:
- parent_final: float32 [10, 2, 256, 512], P('member', None, 'tile', ('nest', 'lev')), parts along dimension 0
- nest_final: float32 [12, 5, 2, 384, 384], P(('member', 'nest'), None, None, 'tile', 'lev'), parts along dimension 0
There are 2 independent parts, one for each index of `member`. A program takes and returns all parts, laid end to end along the dimension named above; an argument that names none is the same for every part. Nothing has to cross between parts.
Inputs may be any that keep to these rules, and one draw needn't show every extreme that they name: `centres`: from one step to the next the row of a centre changes by 1 to 2 cells in either direction and the column by at most 2 cells; rows stay within 64 to 192 and columns within 64 to 448. `slot_storm`: every storm occupies exactly one nest position.
All inputs are finite; a program needn't handle non-finite values.
Results may differ from a plain program's by a relative error of at most 0.0003.
Values sent between devices are 32-bit elements; how exact they have to be, the bound alone decides.
A program may use at most 128 MiB of HBM per device.

v0:
```python
import jax
import jax.numpy as jnp
from jax import lax
from jax.sharding import PartitionSpec as P

FP = 128
BWP = 2
MOVE = 2


def extended(cells, sides, width):
    for axis, dim in sides:
        count = lax.axis_size(axis)
        ends = count - 1
        head = lax.slice_in_dim(cells, 0, width, axis=dim)
        tail = lax.slice_in_dim(cells, cells.shape[dim] - width, cells.shape[dim], axis=dim)
        cells = jnp.concatenate(
            [
                lax.ppermute(tail, axis, [(i, (i + 1) % count) for i in range(ends)]),
                cells,
                lax.ppermute(head, axis, [((i + 1) % count, i) for i in range(ends)]),
            ],
            axis=dim,
        )
    return cells


def tendency(padded, lateral_rate, vertical_rate):
    centre = padded[..., 1:-1, 1:-1, 1:-1]
    lateral = (
        padded[..., 1:-1, 2:, 1:-1]
        + padded[..., 1:-1, :-2, 1:-1]
        + padded[..., 1:-1, 1:-1, 2:]
        + padded[..., 1:-1, 1:-1, :-2]
        - 4.0 * centre
    )
    upright = padded[..., 2:, 1:-1, 1:-1] + padded[..., :-2, 1:-1, 1:-1] - 2.0 * centre
    change = (
        lateral_rate[:, None, None, None] * lateral + vertical_rate[:, None, None, None] * upright
    )
    return (centre, change)


def select_rows(picker, table):
    return jnp.sum(picker[:, :, None] * table[None, :, :], axis=1)


def column_block():
    return lax.axis_index("nest") * lax.axis_size("lev") + lax.axis_index("lev")


def extract(parent_now, anchors):
    fields, level_count, parent_rows, parent_cols = parent_now.shape
    padded = jnp.pad(parent_now, ((0, 0), (0, 0), (FP, FP), (FP, FP)))
    rel_rows = anchors[:, 0] - lax.axis_index("tile") * parent_rows + FP
    rel_cols = anchors[:, 1] - column_block() * parent_cols + FP
    zero_index = jnp.zeros((), jnp.int32)

    def single(corner):
        row_at = corner[0]
        col_at = corner[1]
        within = (
            (row_at >= 0)
            & (row_at <= FP + parent_rows)
            & (col_at >= 0)
            & (col_at <= FP + parent_cols)
        )
        row_at = jnp.clip(row_at, 0, FP + parent_rows)
        col_at = jnp.clip(col_at, 0, FP + parent_cols)
        south = lax.dynamic_slice(
            padded, (zero_index, zero_index, row_at, col_at), (fields, level_count, BWP, FP)
        )
        north = lax.dynamic_slice(
            padded,
            (zero_index, zero_index, row_at + FP - BWP, col_at),
            (fields, level_count, BWP, FP),
        )
        west = lax.dynamic_slice(
            padded, (zero_index, zero_index, row_at, col_at), (fields, level_count, FP, BWP)
        )
        east = lax.dynamic_slice(
            padded,
            (zero_index, zero_index, row_at, col_at + FP - BWP),
            (fields, level_count, FP, BWP),
        )
        sides = jnp.stack(
            [south, north, jnp.swapaxes(west, 2, 3), jnp.swapaxes(east, 2, 3)], axis=2
        )
        return jnp.where(within, sides.reshape(fields, level_count, 4 * BWP * FP), 0.0)

    corners = jnp.stack([rel_rows, rel_cols], axis=1)
    return lax.map(single, corners)


def per_device(parent_field, nest_fields, lateral_rate, vertical_rate, centres, slot_storm):
    fields, level_count, parent_rows, parent_cols = parent_field.shape
    slot_count = nest_fields.shape[0]
    strip_rows = nest_fields.shape[3]
    strip_cols = nest_fields.shape[4]
    storm_count = slot_storm.shape[0]
    steps_total = centres.shape[0] - 1
    tile_at = lax.axis_index("tile")
    nest_at = lax.axis_index("nest")
    lev_at = lax.axis_index("lev")
    nest_span = 3 * FP
    reach_rows = 3 * MOVE
    border = 3 * BWP
    zero_index = jnp.zeros((), jnp.int32)
    storm_ids = jnp.arange(storm_count, dtype=jnp.int32)
    pick_all = (slot_storm[:, None] == storm_ids[None, :]).astype(jnp.int32)
    owned = lax.dynamic_slice_in_dim(slot_storm, nest_at * slot_count, slot_count)
    pick_own = (owned[:, None] == storm_ids[None, :]).astype(jnp.int32)
    global_rows = tile_at * strip_rows + jnp.arange(strip_rows, dtype=jnp.int32)
    global_cols = lev_at * strip_cols + jnp.arange(strip_cols, dtype=jnp.int32)
    row_gap = jnp.minimum(global_rows, nest_span - 1 - global_rows)
    col_gap = jnp.minimum(global_cols, nest_span - 1 - global_cols)
    distance = jnp.minimum(row_gap[:, None], col_gap[None, :])
    weight = jnp.maximum(border - distance, 0).astype(jnp.float32) / jnp.float32(border)
    inside = (distance >= 1).astype(jnp.float32)
    coarse_rows = global_rows // 3
    coarse_cols = global_cols // 3
    south_index = jnp.clip(coarse_rows, 0, BWP - 1)
    north_index = jnp.clip(coarse_rows - (FP - BWP), 0, BWP - 1)
    west_index = jnp.clip(coarse_cols, 0, BWP - 1)
    east_index = jnp.clip(coarse_cols - (FP - BWP), 0, BWP - 1)
    near_south = (coarse_rows < BWP)[:, None]
    near_north = (coarse_rows >= FP - BWP)[:, None]
    near_west = (coarse_cols < BWP)[None, :]
    near_east = (coarse_cols >= FP - BWP)[None, :]

    def relocate(single, offset):
        return lax.dynamic_slice(
            single,
            (zero_index, zero_index, reach_rows + offset[0], reach_rows + offset[1]),
            (fields, level_count, strip_rows, strip_cols),
        )

    def across(zone, zone_index):
        picked = jnp.take(zone, zone_index, axis=3)
        return jnp.take(picked, coarse_cols, axis=4)

    def along(zone, zone_index):
        picked = jnp.take(zone, zone_index, axis=3)
        picked = jnp.take(picked, coarse_rows, axis=4)
        return jnp.swapaxes(picked, 3, 4)

    parent_now = parent_field
    nests_now = nest_fields
    for step_index in range(steps_total):
        padded = extended(parent_now, (("tile", 2), (("nest", "lev"), 3)), 1)
        padded = jnp.pad(padded, ((0, 0), (1, 1), (0, 0), (0, 0)))
        centre, change = tendency(padded, lateral_rate, vertical_rate)
        parent_now = centre + change
        later_pos = select_rows(pick_all, centres[step_index + 1])
        anchors = later_pos - FP // 2
        terms = extract(parent_now, anchors)
        totals = lax.psum(terms, ("tile", "nest", "lev"))
        boundary = lax.dynamic_slice_in_dim(totals, nest_at * slot_count, slot_count, 0)
        boundary = boundary.reshape(slot_count, fields, level_count, 4, BWP, FP)
        south_full = across(boundary[:, :, :, 0], south_index)
        north_full = across(boundary[:, :, :, 1], north_index)
        west_full = along(boundary[:, :, :, 2], west_index)
        east_full = along(boundary[:, :, :, 3], east_index)
        sides_full = jnp.where(near_west, west_full, jnp.where(near_east, east_full, 0.0))
        driving = jnp.where(near_south, south_full, jnp.where(near_north, north_full, sides_full))
        own_later = select_rows(pick_own, centres[step_index + 1])
        own_before = select_rows(pick_own, centres[step_index])
        offsets = 3 * (own_later - own_before)
        widened_nests = extended(nests_now, (("tile", 3), ("lev", 4)), reach_rows)
        shifted = jax.vmap(relocate)(widened_nests, offsets)
        source_rows = global_rows[None, :] + offsets[:, 0:1]
        source_cols = global_cols[None, :] + offsets[:, 1:2]
        rows_fine = (source_rows >= 0) & (source_rows < nest_span)
        cols_fine = (source_cols >= 0) & (source_cols < nest_span)
        keep_mask = (rows_fine[:, :, None] & cols_fine[:, None, :])[:, None, None, :, :]
        retained = jnp.where(keep_mask, shifted, driving)
        relaxed = retained + weight * (driving - retained)
        bordered = extended(relaxed, (("tile", 3), ("lev", 4)), 1)
        bordered = jnp.pad(bordered, ((0, 0), (0, 0), (1, 1), (0, 0), (0, 0)))
        centre, change = tendency(bordered, lateral_rate, vertical_rate)
        nests_now = relaxed + inside * change
    return (parent_now, nests_now)


def solution(mesh):
    placed = (
        P("member", None, "tile", ("nest", "lev")),
        P(("member", "nest"), None, None, "tile", "lev"),
        P(),
        P(),
        P("member", None, None),
        P("member"),
    )
    return jax.shard_map(
        per_device,
        mesh=mesh,
        in_specs=placed,
        out_specs=(
            P("member", None, "tile", ("nest", "lev")),
            P(("member", "nest"), None, None, "tile", "lev"),
        ),
        check_vma=False,
    )
```

profile of v0, /device:TPU:0, one launch (start us, length us, event | category | flops | bytes accessed | tf_op | source)
XLA Modules:
  0.0 790.8 jit_solution(10287252542518076452)
XLA Ops:
  65.0 49.2 %while.32 = (s32[]{:T(128)}, f32[6,5,2,1024]{3,2,1,0:T(2,128)S(1)}, s32[6,2]{0,1:T(2,128)S(1)}, f32[5,2,320,384]{2,3,1,0:T(8,128)}, s32[]{:T(128)}, /*index=5*/s...) while((s32[]{:T(128)}, f32[6,5,2,1024]{3,2,1,0:T(2,128)S(1)}, ...), condition=%wide.region_5.6_spmd, body=%wide.region_4.5_spmd.sunk | while | flops 40981 | bytes 450935 | solution.py:92
  137.1 49.5 %while.33 = (s32[]{:T(128)}, f32[6,5,2,1024]{3,2,1,0:T(2,128)S(1)}, s32[6,2]{0,1:T(2,128)S(1)}, f32[5,2,320,384]{2,3,1,0:T(8,128)}, s32[]{:T(128)}, /*index=5*/s...) while((s32[]{:T(128)}, f32[6,5,2,1024]{3,2,1,0:T(2,128)S(1)}, ...), condition=%wide.region_9.14_spmd, body=%wide.region_8.13_spmd.sunk | while | flops 40981 | bytes 450935 | solution.py:92
  197.9 13.3 %while.34 = (s32[]{:T(128)}, f32[3,5,2,108,204]{3,2,4,1,0:T(2,128)S(1)}, s32[3,5]{1,0:T(4,128)S(1)}, f32[3,5,2,96,192]{3,2,1,0,4:T(2,128)}, s32[]{:T(128)}) while((s32[]{:T(128)}, f32[3,5,2,108,204]{3,2,4,1,0:T(2,128)S(1)}, s32[3,5]{1,0:T(4,128)S(1)}, f32[3,5,2,96,192]{3,2,1,0,4:T(2,128)}, s32[]{:T(128)}) %tuple.212), condition=%wide.while_cond, body=%wide.while_body.sunk | while | flops 2 | bytes 1967757 | solution.py:132
  211.2 70.3 %all-reduce.9.cloned.1.call-done = (f32[6,5,2,1024]{3,2,1,0:T(2,128)}, f32[6,5,2,1024]{3,2,1,0:T(2,128)}) async-done(((f32[6,5,2,1024]{3,2,1,0:T(2,128)}, f32[6,5,2,1024]{3,2,1,0:T(2,128)}), (f32[6,5,2,1024]{3,2,1,0:T(2,128)}, f32[6,5,2,1024]{3,2,1,0:T(2,128)})) %all-reduce.9.cloned.1.call-update) | async-done | bytes 491536 | tf_op jit(solution)/shard_map/psum | solution.py:157
  283.0 12.2 %gather_fusion.14 = f32[192,3,5,2,128]{4,3,2,1,0:T(2,128)S(1)} fusion(f32[3,5,2,2,128]{4,2,3,1,0:T(2,128)S(1)} %bitcast.166, s32[1024]{0:T(1024)S(1)} %pad_clamp_fusion), kind=kCustom, calls=%fused_computation.12.clone | custom fusion | bytes 5899008 | tf_op jit(solution)/shard_map/jit(_take)/gather | solution.py:143
  295.2 11.2 %gather_fusion.6 = f32[192,3,5,2,128]{4,3,2,1,0:T(2,128)} fusion(f32[3,5,2,2,128]{4,2,3,1,0:T(2,128)S(1)} %bitcast.167, s32[1024]{0:T(1024)S(1)} %pad_clamp_fusion), kind=kCustom, calls=%fused_computation.10.clone | custom fusion | bytes 5899008 | tf_op jit(solution)/shard_map/jit(_take)/gather | solution.py:143
  321.2 11.0 %gather_fusion.7 = f32[96,3,5,2,192]{4,3,2,1,0:T(2,128)S(1)} fusion(f32[3,5,2,192,128]{3,2,4,1,0:T(2,128)} %copy.342, s32[1024]{0:T(1024)S(1)} %pad_clamp_fusion.1), kind=kCustom, calls=%fused_computation.13.clone | custom fusion | bytes 4424064 | tf_op jit(solution)/shard_map/jit(_take)/gather | solution.py:144
  337.4 12.1 %gather_fusion.12 = f32[192,3,5,2,128]{4,3,2,1,0:T(2,128)S(1)} fusion(f32[3,5,2,2,128]{4,2,3,1,0:T(2,128)S(1)} %bitcast.169, s32[1024]{0:T(1024)S(1)} %pad_clamp_fusion.2), kind=kCustom, calls=%fused_computation.11.clone | custom fusion | bytes 5899008 | tf_op jit(solution)/shard_map/jit(_take)/gather | solution.py:143
  349.4 10.6 %gather_fusion.4 = f32[192,3,5,2,128]{4,3,2,1,0:T(2,128)} fusion(f32[3,5,2,2,128]{4,2,3,1,0:T(2,128)S(1)} %bitcast.168, s32[1024]{0:T(1024)S(1)} %pad_clamp_fusion.2), kind=kCustom, calls=%fused_computation.2.clone | custom fusion | bytes 5899008 | tf_op jit(solution)/shard_map/jit(_take)/gather | solution.py:143
  374.9 11.4 %gather_fusion.5 = f32[96,3,5,2,192]{4,3,2,1,0:T(2,128)S(1)} fusion(f32[3,5,2,192,128]{3,2,4,1,0:T(2,128)} %copy.339, s32[1024]{0:T(1024)S(1)} %pad_clamp_fusion.1), kind=kCustom, calls=%fused_computation.3.clone | custom fusion | bytes 4424064 | tf_op jit(solution)/shard_map/jit(_take)/gather | solution.py:144
  419.6 12.1 %gather_fusion.3 = f32[192,3,5,2,96]{4,3,2,1,0:T(2,128)} fusion(f32[3,5,2,96,128]{3,2,4,1,0:T(2,128)S(1)} %copy.337, s32[1024]{0:T(1024)S(1)} %pad_clamp_fusion.4), kind=kCustom, calls=%fused_computation.7.clone | custom fusion | bytes 4424448 | tf_op jit(solution)/shard_map/jit(_take)/gather | solution.py:140
  431.7 14.0 %gather_fusion.1 = f32[192,3,5,2,96]{4,3,2,1,0:T(2,128)} fusion(f32[3,5,2,96,128]{3,2,4,1,0:T(2,128)} %copy.335, s32[1024]{0:T(1024)S(1)} %pad_clamp_fusion.4), kind=kCustom, calls=%fused_computation.1.clone | custom fusion | bytes 4424448 | tf_op jit(solution)/shard_map/jit(_take)/gather | solution.py:140
  445.7 9.3 %multiply_add_fusion.3 = f32[3,5,2,96,192]{3,2,1,0,4:T(2,128)S(1)} fusion(f32[3,5,2,96,192]{3,2,1,0,4:T(2,128)} %get-tuple-element.219, pred[3,96,192]{1,0,2:T(4,128)(4,1)S(1)} %copy-done.13, f32[96,3,5,2,192]{0,3,2,1,4:T(2,128)} %copy.343, pred[192]{0:T(512)(128)(4,1)S(1)} %copy-done.18, f32[96,3,5,2,192]{0,3,2,1,4:T(2,128)} %copy.340, ...), kind=kLoop, calls=%fused_computation.97 | loop fusion | flops 6635520 | bytes 13400928 | tf_op jit(solution)/shard_map/add | solution.py:177
  488.7 8.6 %select_maximum_fusion.4 = f32[3,5,4,98,194]{3,2,1,0,4:T(4,128)S(1)} fusion(f32[3,5,2,98,1]{3,2,1,0,4:T(2,128)S(1)} %collective-permute-done.14, f32[3,5,2,98,1]{3,2,1,0,4:T(2,128)S(1)} %collective-permute-done.15, f32[3,5,2,1,192]{3,2,1,0,4:T(2,128)S(1)} %copy-done.2, f32[3,5,2,96,192]{3,2,1,0,4:T(2,128)S(1)} %multiply_add_fusion.3, ...), kind=kLoop, calls=%fused_computation.41 | loop fusion | flops 13688640 | bytes 6844320 | tf_op jit(solution)/shard_map/concatenate | solution.py:17
  497.2 37.4 %multiply_add_fusion.2 = f32[3,5,2,96,192]{3,2,1,0,4:T(2,128)S(1)} fusion(f32[3,5,2,96,192]{3,2,1,0,4:T(2,128)S(1)} %multiply_add_fusion.3, f32[3,5,4,98,194]{3,2,1,0,4:T(4,128)S(1)} %select_maximum_fusion.4, f32[3,5,2,1,192]{3,2,1,0,4:T(2,128)S(1)} %copy-done.2, f32[3,5,2,1,192]{3,2,1,0,4:T(2,128)S(1)} %copy-done.4, ...), kind=kLoop, calls=%fused_computation.96 | loop fusion | flops 11612160 | bytes 8990728 | tf_op jit(solution)/shard_map/add | solution.py:181
  577.9 10.8 %gather_fusion.15 = f32[96,3,5,2,192]{4,3,2,1,0:T(2,128)} fusion(f32[3,5,2,192,128]{3,2,4,1,0:T(2,128)} %copy.367, s32[1024]{0:T(1024)S(1)} %pad_clamp_fusion.1), kind=kCustom, calls=%fused_computation.15.clone | custom fusion | bytes 4424064 | tf_op jit(solution)/shard_map/jit(_take)/gather | solution.py:144
  604.0 10.8 %gather_fusion.13 = f32[96,3,5,2,192]{4,3,2,1,0:T(2,128)} fusion(f32[3,5,2,192,128]{3,2,4,1,0:T(2,128)} %copy.364, s32[1024]{0:T(1024)S(1)} %pad_clamp_fusion.1), kind=kCustom, calls=%fused_computation.14.clone | custom fusion | bytes 4424064 | tf_op jit(solution)/shard_map/jit(_take)/gather | solution.py:144
  626.5 13.9 %gather_fusion.11 = f32[192,3,5,2,96]{4,3,2,1,0:T(2,128)} fusion(f32[3,5,2,96,128]{3,2,4,1,0:T(2,128)} %copy.362, s32[1024]{0:T(1024)S(1)} %pad_clamp_fusion.4), kind=kCustom, calls=%fused_computation.9.clone | custom fusion | bytes 4424448 | tf_op jit(solution)/shard_map/jit(_take)/gather | solution.py:140
  645.0 13.6 %gather_fusion.9 = f32[192,3,5,2,96]{4,3,2,1,0:T(2,128)} fusion(f32[3,5,2,96,128]{3,2,4,1,0:T(2,128)} %copy.360, s32[1024]{0:T(1024)S(1)} %pad_clamp_fusion.4), kind=kCustom, calls=%fused_computation.8.clone | custom fusion | bytes 4424448 | tf_op jit(solution)/shard_map/jit(_take)/gather | solution.py:140
  658.6 9.3 %pad_maximum_fusion.1 = f32[3,5,2,108,204]{3,2,1,0,4:T(2,128)} fusion(f32[3,5,2,108,6]{3,2,1,0,4:T(2,128)S(1)} %collective-permute-done.19, f32[3,5,2,6,192]{3,2,1,0,4:T(2,128)} %copy.354, f32[3,5,2,96,192]{3,2,1,0,4:T(2,128)S(1)} %copy-done.1, f32[3,5,2,6,192]{3,2,1,0,4:T(2,128)} %copy.353, f32[3,5,2,108,6]{3,2,1,0,4:T(2,128)} %collective-permute-done.18), kind=kLoop, calls=%fused_computation.47 | loop fusion | flops 2643840 | bytes 5287680 | tf_op jit(solution)/shard_map/concatenate | solution.py:17
  668.8 18.0 %while.35 = (s32[]{:T(128)}, f32[3,5,2,108,204]{3,2,1,0,4:T(2,128)}, s32[3,5]{1,0:T(4,128)}, f32[3,5,2,96,192]{3,2,1,0,4:T(2,128)S(1)}, s32[]{:T(128)}) while((s32[]{:T(128)}, f32[3,5,2,108,204]{3,2,1,0,4:T(2,128)}, s32[3,5]{1,0:T(4,128)}, f32[3,5,2,96,192]{3,2,1,0,4:T(2,128)S(1)}, s32[]{:T(128)}) %tuple.221), condition=%wide.while_cond.1, body=%wide.while_body.1.sunk | while | flops 2 | bytes 1720473 | solution.py:132
  688.4 9.3 %multiply_add_fusion.1 = f32[3,5,2,96,192]{3,2,1,0,4:T(2,128)S(1)} fusion(f32[3,5,2,96,192]{3,2,1,0,4:T(2,128)} %copy-done.7, pred[3,96,192]{1,0,2:T(4,128)(4,1)S(1)} %broadcast_and_fusion.1, f32[96,3,5,2,192]{0,3,2,1,4:T(2,128)} %copy.368, pred[192]{0:T(512)(128)(4,1)S(1)} %copy-done.19, f32[96,3,5,2,192]{0,3,2,1,4:T(2,128)} %copy.365, ...), kind=kLoop, calls=%fused_computation.95 | loop fusion | flops 6635520 | bytes 13400928 | tf_op jit(solution)/shard_map/add | solution.py:177
  731.3 8.5 %select_maximum_fusion = f32[3,5,4,98,194]{3,2,1,0,4:T(4,128)S(1)} fusion(f32[3,5,2,98,1]{3,2,1,0,4:T(2,128)S(1)} %collective-permute-done.22, f32[3,5,2,98,1]{3,2,1,0,4:T(2,128)S(1)} %collective-permute-done.23, f32[3,5,2,1,192]{3,2,1,0,4:T(2,128)S(1)} %copy-done.3, f32[3,5,2,96,192]{3,2,1,0,4:T(2,128)S(1)} %multiply_add_fusion.1, ...), kind=kLoop, calls=%fused_computation.37 | loop fusion | flops 13688640 | bytes 6844320 | tf_op jit(solution)/shard_map/concatenate | solution.py:17
  739.7 38.3 %multiply_add_fusion = f32[3,5,2,96,192]{3,2,1,0,4:T(2,128)} fusion(f32[3,5,2,96,192]{3,2,1,0,4:T(2,128)S(1)} %multiply_add_fusion.1, f32[3,5,4,98,194]{3,2,1,0,4:T(4,128)S(1)} %select_maximum_fusion, f32[3,5,2,1,192]{3,2,1,0,4:T(2,128)S(1)} %copy-done.3, f32[3,5,2,1,192]{3,2,1,0,4:T(2,128)S(1)} %copy-done.5, ...), kind=kLoop, calls=%fused_computation.94 | loop fusion | flops 11612160 | bytes 8990728 | tf_op jit(solution)/shard_map/add | solution.py:181
  (384 shorter events, 394.1 us)
Async XLA Ops:
  7.2 274.4 %all-reduce.9.cloned.1.call-start = ((), (), s32[]{:S(2)}) async-start(), calls=%async_computation | async-start | bytes 983040 | tf_op jit(solution)/shard_map/psum | solution.py:157
  8.1 25.3 %collective-permute-start = (f32[5,2,1,128]{3,2,1,0:T(1,128)S(1)}, f32[5,2,1,128]{3,2,1,0:T(1,128)S(1)}, u32[]{:S(2)}, u32[]{:S(2)}) collective-permute-start(f32[5,2,1,128]{3,2,1,0:T(1,128)S(1)} %get-tuple-element.438), channel_id=1, source_target_pairs={{4,0},{8,4},{12,8},{5,1},{9,5},{13,9},{6,2},{10,6},{14,10},{7,3},{... | collective-permute-start | bytes 15368 | tf_op jit(solution)/shard_map/ppermute | solution.py:21
  9.4 24.0 %collective-permute-start.1 = (f32[5,2,1,128]{3,2,1,0:T(1,128)S(1)}, f32[5,2,1,128]{3,2,1,0:T(1,128)S(1)}, u32[]{:S(2)}, u32[]{:S(2)}) collective-permute-start(f32[5,2,1,128]{3,2,1,0:T(1,128)S(1)} %get-tuple-element.437), channel_id=1, source_target_pairs={{0,4},{4,8},{8,12},{1,5},{5,9},{9,13},{2,6},{6,10},{10,14},{3,7},{... | collective-permute-start | bytes 15368 | tf_op jit(solution)/shard_map/ppermute | solution.py:19
  16.2 102.9 %collective-permute-start.9 = (f32[3,5,2,6,192]{4,2,3,1,0:T(2,128)S(1)}, f32[3,5,2,6,192]{4,2,3,1,0:T(2,128)}, u32[]{:S(2)}, u32[]{:S(2)}) collective-permute-start(f32[3,5,2,6,192]{4,2,3,1,0:T(2,128)S(1)} %copy.384), channel_id=1, source_target_pairs={{4,0},{8,4},{12,8},{5,1},{9,5},{13,9},{6,2},{10,6},{14,10},{7,3},{... | collective-permute-start | bytes 414728 | tf_op jit(solution)/shard_map/ppermute | solution.py:21
  18.3 105.0 %collective-permute-start.8 = (f32[3,5,2,6,192]{4,2,3,1,0:T(2,128)}, f32[3,5,2,6,192]{4,2,3,1,0:T(2,128)}, u32[]{:S(2)}, u32[]{:S(2)}) collective-permute-start(f32[3,5,2,6,192]{4,2,3,1,0:T(2,128)} %copy.383), channel_id=1, source_target_pairs={{0,4},{4,8},{8,12},{1,5},{5,9},{9,13},{2,6},{6,10},{10,14},{3,7},{... | collective-permute-start | bytes 414728 | tf_op jit(solution)/shard_map/ppermute | solution.py:19
  34.6 4.4 collective-permute-start.2
  35.9 4.3 collective-permute-start.3
  41.3 14.7 %collective-permute-start.4 = (f32[5,2,1,128]{3,2,1,0:T(1,128)S(1)}, f32[5,2,1,128]{3,2,1,0:T(1,128)S(1)}, u32[]{:S(2)}, u32[]{:S(2)}) collective-permute-start(f32[5,2,1,128]{3,2,1,0:T(1,128)S(1)} %get-tuple-element.436), channel_id=1, source_target_pairs={{4,0},{8,4},{12,8},{5,1},{9,5},{13,9},{6,2},{10,6},{14,10},{7,3},{... | collective-permute-start | bytes 15368 | tf_op jit(solution)/shard_map/ppermute | solution.py:21
  42.6 13.4 %collective-permute-start.5 = (f32[5,2,1,128]{3,2,1,0:T(1,128)S(1)}, f32[5,2,1,128]{3,2,1,0:T(1,128)S(1)}, u32[]{:S(2)}, u32[]{:S(2)}) collective-permute-start(f32[5,2,1,128]{3,2,1,0:T(1,128)S(1)} %get-tuple-element.435), channel_id=1, source_target_pairs={{0,4},{4,8},{8,12},{1,5},{5,9},{9,13},{2,6},{6,10},{10,14},{3,7},{... | collective-permute-start | bytes 15368 | tf_op jit(solution)/shard_map/ppermute | solution.py:19
  56.9 57.3 %collective-permute-start.6 = (f32[5,2,66,1]{3,2,1,0:T(8,128)}, f32[5,2,66,1]{3,2,1,0:T(8,128)S(1)}, u32[]{:S(2)}, u32[]{:S(2)}) collective-permute-start(f32[5,2,66,1]{3,2,1,0:T(8,128)} %get-tuple-element.432), channel_id=1, source_target_pairs={{1,0},{2,1},{3,2},{5,4},{6,5},{7,6},{9,8},{10,9},{11,10},{13,12},{... | collective-permute-start | bytes 7928 | tf_op jit(solution)/shard_map/ppermute | solution.py:21
  58.2 56.0 %collective-permute-start.7 = (f32[5,2,66,1]{3,2,1,0:T(8,128)S(1)}, f32[5,2,66,1]{3,2,1,0:T(8,128)S(1)}, u32[]{:S(2)}, u32[]{:S(2)}) collective-permute-start(f32[5,2,66,1]{3,2,1,0:T(8,128)S(1)} %get-tuple-element.431), channel_id=1, source_target_pairs={{0,1},{1,2},{2,3},{4,5},{5,6},{6,7},{8,9},{9,10},{10,11},{12,13},{... | collective-permute-start | bytes 7928 | tf_op jit(solution)/shard_map/ppermute | solution.py:19
  129.4 57.9 %collective-permute-start.11 = (f32[3,5,2,108,6]{3,2,4,1,0:T(2,128)}, f32[3,5,2,108,6]{3,2,4,1,0:T(2,128)S(1)}, u32[]{:S(2)}, u32[]{:S(2)}) collective-permute-start(f32[3,5,2,108,6]{3,2,4,1,0:T(2,128)} %get-tuple-element.422), channel_id=1, source_target_pairs={{1,0},{3,2},{5,4},{7,6},{9,8},{11,10},{13,12},{15,14},{17,16},{19,... | collective-permute-start | bytes 233288 | tf_op jit(solution)/shard_map/ppermute | solution.py:21
  130.7 56.6 %collective-permute-start.10 = (f32[3,5,2,108,6]{3,2,4,1,0:T(2,128)S(1)}, f32[3,5,2,108,6]{3,2,4,1,0:T(2,128)}, u32[]{:S(2)}, u32[]{:S(2)}) collective-permute-start(f32[3,5,2,108,6]{3,2,4,1,0:T(2,128)S(1)} %get-tuple-element.421), channel_id=1, source_target_pairs={{0,1},{2,3},{4,5},{6,7},{8,9},{10,11},{12,13},{14,15},{16,17},{18,... | collective-permute-start | bytes 233288 | tf_op jit(solution)/shard_map/ppermute | solution.py:19
  465.7 9.9 %collective-permute-start.12 = (f32[3,5,2,1,192]{4,2,3,1,0:T(2,128)S(1)}, f32[3,5,2,1,192]{4,2,3,1,0:T(2,128)S(1)}, u32[]{:S(2)}, u32[]{:S(2)}) collective-permute-start(f32[3,5,2,1,192]{4,2,3,1,0:T(2,128)S(1)} %copy.345), channel_id=1, source_target_pairs={{4,0},{8,4},{12,8},{5,1},{9,5},{13,9},{6,2},{10,6},{14,10},{7,3},{... | collective-permute-start | bytes 69128 | tf_op jit(solution)/shard_map/ppermute | solution.py:21
  471.0 7.8 collective-permute-start.13
  483.4 4.6 collective-permute-start.14
  484.8 3.9 collective-permute-start.15
  544.3 10.6 %collective-permute-start.17 = (f32[3,5,2,6,192]{4,2,3,1,0:T(2,128)S(1)}, f32[3,5,2,6,192]{4,2,3,1,0:T(2,128)S(1)}, u32[]{:S(2)}, u32[]{:S(2)}) collective-permute-start(f32[3,5,2,6,192]{4,2,3,1,0:T(2,128)S(1)} %copy.352), channel_id=1, source_target_pairs={{4,0},{8,4},{12,8},{5,1},{9,5},{13,9},{6,2},{10,6},{14,10},{7,3},{... | collective-permute-start | bytes 414728 | tf_op jit(solution)/shard_map/ppermute | solution.py:21
  548.9 9.3 %collective-permute-start.16 = (f32[3,5,2,6,192]{4,2,3,1,0:T(2,128)}, f32[3,5,2,6,192]{4,2,3,1,0:T(2,128)}, u32[]{:S(2)}, u32[]{:S(2)}) collective-permute-start(f32[3,5,2,6,192]{4,2,3,1,0:T(2,128)} %copy.351), channel_id=1, source_target_pairs={{0,4},{4,8},{8,12},{1,5},{5,9},{9,13},{2,6},{6,10},{10,14},{3,7},{... | collective-permute-start | bytes 414728 | tf_op jit(solution)/shard_map/ppermute | solution.py:19
  564.6 94.1 %collective-permute-start.19 = (f32[3,5,2,108,6]{3,2,1,0,4:T(2,128)}, f32[3,5,2,108,6]{3,2,1,0,4:T(2,128)S(1)}, u32[]{:S(2)}, u32[]{:S(2)}) collective-permute-start(f32[3,5,2,108,6]{3,2,1,0,4:T(2,128)} %get-tuple-element.418), channel_id=1, source_target_pairs={{1,0},{3,2},{5,4},{7,6},{9,8},{11,10},{13,12},{15,14},{17,16},{19,... | collective-permute-start | bytes 233288 | tf_op jit(solution)/shard_map/ppermute | solution.py:21
  565.8 92.8 %collective-permute-start.18 = (f32[3,5,2,108,6]{3,2,1,0,4:T(2,128)S(1)}, f32[3,5,2,108,6]{3,2,1,0,4:T(2,128)}, u32[]{:S(2)}, u32[]{:S(2)}) collective-permute-start(f32[3,5,2,108,6]{3,2,1,0,4:T(2,128)S(1)} %get-tuple-element.417), channel_id=1, source_target_pairs={{0,1},{2,3},{4,5},{6,7},{8,9},{10,11},{12,13},{14,15},{16,17},{18,... | collective-permute-start | bytes 233288 | tf_op jit(solution)/shard_map/ppermute | solution.py:19
  708.2 10.0 %collective-permute-start.20 = (f32[3,5,2,1,192]{4,2,3,1,0:T(2,128)S(1)}, f32[3,5,2,1,192]{4,2,3,1,0:T(2,128)S(1)}, u32[]{:S(2)}, u32[]{:S(2)}) collective-permute-start(f32[3,5,2,1,192]{4,2,3,1,0:T(2,128)S(1)} %copy.370), channel_id=1, source_target_pairs={{4,0},{8,4},{12,8},{5,1},{9,5},{13,9},{6,2},{10,6},{14,10},{7,3},{... | collective-permute-start | bytes 69128 | tf_op jit(solution)/shard_map/ppermute | solution.py:21
  713.5 8.0 %collective-permute-start.21 = (f32[3,5,2,1,192]{4,2,3,1,0:T(2,128)S(1)}, f32[3,5,2,1,192]{4,2,3,1,0:T(2,128)S(1)}, u32[]{:S(2)}, u32[]{:S(2)}) collective-permute-start(f32[3,5,2,1,192]{4,2,3,1,0:T(2,128)S(1)} %copy.372), channel_id=1, source_target_pairs={{0,4},{4,8},{8,12},{1,5},{5,9},{9,13},{2,6},{6,10},{10,14},{3,7},{... | collective-permute-start | bytes 69128 | tf_op jit(solution)/shard_map/ppermute | solution.py:19
  726.0 4.5 collective-permute-start.22
  (36 other events, 1209.1 us)
Sparse Core Ops, SparseCore 0:
  187.4 94.0 all-reduce.8
where the time goes:
time: 802 us; the launch traced here: 791 us
  local copies, waits for them, and re-layouts  416 us (52%)
  other arithmetic  168 us (21%)
  waiting for transfers between devices  73.1 us (9%)
  starting transfers between devices  71.3 us (9%)
  loops' own time  46.6 us (6%)
  between operations  15.6 us (2%)
    add x2, other arithmetic, per_device(): nests_now = relaxed + inside * change  75.6 us
    psum x1, waiting for transfers between devices, per_device(): totals = lax.psum(terms, ('tile', 'nest', 'lev'))  70.3 us
    gather x8, local copies, waits for them, and re-layouts, along(): picked = jnp.take(picked, coarse_rows, axis=4)  68.9 us
    ppermute x12, starting transfers between devices, extended(): lax.ppermute(tail, axis, [(i, (i + 1) % count) for i in range(ends)])  55.5 us
    gather x4, local copies, waits for them, and re-layouts, across(): return jnp.take(picked, coarse_cols, axis=4)  53.6 us
    another operation x2, loops' own time, extract(): return lax.map(single, corners)  46.6 us
    gather x4, local copies, waits for them, and re-layouts, along(): picked = jnp.take(zone, zone_index, axis=3)  46.1 us
    concatenate x10, other arithmetic, extended(): jnp.concatenate([lax.ppermute(tail, axis, [(i, (i + 1) % count) for i in...  38.6 us
  transfers between devices with their start and end apart: 25, of which 4 were waited for; matrix products, arithmetic and copies ran while one was open for 28% of the time, Pallas kernels for 0%

commit v1 on v0

v1 whole, which is shorter than its diff:
```python
import functools
import jax
import jax.numpy as jnp
from jax import lax
from jax.experimental import pallas as pl
from jax.experimental.pallas import tpu as pltpu
from jax.sharding import PartitionSpec as P

FP = 128
BWP = 2
MOVE = 2
HALO = 16
LANES = 128
ALONG = 72
SPAN = 3 * FP
BORDER = 3 * BWP
GROUP = ("tile", "nest", "lev")
EXACT = lax.Precision.HIGHEST


def extended(cells, sides, width):
    for axis, dim in sides:
        count = lax.axis_size(axis)
        ends = count - 1
        head = lax.slice_in_dim(cells, 0, width, axis=dim)
        tail = lax.slice_in_dim(cells, cells.shape[dim] - width, cells.shape[dim], axis=dim)
        cells = jnp.concatenate(
            [
                lax.ppermute(tail, axis, [(i, (i + 1) % count) for i in range(ends)]),
                cells,
                lax.ppermute(head, axis, [((i + 1) % count, i) for i in range(ends)]),
            ],
            axis=dim,
        )
    return cells


def advanced(padded, lateral_rate, vertical_rate):
    padded = jnp.pad(padded, ((0, 0), (1, 1), (0, 0), (0, 0)))
    centre = padded[:, 1:-1, 1:-1, 1:-1]
    lateral = (
        padded[:, 1:-1, 2:, 1:-1]
        + padded[:, 1:-1, :-2, 1:-1]
        + padded[:, 1:-1, 1:-1, 2:]
        + padded[:, 1:-1, 1:-1, :-2]
        - 4.0 * centre
    )
    upright = padded[:, 2:, 1:-1, 1:-1] + padded[:, :-2, 1:-1, 1:-1] - 2.0 * centre
    return (
        centre
        + lateral_rate[:, None, None, None] * lateral
        + vertical_rate[:, None, None, None] * upright
    )


def select_rows(picker, table):
    return jnp.sum(picker[:, :, None] * table[None, :, :], axis=1)


def scatter_kernel(counts, x_ref, y_ref, slots, send_sem, recv_sem):
    tiles, nests, levs = counts
    total = tiles * nests * levs
    me = (lax.axis_index("tile") * nests + lax.axis_index("nest")) * levs + lax.axis_index("lev")

    def partner(k):
        other = lax.rem(me + k, total)
        return other, {
            "tile": other // (nests * levs),
            "nest": lax.rem(other // levs, nests),
            "lev": lax.rem(other, levs),
        }

    def copy(k):
        other, place = partner(k)
        return pltpu.make_async_remote_copy(
            src_ref=x_ref.at[other],
            dst_ref=slots.at[k],
            send_sem=send_sem.at[k],
            recv_sem=recv_sem.at[k],
            device_id=place,
            device_id_type=pl.DeviceIdType.MESH,
        )

    barrier = pltpu.get_barrier_semaphore()

    def greet(k, carry):
        pl.semaphore_signal(
            barrier, inc=1, device_id=partner(k)[1], device_id_type=pl.DeviceIdType.MESH
        )
        return carry

    lax.fori_loop(1, total, greet, 0)
    pl.semaphore_wait(barrier, total - 1)

    def begin(k, carry):
        copy(k).start()
        return carry

    lax.fori_loop(1, total, begin, 0)
    y_ref[...] = x_ref[me]

    def finish(k, carry):
        copy(k).wait()
        y_ref[...] += slots[k]
        return carry

    lax.fori_loop(1, total, finish, 0)


def scatter_sum(terms, counts):
    total, rows, lanes = terms.shape
    return pl.pallas_call(
        functools.partial(scatter_kernel, counts),
        out_shape=jax.ShapeDtypeStruct((rows, lanes), jnp.float32),
        in_specs=[pl.BlockSpec(memory_space=pltpu.VMEM)],
        out_specs=pl.BlockSpec(memory_space=pltpu.VMEM),
        scratch_shapes=[
            pltpu.VMEM((total, rows, lanes), jnp.float32),
            pltpu.SemaphoreType.DMA((total,)),
            pltpu.SemaphoreType.DMA((total,)),
        ],
        compiler_params=pltpu.CompilerParams(
            collective_id=0, has_side_effects=True, vmem_limit_bytes=48 * 1024 * 1024
        ),
    )(terms)


def nest_kernel(rows, cols, steps, offs, place, lateral, vertical, x_ref, sn_ref, we_ref, o_ref):
    slot = pl.program_id(0)
    field = pl.program_id(1)
    slots = pl.num_programs(0)
    high, wide = x_ref.shape[3], x_ref.shape[4]
    rate_l = lateral[field]
    rate_v = vertical[field]
    r = lax.broadcasted_iota(jnp.int32, (high, wide), 0) + (place[0] * rows - HALO)
    j = lax.broadcasted_iota(jnp.int32, (high, wide), 1)
    c = j + place[1] * jnp.where(j >= cols, cols - wide, cols)
    gap_r = jnp.minimum(r, SPAN - 1 - r)
    gap_c = jnp.minimum(c, SPAN - 1 - c)
    gap = jnp.minimum(gap_r, gap_c)
    weight = jnp.maximum(BORDER - gap, 0).astype(jnp.float32) / jnp.float32(BORDER)
    inside = gap >= 1
    near_row = gap_r < BORDER
    second_row = ((r >= 3) & (r < BORDER)) | (r >= SPAN - 3)
    second_col = ((c >= 3) & (c < BORDER)) | (c >= SPAN - 3)
    state = [x_ref[0, 0, 0], x_ref[0, 0, 1]]
    for step in range(steps):
        at = (step * slots + slot) * 2
        down = offs[at]
        right = offs[at + 1]
        keep = (r + down >= 0) & (r + down < SPAN) & (c + right >= 0) & (c + right < SPAN)
        turn_r = lax.rem(high - down, high)
        turn_c = lax.rem(wide - right, wide)
        relaxed = []
        for v in range(2):
            k = 2 * step
            along = jnp.where(second_row, sn_ref[0, 0, v, k + 1 : k + 2, :], sn_ref[0, 0, v, k : k + 1, :])
            across = jnp.where(second_col, we_ref[0, 0, v, :, k + 1 : k + 2], we_ref[0, 0, v, :, k : k + 1])
            driving = jnp.where(near_row, along, across)
            moved = pltpu.roll(pltpu.roll(state[v], turn_r, 0), turn_c, 1)
            retained = jnp.where(keep, moved, driving)
            relaxed.append(retained + weight * (driving - retained))
        for v in range(2):
            here = relaxed[v]
            around = (
                pltpu.roll(here, 1, 0)
                + pltpu.roll(here, high - 1, 0)
                + pltpu.roll(here, 1, 1)
                + pltpu.roll(here, wide - 1, 1)
                - 4.0 * here
            )
            change = rate_l * around + rate_v * (relaxed[1 - v] - 2.0 * here)
            state[v] = jnp.where(inside, here + change, here)
    for v in range(2):
        o_ref[0, 0, v] = state[v][HALO : HALO + rows, :cols]


def advance_nests(wide_nests, along, across, offs, place, lateral, vertical, rows, cols, steps):
    slots, fields, levels, high, wide = wide_nests.shape
    spec = lambda *tail: pl.BlockSpec((1, 1) + tail, lambda n, f, *_: (n, f, 0, 0, 0))
    return pl.pallas_call(
        functools.partial(nest_kernel, rows, cols, steps),
        out_shape=jax.ShapeDtypeStruct((slots, fields, levels, rows, cols), jnp.float32),
        grid_spec=pltpu.PrefetchScalarGridSpec(
            num_scalar_prefetch=4,
            grid=(slots, fields),
            in_specs=[
                spec(levels, high, wide),
                spec(levels, 2 * steps, wide),
                spec(levels, high, 2 * steps),
            ],
            out_specs=spec(levels, rows, cols),
        ),
        compiler_params=pltpu.CompilerParams(vmem_limit_bytes=32 * 1024 * 1024),
    )(offs, place, lateral, vertical, wide_nests, along, across)


def per_device(parent_field, nest_fields, lateral_rate, vertical_rate, centres, slot_storm):
    fields, levels, prow, pcol = parent_field.shape
    slots, _, _, rows, cols = nest_fields.shape
    storms = slot_storm.shape[0]
    steps = centres.shape[0] - 1
    tiles = lax.axis_size("tile")
    groups = lax.axis_size("nest")
    levs = lax.axis_size("lev")
    tile_at = lax.axis_index("tile")
    nest_at = lax.axis_index("nest")
    lev_at = lax.axis_index("lev")
    coarse = rows // 3
    assert levs == 2 and tiles > 1 and steps == 2 and levels == 2
    total = tiles * groups * levs

    nearer = jnp.where(lev_at == 0, nest_fields[..., LANES:cols], nest_fields[..., : cols - LANES])
    other = lax.ppermute(nearer, "lev", [(0, 1), (1, 0)])
    wide_nests = jnp.concatenate([nest_fields, other], axis=4)
    wide_nests = extended(wide_nests, (("tile", 3),), HALO)
    wide = wide_nests.shape[4]
    high = wide_nests.shape[3]

    padded = extended(parent_field, (("tile", 2), (("nest", "lev"), 3)), steps)
    first = advanced(padded, lateral_rate, vertical_rate)
    xg = tile_at * prow + jnp.arange(prow, dtype=jnp.int32)
    yg = (nest_at * levs + lev_at) * pcol + jnp.arange(pcol, dtype=jnp.int32)
    xw = tile_at * prow - 1 + jnp.arange(prow + 2, dtype=jnp.int32)
    yw = (nest_at * levs + lev_at) * pcol - 1 + jnp.arange(pcol + 2, dtype=jnp.int32)
    fine_x = (xw >= 0) & (xw < prow * tiles)
    fine_y = (yw >= 0) & (yw < pcol * groups * levs)
    first = jnp.where(fine_x[:, None] & fine_y[None, :], first, 0.0)
    second = advanced(first, lateral_rate, vertical_rate)
    stages = (first[:, :, 1:-1, 1:-1], second)

    storm_ids = jnp.arange(storms, dtype=jnp.int32)
    pick = (slot_storm[:, None] == storm_ids[None, :]).astype(jnp.int32)
    place_at = [select_rows(pick, centres[n]) for n in range(steps + 1)]
    offs = jnp.stack([3 * (place_at[n + 1] - place_at[n]) for n in range(steps)])
    offs = lax.dynamic_slice_in_dim(offs, nest_at * slots, slots, 1).reshape(-1)

    edges = jnp.array([0, 1, FP - 2, FP - 1], jnp.int32)
    lane = jnp.arange(LANES, dtype=jnp.int32)
    starts = jnp.array([0, FP - ALONG], jnp.int32)
    along_at = jnp.where(lane < ALONG, starts[:, None] + lane[None, :], -SPAN * SPAN)
    rows_at = (jnp.arange(tiles, dtype=jnp.int32) * coarse - 4 - ALONG)[:, None] + lane[None, :]
    rows_at = jnp.where((lane >= ALONG) & (rows_at >= 0) & (rows_at < FP), rows_at, -SPAN * SPAN)
    parts = []
    for n in range(steps):
        now = stages[n].reshape(fields * levels, prow, pcol)
        corner = place_at[n + 1] - FP // 2
        row_edge = (corner[:, 0, None, None] + edges[None, :, None] == xg).astype(jnp.float32)
        col_edge = (corner[:, 1, None, None] + edges[None, :, None] == yg).astype(jnp.float32)
        col_pick = (corner[:, 1, None, None, None] + along_at[None, None] == yg[None, :, None, None])
        row_pick = (corner[:, 0, None, None, None] + rows_at[None, None] == xg[None, :, None, None])
        col_pick = col_pick.astype(jnp.float32).reshape(storms, pcol, levs * LANES)
        row_pick = row_pick.astype(jnp.float32).reshape(storms, prow, tiles * LANES)
        sn = jnp.einsum("jrx,fxy->jrfy", row_edge, now, precision=EXACT)
        sn = jnp.einsum("jrfy,jyc->jrfc", sn, col_pick, precision=EXACT)
        we = jnp.einsum("jky,fxy->jkfx", col_edge, now, precision=EXACT)
        we = jnp.einsum("jkfx,jxc->jkfc", we, row_pick, precision=EXACT)
        sn = sn.reshape(groups, slots, 2, 2, fields * levels, levs, LANES)
        we = we.reshape(groups, slots, 2, 2, fields * levels, tiles, LANES)
        sn_low = jnp.moveaxis(sn[:, :, 0], 4, 1)
        sn_high = jnp.moveaxis(sn[:, :, 1], 4, 1)
        we = jnp.transpose(we, (5, 0, 2, 1, 3, 4, 6))
        parts.append(
            jnp.concatenate(
                [(we[0] + sn_low)[None], we[1:-1], (we[-1] + sn_high)[None]], axis=0
            )
        )
    terms = jnp.stack(parts, axis=4)
    terms = terms.reshape(total, slots * steps * 2 * fields * levels, LANES)
    zone = scatter_sum(terms, (tiles, groups, levs))
    zone = zone.reshape(slots, 2 * steps, fields, levels, LANES)

    jj = jnp.arange(wide, dtype=jnp.int32)
    col_cell = jj + lev_at * jnp.where(jj >= cols, cols - wide, cols)
    row_cell = tile_at * rows - HALO + jnp.arange(high, dtype=jnp.int32)
    spread_c = (lane[:, None] < ALONG) & (col_cell // 3 - lev_at * (FP - ALONG) == lane[:, None])
    spread_r = (lane[:, None] >= ALONG) & (
        row_cell // 3 - (tile_at * coarse - 4 - ALONG) == lane[:, None]
    )
    along = jnp.einsum("nkfvl,lc->nfvkc", zone, spread_c.astype(jnp.float32), precision=EXACT)
    across = jnp.einsum("nkfvl,lr->nfvrk", zone, spread_r.astype(jnp.float32), precision=EXACT)
    place = jnp.stack([tile_at, lev_at]).astype(jnp.int32)
    nests = advance_nests(
        wide_nests, along, across, offs, place, lateral_rate, vertical_rate, rows, cols, steps
    )
    return (second, nests)


def solution(mesh):
    placed = (
        P("member", None, "tile", ("nest", "lev")),
        P(("member", "nest"), None, None, "tile", "lev"),
        P(),
        P(),
        P("member", None, None),
        P("member"),
    )
    return jax.shard_map(
        per_device,
        mesh=mesh,
        in_specs=placed,
        out_specs=(
            P("member", None, "tile", ("nest", "lev")),
            P(("member", "nest"), None, None, "tile", "lev"),
        ),
        check_vma=False,
    )
```

time: 802 us -> 99.3 us (0.12); the launches traced: 791 us -> 98.9 us
  local copies, waits for them, and re-layouts: 416 us -> 11.3 us
  other arithmetic: 168 us -> 7.61 us
  waiting for transfers between devices: 73.1 us -> 14.1 us
  starting transfers between devices: 71.3 us -> 19.3 us
  loops' own time: 46.6 us -> 0 us
  Pallas kernels: 0 us -> 40.3 us
  between operations: 15.6 us -> 1.15 us
    gather x39 -> x0, local copies, waits for them, and re-layouts: 211 us -> none  [the longest x8 68.9 us: along(): picked = jnp.take(picked, coarse_rows, axis=4)]
    add x10 -> x8, other arithmetic: 95.5 us -> 0.59 us  [the longest x2 0.28 us: per_device(): we[0] + sn_low]
    psum x1 -> x0, waiting for transfers between devices: 70.3 us -> none  [per_device(): totals = lax.psum(terms, ('tile', 'nest', 'lev'))]
    select_n x32 -> x0, local copies, waits for them, and re-layouts: 50 us -> none  [the longest x4 32 us: along(): picked = jnp.take(zone, zone_index, axis=3)]
    another operation x4 -> x0, loops' own time: 46.6 us -> none  [the longest x2 46.6 us: extract(): return lax.map(single, corners)]
    pallas_call x0 -> x2, Pallas kernels: none -> 40.3 us  [the longest x1 26.8 us: scatter_sum(): pl.pallas_call(functools.partial(scatter_kernel, counts), out_shape=jax.S...]
    ppermute x12 -> x3, starting transfers between devices: 55.5 us -> 15.2 us  [extended(): lax.ppermute(tail, axis, [(i, (i + 1) % count) for i in range(ends)])]
    concatenate x10 -> x3, other arithmetic: 38.6 us -> 1.12 us  [extended(): jnp.concatenate([lax.ppermute(tail, axis, [(i, (i + 1) % count) for i in...]
  transfers between devices with their start and end apart: 25 -> 7, of which waited for: 4 -> 3; matrix products, arithmetic and copies ran while one was open for 28% -> 18% of each run, Pallas kernels for 0% -> 27%
where the time goes in v1:
time: 99.3 us; the launch traced here: 98.9 us
  Pallas kernels  40.3 us (41%)
  starting transfers between devices  19.3 us (19%)
  waiting for transfers between devices  14.1 us (14%)
  local copies, waits for them, and re-layouts  11.3 us (11%)
  other arithmetic  7.61 us (8%)
  matrix products  5.1 us (5%)
  between operations  1.15 us (1%)
    pallas_call x1, Pallas kernels, scatter_sum(): pl.pallas_call(functools.partial(scatter_kernel, counts), out_shape=jax.S...  26.8 us
    ppermute x3, starting transfers between devices, extended(): lax.ppermute(tail, axis, [(i, (i + 1) % count) for i in range(ends)])  15.2 us
    pallas_call x1, Pallas kernels, advance_nests(): pl.pallas_call(functools.partial(nest_kernel, rows, cols, steps), out_sha...  13.5 us
    ppermute x3, waiting for transfers between devices, extended(): lax.ppermute(tail, axis, [(i, (i + 1) % count) for i in range(ends)])  7.36 us
    ppermute x3, waiting for transfers between devices, extended(): lax.ppermute(head, axis, [((i + 1) % count, i) for i in range(ends)])  6.75 us
    ppermute x3, starting transfers between devices, extended(): lax.ppermute(head, axis, [((i + 1) % count, i) for i in range(ends)])  4.06 us
    ppermute x1, local copies, waits for them, and re-layouts, per_device(): other = lax.ppermute(nearer, 'lev', [(0, 1), (1, 0)])  2.77 us
    unnamed x22, local copies, waits for them, and re-layouts  2.59 us
  transfers between devices with their start and end apart: 7, of which 3 were waited for; matrix products, arithmetic and copies ran while one was open for 18% of the time, Pallas kernels for 27%

profile of v1, /device:TPU:0, one launch (start us, length us, event | category | flops | bytes accessed | tf_op | source)
XLA Modules:
  0.0 98.9 jit_solution(14907973598853647752)
XLA Ops:
  0.6 0.8 fusion.88
  1.4 4.9 %collective-permute-start = (f32[5,2,2,128]{3,2,1,0:T(2,128)S(1)}, f32[5,2,2,128]{3,2,1,0:T(2,128)S(1)}, u32[]{:S(2)}, u32[]{:S(2)}) collective-permute-start(f32[5,2,2,128]{3,2,1,0:T(2,128)S(1)} %get-tuple-element.19), channel_id=1, source_target_pairs={{0,4},{4,8},{8,12},{1,5},{5,9},{9,13},{2,6},{6,10},{10,14},{3,7},{... | collective-permute-start | bytes 30728 | tf_op jit(solution)/shard_map/ppermute | solution.py:29
  6.4 1.3 %collective-permute-start.1 = (f32[5,2,2,128]{3,2,1,0:T(2,128)S(1)}, f32[5,2,2,128]{3,2,1,0:T(2,128)S(1)}, u32[]{:S(2)}, u32[]{:S(2)}) collective-permute-start(f32[5,2,2,128]{3,2,1,0:T(2,128)S(1)} %get-tuple-element.20), channel_id=1, source_target_pairs={{4,0},{8,4},{12,8},{5,1},{9,5},{13,9},{6,2},{10,6},{14,10},{7,3},{... | collective-permute-start | bytes 30728 | tf_op jit(solution)/shard_map/ppermute | solution.py:31
  7.7 2.0 %fusion.85 = (f32[3,5,2,96,64]{4,3,2,1,0:T(8,128)S(1)}, f32[3,5,2,96,64]{4,3,2,1,0:T(8,128)S(1)}) fusion(f32[3,5,2,96,192]{4,3,2,1,0:T(8,128)} %param.9), kind=kLoop, calls=%fused_computation.161 | loop fusion | bytes 2949120 | tf_op jit(solution)/shard_map/slice | solution.py:213
  9.7 1.4 %copy.154 = f32[3,5,2,96,64]{3,4,2,1,0:T(8,128)} copy(f32[3,5,2,96,64]{4,3,2,1,0:T(8,128)S(1)} %get-tuple-element.11) | data formatting | bytes 1474560
  11.6 0.7 copy-done.4
  12.3 1.1 %broadcast_select_fusion = f32[3,5,2,96,64]{3,4,2,1,0:T(8,128)} fusion(f32[3,5,2,96,64]{3,4,2,1,0:T(8,128)S(1)} %copy.153, f32[3,5,2,96,64]{3,4,2,1,0:T(8,128)S(1)} %copy-done.4, pred[]{:T(512)S(6)} %eq.71), kind=kLoop, calls=%fused_computation.44 | loop fusion | flops 184320 | bytes 2211841 | tf_op jit(solution)/shard_map/jit(_where)/select_n | solution.py:213
  15.2 2.4 %collective-permute-start.2 = (f32[5,2,68,2]{3,2,1,0:T(8,128)S(1)}, f32[5,2,68,2]{3,2,1,0:T(8,128)S(1)}, u32[]{:S(2)}, u32[]{:S(2)}) collective-permute-start(f32[5,2,68,2]{3,2,1,0:T(8,128)S(1)} %get-tuple-element.17), channel_id=1, source_target_pairs={{0,1},{1,2},{2,3},{4,5},{5,6},{6,7},{8,9},{9,10},{10,11},{12,13},{... | collective-permute-start | bytes 16328 | tf_op jit(solution)/shard_map/ppermute | solution.py:29
  17.6 1.3 %collective-permute-start.3 = (f32[5,2,68,2]{3,2,1,0:T(8,128)S(1)}, f32[5,2,68,2]{3,2,1,0:T(8,128)S(1)}, u32[]{:S(2)}, u32[]{:S(2)}) collective-permute-start(f32[5,2,68,2]{3,2,1,0:T(8,128)S(1)} %get-tuple-element.18), channel_id=1, source_target_pairs={{1,0},{2,1},{3,2},{5,4},{6,5},{7,6},{9,8},{10,9},{11,10},{13,12},{... | collective-permute-start | bytes 16328 | tf_op jit(solution)/shard_map/ppermute | solution.py:31
  19.2 2.6 %collective-permute-done.3 = f32[5,2,68,2]{3,2,1,0:T(8,128)S(1)} collective-permute-done((f32[5,2,68,2]{3,2,1,0:T(8,128)S(1)}, f32[5,2,68,2]{3,2,1,0:T(8,128)S(1)}, u32[]{:S(2)}, u32[]{:S(2)}) %collective-permute-start.3) | collective-permute-done | bytes 5472 | tf_op jit(solution)/shard_map/ppermute | solution.py:31
  22.2 1.1 %fusion.16 = f32[5,2,66,130]{3,2,1,0:T(8,128)S(1)} fusion(f32[5,2,68,132]{3,2,1,0:T(8,128)S(1)} %pad_maximum_fusion.8, f32[5,2,68,2]{3,2,1,0:T(8,128)S(1)} %collective-permute-done.2, f32[5,2,2,128]{3,2,1,0:T(2,128)S(1)} %collective-permute-done.1, f32[5,2,64,128]{3,2,1,0:T(8,128)S(1)} %copy-done.5, f32[5,2,2,128]{3,2,1,0:T(2,128)S(1)} %collective-permute-done, ...), kind=kLoop, calls=%fused_computation.24 | loop fusion | flops 1630200 | bytes 4397216 | tf_op jit(solution)/shard_map/jit(_where)/select_n | solution.py:228
  24.4 0.6 fusion.6
  25.8 0.6 fusion.60
  28.1 0.6 fusion.2
  31.4 26.8 %shard_map.95 = f32[120,128]{1,0:T(8,128)S(1)} custom-call(f32[16,120,128]{2,1,0:T(8,128)S(1)} %copy.128.x_ref), custom_call_target="tpu_custom_call" | custom-call | tf_op jit(solution)/shard_map/pallas_call | solution.py:112
  58.2 2.8 %copy.109 = f32[3,5,2,96,64]{4,3,2,1,0:T(8,128)} copy(f32[3,5,2,96,64]{3,4,2,1,0:T(8,128)} %collective-permute-done.4) | data formatting | bytes 1474560 | tf_op jit(solution)/shard_map/ppermute | solution.py:214
  61.0 1.4 %pad_maximum_fusion.10 = (f32[3,5,2,16,256]{4,3,2,1,0:T(8,128)S(1)}, f32[3,5,2,16,256]{4,3,2,1,0:T(8,128)S(1)}) fusion(f32[3,5,2,96,64]{4,3,2,1,0:T(8,128)} %copy.109, f32[3,5,2,96,192]{4,3,2,1,0:T(8,128)S(1)} %copy-done.2), kind=kLoop, calls=%fused_computation.39 | loop fusion | flops 245760 | bytes 3932160 | tf_op jit(solution)/shard_map/slice | solution.py:26
  62.4 7.9 %collective-permute-start.5 = (f32[3,5,2,16,256]{4,3,2,1,0:T(8,128)S(1)}, f32[3,5,2,16,256]{4,3,2,1,0:T(8,128)S(1)}, u32[]{:S(2)}, u32[]{:S(2)}) collective-permute-start(f32[3,5,2,16,256]{4,3,2,1,0:T(8,128)S(1)} %get-tuple-element.9), channel_id=1, source_target_pairs={{0,4},{4,8},{8,12},{1,5},{5,9},{9,13},{2,6},{6,10},{10,14},{3,7},{... | collective-permute-start | bytes 1474568 | tf_op jit(solution)/shard_map/ppermute | solution.py:29
  70.3 1.5 %collective-permute-start.6 = (f32[3,5,2,16,256]{4,3,2,1,0:T(8,128)S(1)}, f32[3,5,2,16,256]{4,3,2,1,0:T(8,128)S(1)}, u32[]{:S(2)}, u32[]{:S(2)}) collective-permute-start(f32[3,5,2,16,256]{4,3,2,1,0:T(8,128)S(1)} %get-tuple-element.10), channel_id=1, source_target_pairs={{4,0},{8,4},{12,8},{5,1},{9,5},{13,9},{6,2},{10,6},{14,10},{7,3},{... | collective-permute-start | bytes 1474568 | tf_op jit(solution)/shard_map/ppermute | solution.py:31
  72.1 1.1 %convolution_bitcast_fusion.we_ref = f32[3,5,2,128,4]{4,3,2,1,0:T(8,128)S(1)} fusion(f32[3,4,5,2,128]{4,3,2,1,0:T(2,128)S(1)} %bitcast.151, s32[128]{0:T(128)S(1)} %fusion.84, pred[128]{0:T(512)(128)(4,1)S(1)} %iota_compare_fusion.3), kind=kOutput, calls=%fused_computation.5 | convolution fusion | flops 23642112 | bytes 123520 | tf_op jit(solution)/shard_map/nkfvl,lr->nfvrk/dot_general | solution.py:281
  73.2 7.4 %collective-permute-done.5 = f32[3,5,2,16,256]{4,3,2,1,0:T(8,128)S(1)} collective-permute-done((f32[3,5,2,16,256]{4,3,2,1,0:T(8,128)S(1)}, f32[3,5,2,16,256]{4,3,2,1,0:T(8,128)S(1)}, u32[]{:S(2)}, u32[]{:S(2)}) %collective-permute-start.5) | collective-permute-done | bytes 491552 | tf_op jit(solution)/shard_map/ppermute | solution.py:29
  80.6 4.1 %collective-permute-done.6 = f32[3,5,2,16,256]{4,3,2,1,0:T(8,128)S(1)} collective-permute-done((f32[3,5,2,16,256]{4,3,2,1,0:T(8,128)S(1)}, f32[3,5,2,16,256]{4,3,2,1,0:T(8,128)S(1)}, u32[]{:S(2)}, u32[]{:S(2)}) %collective-permute-start.6) | collective-permute-done | bytes 491552 | tf_op jit(solution)/shard_map/ppermute | solution.py:31
  84.7 0.7 pad_maximum_fusion.x_ref
  85.4 13.5 %shard_map.96 = f32[3,5,2,96,192]{4,3,2,1,0:T(8,128)} custom-call(s32[12]{0:T(128)S(1)} %reshape.412.offs, s32[2]{0:T(128)S(1)} %pad_add_fusion.place, f32[5]{0:T(128)S(1)} %copy-done.1, f32[5]{0:T(128)S(1)} %copy-done, f32[3,5,2,128,256]{4,3,2,1,0:T(8,128)S(1)} %pad_maximum_fusion.x_ref, f32[3,5,2,4,256]{4,3,2,1,0:T(4,128)S(1)} %convolution_bitcast_fusion.1.sn_ref, ...), custom_call_target="tpu_custom_call" | custom-call | tf_op jit(solution)/shard_map/pallas_call | solution.py:181
  (83 shorter events, 9.3 us)
Async XLA Ops:
  1.4 13.5 %collective-permute-start = (f32[5,2,2,128]{3,2,1,0:T(2,128)S(1)}, f32[5,2,2,128]{3,2,1,0:T(2,128)S(1)}, u32[]{:S(2)}, u32[]{:S(2)}) collective-permute-start(f32[5,2,2,128]{3,2,1,0:T(2,128)S(1)} %get-tuple-element.19), channel_id=1, source_target_pairs={{0,4},{4,8},{8,12},{1,5},{5,9},{9,13},{2,6},{6,10},{10,14},{3,7},{... | collective-permute-start | bytes 30728 | tf_op jit(solution)/shard_map/ppermute | solution.py:29
  6.4 8.6 %collective-permute-start.1 = (f32[5,2,2,128]{3,2,1,0:T(2,128)S(1)}, f32[5,2,2,128]{3,2,1,0:T(2,128)S(1)}, u32[]{:S(2)}, u32[]{:S(2)}) collective-permute-start(f32[5,2,2,128]{3,2,1,0:T(2,128)S(1)} %get-tuple-element.20), channel_id=1, source_target_pairs={{4,0},{8,4},{12,8},{5,1},{9,5},{13,9},{6,2},{10,6},{14,10},{7,3},{... | collective-permute-start | bytes 30728 | tf_op jit(solution)/shard_map/ppermute | solution.py:31
  11.1 1.2 %copy-start.4 = (f32[3,5,2,96,64]{3,4,2,1,0:T(8,128)S(1)}, f32[3,5,2,96,64]{3,4,2,1,0:T(8,128)}, u32[]{:S(2)}) copy-start(f32[3,5,2,96,64]{3,4,2,1,0:T(8,128)} %copy.154) | copy-start | bytes 2211844
  11.1 2.4 %copy-start.7 = (s32[3,6,2]{1,2,0:T(2,128)S(1)}, s32[3,6,2]{1,2,0:T(2,128)}, u32[]{:S(2)}) copy-start(s32[3,6,2]{1,2,0:T(2,128)} %param.12) | copy-start | bytes 436
  11.1 2.4 %copy-start.8 = (s32[6]{0:T(128)S(1)}, s32[6]{0:T(128)}, u32[]{:S(2)}) copy-start(s32[6]{0:T(128)} %param.13) | copy-start | bytes 76
  11.1 3.5 %copy-start.9 = (s32[4]{0:T(128)S(1)}, s32[4]{0:T(128)}, u32[]{:S(2)}) copy-start(s32[4]{0:T(128)} %constant.96.clone) | copy-start | bytes 52
  11.6 3.4 %copy-start.5 = (f32[5,2,64,128]{3,2,1,0:T(8,128)S(1)}, f32[5,2,64,128]{3,2,1,0:T(8,128)}, u32[]{:S(2)}) copy-start(f32[5,2,64,128]{3,2,1,0:T(8,128)} %param.8) | copy-start | bytes 983044
  12.3 9.9 %copy-start = (f32[5]{0:T(128)S(1)}, f32[5]{0:T(128)}, u32[]{:S(2)}) copy-start(f32[5]{0:T(128)} %vertical.1) | copy-start | bytes 64
  12.3 9.9 %copy-start.1 = (f32[5]{0:T(128)S(1)}, f32[5]{0:T(128)}, u32[]{:S(2)}) copy-start(f32[5]{0:T(128)} %lateral.1) | copy-start | bytes 64
  13.4 44.9 %collective-permute-start.4 = (f32[3,5,2,96,64]{3,4,2,1,0:T(8,128)}, f32[3,5,2,96,64]{3,4,2,1,0:T(8,128)}, u32[]{:S(2)}, u32[]{:S(2)}) collective-permute-start(f32[3,5,2,96,64]{3,4,2,1,0:T(8,128)} %broadcast_select_fusion), channel_id=1, source_target_pairs={{0,1},{1,0},{2,3},{3,2},{4,5},{5,4},{6,7},{7,6},{8,9},{9,8},{10,11... | collective-permute-start | bytes 2211848 | tf_op jit(solution)/shard_map/ppermute | solution.py:214
  15.2 4.0 %collective-permute-start.2 = (f32[5,2,68,2]{3,2,1,0:T(8,128)S(1)}, f32[5,2,68,2]{3,2,1,0:T(8,128)S(1)}, u32[]{:S(2)}, u32[]{:S(2)}) collective-permute-start(f32[5,2,68,2]{3,2,1,0:T(8,128)S(1)} %get-tuple-element.17), channel_id=1, source_target_pairs={{0,1},{1,2},{2,3},{4,5},{5,6},{6,7},{8,9},{9,10},{10,11},{12,13},{... | collective-permute-start | bytes 16328 | tf_op jit(solution)/shard_map/ppermute | solution.py:29
  17.6 4.2 %collective-permute-start.3 = (f32[5,2,68,2]{3,2,1,0:T(8,128)S(1)}, f32[5,2,68,2]{3,2,1,0:T(8,128)S(1)}, u32[]{:S(2)}, u32[]{:S(2)}) collective-permute-start(f32[5,2,68,2]{3,2,1,0:T(8,128)S(1)} %get-tuple-element.18), channel_id=1, source_target_pairs={{1,0},{2,1},{3,2},{5,4},{6,5},{7,6},{9,8},{10,9},{11,10},{13,12},{... | collective-permute-start | bytes 16328 | tf_op jit(solution)/shard_map/ppermute | solution.py:31
  23.8 3.3 %copy-start.6 = (f32[5,2,64,128]{3,2,1,0:T(8,128)}, f32[5,2,64,128]{3,2,1,0:T(8,128)S(1)}, u32[]{:S(2)}) copy-start(f32[5,2,64,128]{3,2,1,0:T(8,128)S(1)} %get-tuple-element.14) | copy-start | bytes 983044
  31.1 29.9 %copy-start.2 = (f32[3,5,2,96,192]{4,3,2,1,0:T(8,128)S(1)}, f32[3,5,2,96,192]{4,3,2,1,0:T(8,128)}, u32[]{:S(2)}) copy-start(f32[3,5,2,96,192]{4,3,2,1,0:T(8,128)} %param.9) | copy-start | bytes 6635524
  61.0 23.7 %copy-start.3 = (f32[3,5,2,96,64]{4,3,2,1,0:T(8,128)S(1)}, f32[3,5,2,96,64]{4,3,2,1,0:T(8,128)}, u32[]{:S(2)}) copy-start(f32[3,5,2,96,64]{4,3,2,1,0:T(8,128)} %copy.109) | copy-start | bytes 2211844
  62.4 18.1 %collective-permute-start.5 = (f32[3,5,2,16,256]{4,3,2,1,0:T(8,128)S(1)}, f32[3,5,2,16,256]{4,3,2,1,0:T(8,128)S(1)}, u32[]{:S(2)}, u32[]{:S(2)}) collective-permute-start(f32[3,5,2,16,256]{4,3,2,1,0:T(8,128)S(1)} %get-tuple-element.9), channel_id=1, source_target_pairs={{0,4},{4,8},{8,12},{1,5},{5,9},{9,13},{2,6},{6,10},{10,14},{3,7},{... | collective-permute-start | bytes 1474568 | tf_op jit(solution)/shard_map/ppermute | solution.py:29
  70.3 14.4 %collective-permute-start.6 = (f32[3,5,2,16,256]{4,3,2,1,0:T(8,128)S(1)}, f32[3,5,2,16,256]{4,3,2,1,0:T(8,128)S(1)}, u32[]{:S(2)}, u32[]{:S(2)}) collective-permute-start(f32[3,5,2,16,256]{4,3,2,1,0:T(8,128)S(1)} %get-tuple-element.10), channel_id=1, source_target_pairs={{4,0},{8,4},{12,8},{5,1},{9,5},{13,9},{6,2},{10,6},{14,10},{7,3},{... | collective-permute-start | bytes 1474568 | tf_op jit(solution)/shard_map/ppermute | solution.py:31

commit v2 on v1

v2 whole, which is shorter than its diff:
```python
import functools
import jax
import jax.numpy as jnp
from jax import lax
from jax.experimental import pallas as pl
from jax.experimental.pallas import tpu as pltpu
from jax.sharding import PartitionSpec as P

FP = 128
BWP = 2
MOVE = 2
HALO = 16
LANES = 128
ALONG = 72
SPAN = 3 * FP
BORDER = 3 * BWP
EXACT = lax.Precision.HIGHEST


def select_rows(picker, table):
    return jnp.sum(picker[:, :, None] * table[None, :, :], axis=1)


MESH = pl.DeviceIdType.MESH


def halo_kernel(counts, p_ref, n_ref, lat_ref, ver_ref, one_ref, two_ref, w_ref,
                field, side, pack, held, cols_out, cols_in, send, recv):
    tiles, groups, levs = counts
    tile_at = lax.axis_index("tile")
    nest_at = lax.axis_index("nest")
    lev_at = lax.axis_index("lev")
    planes, prow, pcol = p_ref.shape
    blocks, rows, cols = n_ref.shape
    half = cols - LANES
    edge = 8
    above = tile_at > 0
    below = tile_at < tiles - 1
    beyond = ((lev_at == 0) & (nest_at > 0)) | ((lev_at == 1) & (nest_at < groups - 1))
    step_out = 2 * lev_at - 1
    sibling = {"lev": 1 - lev_at}
    outer = {"nest": jnp.clip(nest_at + step_out, 0, groups - 1), "lev": 1 - lev_at}
    upper = {"tile": jnp.maximum(tile_at - 1, 0)}
    lower = {"tile": jnp.minimum(tile_at + 1, tiles - 1)}

    def remote(src, dst, at, landing, place):
        return pltpu.make_async_remote_copy(
            src_ref=src,
            dst_ref=dst,
            send_sem=send.at[at],
            recv_sem=recv.at[landing],
            device_id=place,
            device_id_type=MESH,
        )

    barrier = pltpu.get_barrier_semaphore()

    def greet(place):
        pl.semaphore_signal(barrier, inc=1, device_id=place, device_id_type=MESH)

    greet(sibling)
    pl.when(above)(lambda: greet(upper))
    pl.when(below)(lambda: greet(lower))
    pl.when(beyond)(lambda: greet(outer))
    pl.semaphore_wait(
        barrier,
        1 + above.astype(jnp.int32) + below.astype(jnp.int32) + beyond.astype(jnp.int32),
    )

    rows_up = remote(p_ref.at[:, pl.ds(0, edge)], field.at[:, pl.ds(prow + edge, edge)], 0, 0, upper)
    rows_down = remote(p_ref.at[:, pl.ds(prow - edge, edge)], field.at[:, pl.ds(0, edge)], 1, 1, lower)
    pl.when(above)(rows_up.start)
    pl.when(below)(rows_down.start)

    def gather(i, carry):
        def nearer(b):
            return jnp.where(lev_at == 0, n_ref[b, :, LANES:], n_ref[b, :, :half])

        pack[i] = jnp.concatenate([nearer(2 * i), nearer(2 * i + 1)], axis=1)
        return carry

    lax.fori_loop(0, blocks // 2, gather, 0)
    across = remote(pack, held, 4, 4, sibling)
    across.start()

    field[:, edge : edge + prow, :] = p_ref[...]

    @pl.when(jnp.logical_not(above))
    def _():
        field[:, :edge, :] = jnp.zeros((planes, edge, pcol), jnp.float32)

    @pl.when(jnp.logical_not(below))
    def _():
        field[:, prow + edge :, :] = jnp.zeros((planes, edge, pcol), jnp.float32)

    pl.when(above)(rows_up.wait_send)
    pl.when(below)(rows_down.wait_send)
    pl.when(below)(rows_up.wait_recv)
    pl.when(above)(rows_down.wait_recv)

    tall = prow + 2 * edge
    lane = lax.broadcasted_iota(jnp.int32, (tall, LANES), 1)
    first = jnp.zeros((tall, LANES), jnp.float32)
    last = jnp.zeros((tall, LANES), jnp.float32)
    for f in range(planes):
        mine = (lane == 2 * f) | (lane == 2 * f + 1)
        here = field[f]
        first = jnp.where(mine, pltpu.roll(here, 2 * f, 1) if f else here, first)
        last = jnp.where(mine, pltpu.roll(here, 2 * f + 2, 1), last)
    cols_out[0] = jnp.where(lev_at == 0, last, first)
    cols_out[1] = jnp.where(lev_at == 0, first, last)
    to_sibling = remote(cols_out.at[0], cols_in.at[0], 2, 2, sibling)
    to_outer = remote(cols_out.at[1], cols_in.at[1], 3, 3, outer)
    to_sibling.start()
    pl.when(beyond)(to_outer.start)

    @pl.when(jnp.logical_not(beyond))
    def _():
        cols_in[1] = jnp.zeros((tall, LANES), jnp.float32)

    across.wait()

    def widen(i, carry):
        both = held[i]
        for o in range(2):
            b = 2 * i + o
            w_ref[b, HALO : HALO + rows, :LANES] = n_ref[b, :, :LANES]
            w_ref[b, HALO : HALO + rows, LANES:] = jnp.concatenate(
                [n_ref[b, :, LANES:], both[:, o * half : (o + 1) * half]], axis=1
            )
        return carry

    lax.fori_loop(0, blocks // 2, widen, 0)
    nest_up = remote(w_ref.at[:, pl.ds(HALO, HALO)], w_ref.at[:, pl.ds(HALO + rows, HALO)], 5, 5, upper)
    nest_down = remote(w_ref.at[:, pl.ds(rows, HALO)], w_ref.at[:, pl.ds(0, HALO)], 6, 6, lower)
    pl.when(above)(nest_up.start)
    pl.when(below)(nest_down.start)

    @pl.when(jnp.logical_not(above))
    def _():
        w_ref[:, :HALO, :] = jnp.zeros((blocks, HALO, 2 * LANES), jnp.float32)

    @pl.when(jnp.logical_not(below))
    def _():
        w_ref[:, HALO + rows :, :] = jnp.zeros((blocks, HALO, 2 * LANES), jnp.float32)

    to_sibling.wait()
    pl.when(beyond)(to_outer.wait)
    left = jnp.where(lev_at == 0, cols_in[1], cols_in[0])
    right = jnp.where(lev_at == 0, cols_in[0], cols_in[1])
    for f in range(planes):
        after = pltpu.roll(right, LANES - 2 * f, 1) if f else right
        before = pltpu.roll(left, LANES - 2 - 2 * f, 1)
        side[f] = jnp.where(lane < 2, after, jnp.where(lane >= LANES - 2, before, 0.0))

    wide = 2 * LANES
    x = tile_at * prow - edge + lax.broadcasted_iota(jnp.int32, (tall, wide), 0)
    y = lax.broadcasted_iota(jnp.int32, (tall, wide), 1)
    y = (nest_at * levs + lev_at) * pcol + jnp.where(y >= LANES + 2, y - wide, y)
    domain = (x >= 0) & (x < prow * tiles) & (y >= 0) & (y < pcol * groups * levs)

    def advance(i, carry):
        rate_l = lat_ref[i]
        rate_v = ver_ref[i]
        now = [jnp.concatenate([field[2 * i + v], side[2 * i + v]], axis=1) for v in range(2)]
        for step, out in ((0, one_ref), (1, two_ref)):
            later = []
            for v in range(2):
                here = now[v]
                around = (
                    pltpu.roll(here, 1, 0)
                    + pltpu.roll(here, tall - 1, 0)
                    + pltpu.roll(here, 1, 1)
                    + pltpu.roll(here, wide - 1, 1)
                    - 4.0 * here
                )
                change = rate_l * around + rate_v * (now[1 - v] - 2.0 * here)
                later.append(jnp.where(domain, here + change, 0.0))
            now = later
            for v in range(2):
                out[2 * i + v] = now[v][edge : edge + prow, :pcol]
        return carry

    lax.fori_loop(0, planes // 2, advance, 0)

    pl.when(above)(nest_up.wait_send)
    pl.when(below)(nest_down.wait_send)
    pl.when(below)(nest_up.wait_recv)
    pl.when(above)(nest_down.wait_recv)


def exchange_halos(parent, nests, lateral, vertical, counts):
    planes, prow, pcol = parent.shape
    blocks, rows, cols = nests.shape
    assert pcol == LANES and planes % 2 == 0 and blocks % 2 == 0 and 2 * (cols - LANES) == LANES
    vmem = pl.BlockSpec(memory_space=pltpu.VMEM)
    smem = pl.BlockSpec(memory_space=pltpu.SMEM)
    tall = prow + 16
    shape = lambda *dims: jax.ShapeDtypeStruct(dims, jnp.float32)
    return pl.pallas_call(
        functools.partial(halo_kernel, counts),
        out_shape=(
            shape(planes, prow, pcol),
            shape(planes, prow, pcol),
            shape(blocks, rows + 2 * HALO, 2 * LANES),
        ),
        in_specs=[vmem, vmem, smem, smem],
        out_specs=(vmem, vmem, vmem),
        scratch_shapes=[
            pltpu.VMEM((planes, tall, LANES), jnp.float32),
            pltpu.VMEM((planes, tall, LANES), jnp.float32),
            pltpu.VMEM((blocks // 2, rows, LANES), jnp.float32),
            pltpu.VMEM((blocks // 2, rows, LANES), jnp.float32),
            pltpu.VMEM((2, tall, LANES), jnp.float32),
            pltpu.VMEM((2, tall, LANES), jnp.float32),
            pltpu.SemaphoreType.DMA((7,)),
            pltpu.SemaphoreType.DMA((7,)),
        ],
        compiler_params=pltpu.CompilerParams(
            collective_id=1, has_side_effects=True, vmem_limit_bytes=48 * 1024 * 1024
        ),
    )(parent, nests, lateral, vertical)


def zone_kernel(counts, we_ref, sn_ref, we_out, sn_out, we_sum, sn_sum, we_in, sn_in,
                pair_send, pair_recv, we_send, we_recv, sn_send, sn_recv):
    tiles, groups, levs = counts
    chips = tiles * groups
    tile_at = lax.axis_index("tile")
    nest_at = lax.axis_index("nest")
    lev_at = lax.axis_index("lev")
    me = tile_at * groups + nest_at
    edge = (tile_at == 0) | (tile_at == tiles - 1)
    sibling = {"lev": 1 - lev_at}

    def chip(k):
        other = lax.rem(me + k, chips)
        return other, other // groups, lax.rem(other, groups)

    def we_copy(k):
        other, t, g = chip(k)
        return pltpu.make_async_remote_copy(
            src_ref=we_sum.at[other],
            dst_ref=we_in.at[k],
            send_sem=we_send.at[k],
            recv_sem=we_recv.at[k],
            device_id={"tile": t, "nest": g},
            device_id_type=MESH,
        )

    def sn_copy(k):
        other, t, g = chip(k)
        side = jnp.where(t == 0, 0, 1)
        return pltpu.make_async_remote_copy(
            src_ref=sn_sum.at[side * groups + g],
            dst_ref=sn_in.at[k],
            send_sem=sn_send.at[k],
            recv_sem=sn_recv.at[k],
            device_id={"tile": t, "nest": g},
            device_id_type=MESH,
        )

    def to_edge(k):
        other, t, g = chip(k)
        return (t == 0) | (t == tiles - 1)

    barrier = pltpu.get_barrier_semaphore()
    pl.semaphore_signal(barrier, inc=1, device_id=sibling, device_id_type=MESH)

    def greet(k, carry):
        other, t, g = chip(k)
        pl.semaphore_signal(
            barrier, inc=1, device_id={"tile": t, "nest": g}, device_id_type=MESH
        )
        return carry

    lax.fori_loop(1, chips, greet, 0)
    pl.semaphore_wait(barrier, chips)

    pairs = []
    for at, (src, dst) in enumerate(((sn_ref, sn_sum), (we_ref, we_sum))):
        pair = pltpu.make_async_remote_copy(
            src_ref=src.at[1 - lev_at],
            dst_ref=dst,
            send_sem=pair_send.at[at],
            recv_sem=pair_recv.at[at],
            device_id=sibling,
            device_id_type=MESH,
        )
        pair.start()
        pairs.append(pair)
    pairs[0].wait()
    sn_sum[...] += sn_ref[lev_at]

    def begin_sn(k, carry):
        pl.when(to_edge(k))(lambda: sn_copy(k).start())
        return carry

    lax.fori_loop(1, chips, begin_sn, 0)
    pairs[1].wait()
    we_sum[...] += we_ref[lev_at]

    def begin_we(k, carry):
        we_copy(k).start()
        return carry

    lax.fori_loop(1, chips, begin_we, 0)

    we_out[...] = we_sum[me]
    side_at = jnp.where(tile_at == 0, 0, 1)
    sn_out[...] = sn_sum[side_at * groups + nest_at]

    def finish(k, carry):
        pl.when(to_edge(k))(lambda: sn_copy(k).wait_send())

        @pl.when(edge)
        def _():
            sn_copy(k).wait_recv()
            sn_out[...] += sn_in[k]

        we_copy(k).wait()
        we_out[...] += we_in[k]
        return carry

    lax.fori_loop(1, chips, finish, 0)


def sum_zones(we, sn, counts):
    tiles, groups, levs = counts
    chips = tiles * groups
    vmem = pl.BlockSpec(memory_space=pltpu.VMEM)
    return pl.pallas_call(
        functools.partial(zone_kernel, counts),
        out_shape=(
            jax.ShapeDtypeStruct(we.shape[2:], jnp.float32),
            jax.ShapeDtypeStruct(sn.shape[2:], jnp.float32),
        ),
        in_specs=[vmem, vmem],
        out_specs=(vmem, vmem),
        scratch_shapes=[
            pltpu.VMEM(we.shape[1:], jnp.float32),
            pltpu.VMEM(sn.shape[1:], jnp.float32),
            pltpu.VMEM((chips,) + we.shape[2:], jnp.float32),
            pltpu.VMEM((chips,) + sn.shape[2:], jnp.float32),
            pltpu.SemaphoreType.DMA((2,)),
            pltpu.SemaphoreType.DMA((2,)),
            pltpu.SemaphoreType.DMA((chips,)),
            pltpu.SemaphoreType.DMA((chips,)),
            pltpu.SemaphoreType.DMA((chips,)),
            pltpu.SemaphoreType.DMA((chips,)),
        ],
        compiler_params=pltpu.CompilerParams(
            collective_id=0, has_side_effects=True, vmem_limit_bytes=48 * 1024 * 1024
        ),
    )(we, sn)


def nest_kernel(rows, cols, steps, offs, place, lateral, vertical, x_ref, sn_ref, we_ref, o_ref):
    slot = pl.program_id(0)
    field = pl.program_id(1)
    slots = pl.num_programs(0)
    high, wide = x_ref.shape[3], x_ref.shape[4]
    rate_l = lateral[field]
    rate_v = vertical[field]
    r = lax.broadcasted_iota(jnp.int32, (high, wide), 0) + (place[0] * rows - HALO)
    j = lax.broadcasted_iota(jnp.int32, (high, wide), 1)
    c = j + place[1] * jnp.where(j >= cols, cols - wide, cols)
    gap_r = jnp.minimum(r, SPAN - 1 - r)
    gap_c = jnp.minimum(c, SPAN - 1 - c)
    gap = jnp.minimum(gap_r, gap_c)
    weight = jnp.maximum(BORDER - gap, 0).astype(jnp.float32) / jnp.float32(BORDER)
    inside = gap >= 1
    near_row = gap_r < BORDER
    second_row = ((r >= 3) & (r < BORDER)) | (r >= SPAN - 3)
    second_col = ((c >= 3) & (c < BORDER)) | (c >= SPAN - 3)
    state = [x_ref[0, 0, 0], x_ref[0, 0, 1]]
    for step in range(steps):
        at = (step * slots + slot) * 2
        down = offs[at]
        right = offs[at + 1]
        keep = (r + down >= 0) & (r + down < SPAN) & (c + right >= 0) & (c + right < SPAN)
        turn_r = lax.rem(high - down, high)
        turn_c = lax.rem(wide - right, wide)
        relaxed = []
        for v in range(2):
            k = 2 * step
            along = jnp.where(second_row, sn_ref[0, 0, v, k + 1 : k + 2, :], sn_ref[0, 0, v, k : k + 1, :])
            across = jnp.where(second_col, we_ref[0, 0, v, :, k + 1 : k + 2], we_ref[0, 0, v, :, k : k + 1])
            driving = jnp.where(near_row, along, across)
            moved = pltpu.roll(pltpu.roll(state[v], turn_r, 0), turn_c, 1)
            retained = jnp.where(keep, moved, driving)
            relaxed.append(retained + weight * (driving - retained))
        for v in range(2):
            here = relaxed[v]
            around = (
                pltpu.roll(here, 1, 0)
                + pltpu.roll(here, high - 1, 0)
                + pltpu.roll(here, 1, 1)
                + pltpu.roll(here, wide - 1, 1)
                - 4.0 * here
            )
            change = rate_l * around + rate_v * (relaxed[1 - v] - 2.0 * here)
            state[v] = jnp.where(inside, here + change, here)
    for v in range(2):
        o_ref[0, 0, v] = state[v][HALO : HALO + rows, :cols]


def advance_nests(wide_nests, along, across, offs, place, lateral, vertical, rows, cols, steps):
    slots, fields, levels, high, wide = wide_nests.shape
    spec = lambda *tail: pl.BlockSpec((1, 1) + tail, lambda n, f, *_: (n, f, 0, 0, 0))
    return pl.pallas_call(
        functools.partial(nest_kernel, rows, cols, steps),
        out_shape=jax.ShapeDtypeStruct((slots, fields, levels, rows, cols), jnp.float32),
        grid_spec=pltpu.PrefetchScalarGridSpec(
            num_scalar_prefetch=4,
            grid=(slots, fields),
            in_specs=[
                spec(levels, high, wide),
                spec(levels, 2 * steps, wide),
                spec(levels, high, 2 * steps),
            ],
            out_specs=spec(levels, rows, cols),
        ),
        compiler_params=pltpu.CompilerParams(vmem_limit_bytes=32 * 1024 * 1024),
    )(offs, place, lateral, vertical, wide_nests, along, across)


def per_device(parent_field, nest_fields, lateral_rate, vertical_rate, centres, slot_storm):
    fields, levels, prow, pcol = parent_field.shape
    slots, _, _, rows, cols = nest_fields.shape
    storms = slot_storm.shape[0]
    steps = centres.shape[0] - 1
    tiles = lax.axis_size("tile")
    groups = lax.axis_size("nest")
    levs = lax.axis_size("lev")
    tile_at = lax.axis_index("tile")
    nest_at = lax.axis_index("nest")
    lev_at = lax.axis_index("lev")
    coarse = rows // 3
    assert levs == 2 and tiles > 1 and steps == 2 and levels == 2

    counts = (tiles, groups, levs)
    planes = fields * levels
    first, second, wide_nests = exchange_halos(
        parent_field.reshape(planes, prow, pcol),
        nest_fields.reshape(slots * planes, rows, cols),
        lateral_rate,
        vertical_rate,
        counts,
    )
    high, wide = wide_nests.shape[1:]
    wide_nests = wide_nests.reshape(slots, fields, levels, high, wide)
    stages = (first, second)
    xg = tile_at * prow + jnp.arange(prow, dtype=jnp.int32)
    yg = (nest_at * levs + lev_at) * pcol + jnp.arange(pcol, dtype=jnp.int32)

    storm_ids = jnp.arange(storms, dtype=jnp.int32)
    pick = (slot_storm[:, None] == storm_ids[None, :]).astype(jnp.int32)
    place_at = [select_rows(pick, centres[n]) for n in range(steps + 1)]
    offs = jnp.stack([3 * (place_at[n + 1] - place_at[n]) for n in range(steps)])
    offs = lax.dynamic_slice_in_dim(offs, nest_at * slots, slots, 1).reshape(-1)

    edges = jnp.array([0, 1, FP - 2, FP - 1], jnp.int32)
    deep = coarse + 8
    rows_at = (jnp.arange(tiles, dtype=jnp.int32) * coarse - 4)[:, None] + jnp.arange(deep, dtype=jnp.int32)
    rows_at = jnp.where((rows_at >= 0) & (rows_at < FP), rows_at, -SPAN * SPAN)
    lanes = -(-slots * ALONG // LANES) * LANES
    lane = jnp.arange(lanes, dtype=jnp.int32)
    starts = jnp.array([0, FP - ALONG], jnp.int32)
    along_at = starts[None, :, None] + lane - ALONG * jnp.arange(slots, dtype=jnp.int32)[:, None, None]
    own_lane = lane // ALONG == jnp.arange(slots, dtype=jnp.int32)[:, None, None]
    along_at = jnp.where(own_lane, along_at, -SPAN * SPAN)
    sn_parts = []
    we_parts = []
    for n in range(steps):
        now = stages[n]
        corner = place_at[n + 1] - FP // 2
        row_edge = (corner[:, 0, None, None] + edges[None, :, None] == xg).astype(jnp.float32)
        col_edge = (corner[:, 1, None, None] + edges[None, :, None] == yg).astype(jnp.float32)
        col_at = corner[:, 1].reshape(groups, slots, 1, 1, 1) + along_at[None, :, :, None, :]
        col_pick = (col_at == yg[:, None]).astype(jnp.float32)
        row_pick = (corner[:, 0, None, None, None] + rows_at[None, :, :, None] == xg).astype(jnp.float32)
        sn = jnp.einsum("jrx,fxy->jrfy", row_edge, now, precision=EXACT)
        sn = sn.reshape(groups, slots, 2, 2, planes, pcol)
        sn_parts.append(jnp.einsum("gnhkfy,gnlyc->lhgkfc", sn, col_pick, precision=EXACT))
        we = jnp.einsum("jky,fxy->jkfx", col_edge, now, precision=EXACT)
        we = jnp.einsum("jtrx,jkfx->jtrkf", row_pick, we, precision=EXACT)
        we_parts.append(we.reshape(groups, slots, tiles, deep, levs, 2, planes))
    sn = jnp.stack(sn_parts, axis=3).reshape(levs, 2 * groups, steps * 2 * planes, lanes)
    we = jnp.stack(we_parts, axis=0)
    we = jnp.transpose(we, (5, 3, 1, 4, 2, 6, 0, 7))
    we = we.reshape(levs, tiles * groups, deep, slots * 2 * steps * planes)
    we = jnp.pad(we, ((0, 0), (0, 0), (0, 0), (0, -we.shape[3] % LANES)))
    we, sn = sum_zones(we, sn, counts)

    jj = jnp.arange(wide, dtype=jnp.int32)
    col_cell = jj + lev_at * jnp.where(jj >= cols, cols - wide, cols)
    row_cell = tile_at * rows - HALO + jnp.arange(high, dtype=jnp.int32)
    from_col = col_cell // 3 - lev_at * (FP - ALONG)
    spread_c = (own_lane[:, 0, :, None] & (from_col == (lane % ALONG)[:, None])).astype(jnp.float32)
    from_row = row_cell // 3 - (tile_at * coarse - 4)
    spread_r = (from_row[:, None] == jnp.arange(deep, dtype=jnp.int32)).astype(jnp.float32)
    along = jnp.einsum("ql,nlc->nqc", sn, spread_c, precision=EXACT)
    along = along.reshape(slots, 2 * steps, fields, levels, wide)
    along = jnp.transpose(along, (0, 2, 3, 1, 4))
    across = jnp.einsum("rq,qm->rm", spread_r, we, precision=EXACT)
    across = across[:, : slots * 2 * steps * planes].reshape(high, slots, 2, steps, fields, levels)
    across = jnp.transpose(across, (1, 4, 5, 0, 3, 2)).reshape(slots, fields, levels, high, 2 * steps)
    place = jnp.stack([tile_at, lev_at]).astype(jnp.int32)
    nests = advance_nests(
        wide_nests, along, across, offs, place, lateral_rate, vertical_rate, rows, cols, steps
    )
    return (second.reshape(parent_field.shape), nests)


def solution(mesh):
    placed = (
        P("member", None, "tile", ("nest", "lev")),
        P(("member", "nest"), None, None, "tile", "lev"),
        P(),
        P(),
        P("member", None, None),
        P("member"),
    )
    return jax.shard_map(
        per_device,
        mesh=mesh,
        in_specs=placed,
        out_specs=(
            P("member", None, "tile", ("nest", "lev")),
            P(("member", "nest"), None, None, "tile", "lev"),
        ),
        check_vma=False,
    )
```

time: 99.3 us -> 72.3 us (0.73)
  starting transfers between devices: 19.3 us -> 0 us
  waiting for transfers between devices: 14.1 us -> 0 us
  Pallas kernels: 40.3 us -> 51 us
  other arithmetic: 7.61 us -> 3.18 us
  matrix products: 5.1 us -> 6.17 us
    ppermute x7 -> x0, starting transfers between devices: 19.3 us -> none  [the longest x3 15.2 us: extended(): lax.ppermute(tail, axis, [(i, (i + 1) % count) for i in range(ends)])]
    ppermute x7 -> x0, waiting for transfers between devices: 14.1 us -> none  [the longest x3 7.36 us: extended(): lax.ppermute(tail, axis, [(i, (i + 1) % count) for i in range(ends)])]
    pallas_call x1 -> x2, Pallas kernels: 26.8 us -> 37.6 us  [the longest x1 23.3 us: exchange_halos(): pl.pallas_call(functools.partial(halo_kernel, counts), out_shape=(shape(p...]
    unnamed x22 -> x15, local copies, waits for them, and re-layouts: 2.59 us -> 6.95 us
    slice x10 -> x0, local copies, waits for them, and re-layouts: 3.56 us -> none  [the longest x1 2.03 us: per_device(): nest_fields[..., :cols - LANES]]
    ppermute x1 -> x0, local copies, waits for them, and re-layouts: 2.77 us -> none  [per_device(): other = lax.ppermute(nearer, 'lev', [(0, 1), (1, 0)])]
    select_n x4, other arithmetic: 2.31 us -> 0.17 us  [the longest x1 0.07 us: per_device(): rows_at = jnp.where((rows_at >= 0) & (rows_at < FP), rows_at, -SPAN * SPAN)]
    slice x2 -> x0, other arithmetic: 1.89 us -> none  [the longest x1 1.39 us: extended(): lax.slice_in_dim(cells, cells.shape[dim] - width, cells.shape[dim], axis=...]
  transfers between devices with their start and end apart: 7 -> 0, of which waited for: 3 -> 0; matrix products, arithmetic and copies ran while one was open for 18% -> 0% of each run, Pallas kernels for 27% -> 0%
where the time goes in v2:
time: 72.3 us; the launch traced here: 72 us
  Pallas kernels  51 us (71%)
  local copies, waits for them, and re-layouts  10.7 us (15%)
  matrix products  6.17 us (9%)
  other arithmetic  3.18 us (4%)
  between operations  0.91 us (1%)
    pallas_call x1, Pallas kernels, exchange_halos(): pl.pallas_call(functools.partial(halo_kernel, counts), out_shape=(shape(p...  23.3 us
    pallas_call x1, Pallas kernels, sum_zones(): pl.pallas_call(functools.partial(zone_kernel, counts), out_shape=(jax.Sha...  14.3 us
    pallas_call x1, Pallas kernels, advance_nests(): pl.pallas_call(functools.partial(nest_kernel, rows, cols, steps), out_sha...  13.4 us
    unnamed x15, local copies, waits for them, and re-layouts  6.95 us
    dot_general x2, matrix products, per_device(): we = jnp.einsum('jtrx,jkfx->jtrkf', row_pick, we, precision=EXACT)  2.38 us

profile of v2, /device:TPU:0, one launch (start us, length us, event | category | flops | bytes accessed | tf_op | source)
XLA Modules:
  0.0 72.0 jit_solution(4576110041959589936)
XLA Ops:
  1.0 0.7 slice_bitcast_fusion.2
  1.7 0.7 %fusion.53 = s32[6,6]{1,0:T(8,128)S(1)} fusion(s32[6]{0:T(128)} %param.13), kind=kLoop, calls=%fused_computation.75 | loop fusion | flops 72 | bytes 168 | tf_op jit(solution)/shard_map/convert_element_type | solution.py:458
  2.4 0.4 multiply_reduce_fusion.1
  3.7 0.7 %broadcast_add_fusion.7 = (s32[6,4]{0,1:T(4,128)S(1)}, s32[6,4]{0,1:T(4,128)S(1)}, s32[6,4]{0,1:T(4,128)S(1)}, s32[6,4]{0,1:T(4,128)S(1)}) fusion(s32[6]{0:T(128)S(1)} %get-tuple-element.36, s32[4]{0:T(128)} %constant.87.clone, s32[6]{0:T(128)S(1)} %get-tuple-element.14, s32[6]{0:T(128)S(1)} %get-tuple-element.15, s32[6]{0:T(128)S(1)} %get-tuple-element.37), kind=kLoop, calls=%fused_computation.98 | loop fusion | flops 96 | bytes 496 | tf_op jit(solution)/shard_map/add | solution.py:478
  5.0 1.8 %copy-done.1 = f32[3,5,2,96,192]{4,3,2,1,0:T(8,128)S(1)} copy-done((f32[3,5,2,96,192]{4,3,2,1,0:T(8,128)S(1)}, f32[3,5,2,96,192]{4,3,2,1,0:T(8,128)}, u32[]{:S(2)}) %copy-start.1) | copy-done | bytes 2211864
  6.8 1.0 %copy-done.2 = f32[5,2,64,128]{3,2,1,0:T(8,128)S(1)} copy-done((f32[5,2,64,128]{3,2,1,0:T(8,128)S(1)}, f32[5,2,64,128]{3,2,1,0:T(8,128)}, u32[]{:S(2)}) %copy-start.2) | copy-done | bytes 327704
  7.8 0.7 copy-done.3
  8.4 0.7 copy-done.5
  9.1 23.3 %shard_map.95 = (f32[10,64,128]{2,1,0:T(8,128)S(1)}, f32[10,64,128]{2,1,0:T(8,128)S(1)}, f32[30,128,256]{2,1,0:T(8,128)}) custom-call(f32[10,64,128]{2,1,0:T(8,128)S(1)} %bitcast.108, f32[30,96,192]{2,1,0:T(8,128)S(1)} %bitcast.106, f32[5]{0:T(128)S(1)} %copy-done.3, f32[5]{0:T(128)S(1)} %copy-done.5), custom_call_target="tpu_custom_call" | custom-call | tf_op jit(solution)/shard_map/pallas_call | solution.py:200
  32.6 0.6 convolution_bitcast_fusion.2
  33.4 0.6 convolution_bitcast_fusion.1
  34.0 0.7 %fusion.9 = f32[2,2,2,1,2,10,256]{6,5,4,1,0,2,3:T(8,128)S(1)} fusion(s32[2,3,2,256]{3,1,2,0:T(4,128)S(1)} %get-tuple-element.20, s32[128]{0:T(128)S(1)} %iota_add_fusion.2, f32[2,3,2,2,10,128,1]{5,3,2,4,1,0,6:T(2,128)S(1)} %bitcast.116), kind=kOutput, calls=%fused_computation.7 | convolution fusion | flops 189136896 | bytes 299520 | tf_op jit(solution)/shard_map/gnhkfy,gnlyc->lhgkfc/dot_general | solution.py:485
  34.7 0.7 fusion.6
  35.8 1.2 %fusion.17 = f32[6,4,40,4,10]{2,4,3,1,0:T(8,128)S(1)} fusion(s32[6,4,40]{2,1,0:T(4,128)S(1)} %get-tuple-element.29, s32[64]{0:T(128)S(1)} %iota_add_fusion.3, f32[6,4,10,64,1]{3,1,2,0,4:T(4,128)S(1)} %convolution_bitcast_fusion.1), kind=kOutput, calls=%fused_computation.18 | convolution fusion | flops 29552640 | bytes 219136 | tf_op jit(solution)/shard_map/jtrx,jkfx->jtrkf/dot_general | solution.py:487
  37.0 0.4 copy.67
  37.4 1.2 %fusion.19 = f32[6,4,40,4,10]{2,4,3,1,0:T(8,128)S(1)} fusion(s32[64]{0:T(128)S(1)} %iota_add_fusion.3, s32[6,4,40]{2,1,0:T(4,128)S(1)} %get-tuple-element.28, f32[6,4,10,64,1]{3,1,2,0,4:T(4,128)S(1)} %convolution_bitcast_fusion.2), kind=kOutput, calls=%fused_computation.20 | convolution fusion | flops 29552640 | bytes 219136 | tf_op jit(solution)/shard_map/jtrx,jkfx->jtrkf/dot_general | solution.py:487
  38.6 0.4 copy.66
  39.0 0.5 pad_maximum_fusion
  39.9 14.3 %shard_map.96 = (f32[40,128]{1,0:T(8,128)S(1)}, f32[40,256]{1,0:T(8,128)S(1)}) custom-call(f32[2,8,40,128]{3,2,1,0:T(8,128)S(1)} %pad.4.we_ref, f32[2,4,40,256]{3,2,1,0:T(8,128)S(1)} %copy.74.sn_ref), custom_call_target="tpu_custom_call" | custom-call | tf_op jit(solution)/shard_map/pallas_call | solution.py:332
  54.2 0.5 convolution_bitcast_fusion
  55.1 0.6 copy.77.we_ref
  55.7 2.1 %copy-done = f32[30,128,256]{2,1,0:T(8,128)S(1)} copy-done((f32[30,128,256]{2,1,0:T(8,128)S(1)}, f32[30,128,256]{2,1,0:T(8,128)}, u32[]{:S(2)}) %copy-start) | copy-done | bytes 3932184
  57.9 13.4 %shard_map.97 = f32[3,5,2,96,192]{4,3,2,1,0:T(8,128)} custom-call(s32[12]{0:T(128)S(1)} %reshape.436.offs, s32[2]{0:T(128)S(1)} %pad_add_fusion.place, f32[5]{0:T(128)S(1)} %copy-done.4, f32[5]{0:T(128)S(1)} %copy-done.6, f32[3,5,2,128,256]{4,3,2,1,0:T(8,128)S(1)} %bitcast.104, f32[3,5,2,4,256]{4,3,2,1,0:T(4,128)S(1)} %bitcast.107, ...), custom_call_target="tpu_custom_call" | custom-call | tf_op jit(solution)/shard_map/pallas_call | solution.py:411
  71.2 0.7 %copy.117 = f32[5,2,64,128]{3,2,1,0:T(8,128)} copy(f32[5,2,64,128]{3,2,1,0:T(8,128)S(1)} %bitcast.105) | data formatting | bytes 655360
  (48 shorter events, 3.3 us)
Async XLA Ops:
  5.0 1.8 %copy-start.1 = (f32[3,5,2,96,192]{4,3,2,1,0:T(8,128)S(1)}, f32[3,5,2,96,192]{4,3,2,1,0:T(8,128)}, u32[]{:S(2)}) copy-start(f32[3,5,2,96,192]{4,3,2,1,0:T(8,128)} %param.9) | copy-start | bytes 6635524
  6.8 1.0 %copy-start.2 = (f32[5,2,64,128]{3,2,1,0:T(8,128)S(1)}, f32[5,2,64,128]{3,2,1,0:T(8,128)}, u32[]{:S(2)}) copy-start(f32[5,2,64,128]{3,2,1,0:T(8,128)} %param.8) | copy-start | bytes 983044
  7.8 0.7 copy-start.3
  8.4 0.7 copy-start.5
  39.8 15.9 %copy-start.4 = (f32[5]{0:T(128)S(1)}, f32[5]{0:T(128)}, u32[]{:S(2)}) copy-start(f32[5]{0:T(128)} %lateral.1) | copy-start | bytes 64
  39.9 15.9 %copy-start.6 = (f32[5]{0:T(128)S(1)}, f32[5]{0:T(128)}, u32[]{:S(2)}) copy-start(f32[5]{0:T(128)} %vertical.1) | copy-start | bytes 64
  55.7 2.1 %copy-start = (f32[30,128,256]{2,1,0:T(8,128)S(1)}, f32[30,128,256]{2,1,0:T(8,128)}, u32[]{:S(2)}) copy-start(f32[30,128,256]{2,1,0:T(8,128)} %get-tuple-element.8) | copy-start | bytes 11796484

commit v3 on v2

--- a/solution.py
+++ b/solution.py
@@ -17,15 +17,11 @@
 EXACT = lax.Precision.HIGHEST
 
 
-def select_rows(picker, table):
-    return jnp.sum(picker[:, :, None] * table[None, :, :], axis=1)
-
-
 MESH = pl.DeviceIdType.MESH
 
 
-def halo_kernel(counts, p_ref, n_ref, lat_ref, ver_ref, one_ref, two_ref, w_ref,
-                field, side, pack, held, cols_out, cols_in, send, recv):
+def halo_kernel(counts, p_hbm, n_hbm, lat_ref, ver_ref, stage_ref, w_ref,
+                p_ref, n_ref, load, field, side, pack, held, cols_out, cols_in, send, recv):
     tiles, groups, levs = counts
     tile_at = lax.axis_index("tile")
     nest_at = lax.axis_index("nest")
@@ -53,6 +49,10 @@
             device_id_type=MESH,
         )
 
+    load_parent = pltpu.make_async_copy(p_hbm, p_ref, load.at[0])
+    load_nests = pltpu.make_async_copy(n_hbm, n_ref, load.at[1])
+    load_parent.start()
+    load_nests.start()
     barrier = pltpu.get_barrier_semaphore()
 
     def greet(place):
@@ -67,10 +67,13 @@
         1 + above.astype(jnp.int32) + below.astype(jnp.int32) + beyond.astype(jnp.int32),
     )
 
+    load_parent.wait()
     rows_up = remote(p_ref.at[:, pl.ds(0, edge)], field.at[:, pl.ds(prow + edge, edge)], 0, 0, upper)
     rows_down = remote(p_ref.at[:, pl.ds(prow - edge, edge)], field.at[:, pl.ds(0, edge)], 1, 1, lower)
     pl.when(above)(rows_up.start)
     pl.when(below)(rows_down.start)
+
+    load_nests.wait()
 
     def gather(i, carry):
         def nearer(b):
@@ -124,25 +127,27 @@
         both = held[i]
         for o in range(2):
             b = 2 * i + o
-            w_ref[b, HALO : HALO + rows, :LANES] = n_ref[b, :, :LANES]
-            w_ref[b, HALO : HALO + rows, LANES:] = jnp.concatenate(
-                [n_ref[b, :, LANES:], both[:, o * half : (o + 1) * half]], axis=1
-            )
+            whole = n_ref[b, :, :LANES]
+            mixed = jnp.concatenate([n_ref[b, :, LANES:], both[:, o * half : (o + 1) * half]], axis=1)
+            w_ref[b, 0, HALO : HALO + rows, :] = jnp.where(lev_at == 0, whole, mixed)
+            w_ref[b, 1, HALO : HALO + rows, :] = jnp.where(lev_at == 0, mixed, whole)
         return carry
 
     lax.fori_loop(0, blocks // 2, widen, 0)
-    nest_up = remote(w_ref.at[:, pl.ds(HALO, HALO)], w_ref.at[:, pl.ds(HALO + rows, HALO)], 5, 5, upper)
-    nest_down = remote(w_ref.at[:, pl.ds(rows, HALO)], w_ref.at[:, pl.ds(0, HALO)], 6, 6, lower)
+    nest_up = remote(
+        w_ref.at[:, :, pl.ds(HALO, HALO)], w_ref.at[:, :, pl.ds(HALO + rows, HALO)], 5, 5, upper
+    )
+    nest_down = remote(w_ref.at[:, :, pl.ds(rows, HALO)], w_ref.at[:, :, pl.ds(0, HALO)], 6, 6, lower)
     pl.when(above)(nest_up.start)
     pl.when(below)(nest_down.start)
 
     @pl.when(jnp.logical_not(above))
     def _():
-        w_ref[:, :HALO, :] = jnp.zeros((blocks, HALO, 2 * LANES), jnp.float32)
+        w_ref[:, :, :HALO, :] = jnp.zeros((blocks, 2, HALO, LANES), jnp.float32)
 
     @pl.when(jnp.logical_not(below))
     def _():
-        w_ref[:, HALO + rows :, :] = jnp.zeros((blocks, HALO, 2 * LANES), jnp.float32)
+        w_ref[:, :, HALO + rows :, :] = jnp.zeros((blocks, 2, HALO, LANES), jnp.float32)
 
     to_sibling.wait()
     pl.when(beyond)(to_outer.wait)
@@ -163,7 +168,7 @@
         rate_l = lat_ref[i]
         rate_v = ver_ref[i]
         now = [jnp.concatenate([field[2 * i + v], side[2 * i + v]], axis=1) for v in range(2)]
-        for step, out in ((0, one_ref), (1, two_ref)):
+        for step in range(2):
             later = []
             for v in range(2):
                 here = now[v]
@@ -178,7 +183,7 @@
                 later.append(jnp.where(domain, here + change, 0.0))
             now = later
             for v in range(2):
-                out[2 * i + v] = now[v][edge : edge + prow, :pcol]
+                stage_ref[step, 2 * i + v] = now[v][edge : edge + prow, :pcol]
         return carry
 
     lax.fori_loop(0, planes // 2, advance, 0)
@@ -195,18 +200,21 @@
     assert pcol == LANES and planes % 2 == 0 and blocks % 2 == 0 and 2 * (cols - LANES) == LANES
     vmem = pl.BlockSpec(memory_space=pltpu.VMEM)
     smem = pl.BlockSpec(memory_space=pltpu.SMEM)
+    anywhere = pl.BlockSpec(memory_space=pl.ANY)
     tall = prow + 16
     shape = lambda *dims: jax.ShapeDtypeStruct(dims, jnp.float32)
     return pl.pallas_call(
         functools.partial(halo_kernel, counts),
         out_shape=(
-            shape(planes, prow, pcol),
-            shape(planes, prow, pcol),
-            shape(blocks, rows + 2 * HALO, 2 * LANES),
+            shape(2, planes, prow, pcol),
+            shape(blocks, 2, rows + 2 * HALO, LANES),
         ),
-        in_specs=[vmem, vmem, smem, smem],
-        out_specs=(vmem, vmem, vmem),
+        in_specs=[anywhere, anywhere, smem, smem],
+        out_specs=(vmem, vmem),
         scratch_shapes=[
+            pltpu.VMEM((planes, prow, pcol), jnp.float32),
+            pltpu.VMEM((blocks, rows, cols), jnp.float32),
+            pltpu.SemaphoreType.DMA((2,)),
             pltpu.VMEM((planes, tall, LANES), jnp.float32),
             pltpu.VMEM((planes, tall, LANES), jnp.float32),
             pltpu.VMEM((blocks // 2, rows, LANES), jnp.float32),
@@ -217,7 +225,7 @@
             pltpu.SemaphoreType.DMA((7,)),
         ],
         compiler_params=pltpu.CompilerParams(
-            collective_id=1, has_side_effects=True, vmem_limit_bytes=48 * 1024 * 1024
+            collective_id=1, has_side_effects=True, vmem_limit_bytes=24 * 1024 * 1024
         ),
     )(parent, nests, lateral, vertical)
 
@@ -328,6 +336,7 @@
 def sum_zones(we, sn, counts):
     tiles, groups, levs = counts
     chips = tiles * groups
+    room = 8 * 1024 * 1024 + 4 * sum(a.size * (2 * levs + 2) for a in (we, sn)) // levs
     vmem = pl.BlockSpec(memory_space=pltpu.VMEM)
     return pl.pallas_call(
         functools.partial(zone_kernel, counts),
@@ -350,78 +359,152 @@
             pltpu.SemaphoreType.DMA((chips,)),
         ],
         compiler_params=pltpu.CompilerParams(
-            collective_id=0, has_side_effects=True, vmem_limit_bytes=48 * 1024 * 1024
+            collective_id=0, has_side_effects=True, vmem_limit_bytes=room
         ),
     )(we, sn)
 
 
-def nest_kernel(rows, cols, steps, offs, place, lateral, vertical, x_ref, sn_ref, we_ref, o_ref):
-    slot = pl.program_id(0)
-    field = pl.program_id(1)
-    slots = pl.num_programs(0)
-    high, wide = x_ref.shape[3], x_ref.shape[4]
-    rate_l = lateral[field]
-    rate_v = vertical[field]
-    r = lax.broadcasted_iota(jnp.int32, (high, wide), 0) + (place[0] * rows - HALO)
-    j = lax.broadcasted_iota(jnp.int32, (high, wide), 1)
-    c = j + place[1] * jnp.where(j >= cols, cols - wide, cols)
-    gap_r = jnp.minimum(r, SPAN - 1 - r)
-    gap_c = jnp.minimum(c, SPAN - 1 - c)
-    gap = jnp.minimum(gap_r, gap_c)
-    weight = jnp.maximum(BORDER - gap, 0).astype(jnp.float32) / jnp.float32(BORDER)
-    inside = gap >= 1
-    near_row = gap_r < BORDER
-    second_row = ((r >= 3) & (r < BORDER)) | (r >= SPAN - 3)
-    second_col = ((c >= 3) & (c < BORDER)) | (c >= SPAN - 3)
-    state = [x_ref[0, 0, 0], x_ref[0, 0, 1]]
-    for step in range(steps):
-        at = (step * slots + slot) * 2
-        down = offs[at]
-        right = offs[at + 1]
+def nest_kernel(shape, steps, offs, place, lateral, vertical, x_ref, sn_ref, we_ref, o_hbm,
+                relaxed, state, done, col_mix, row_mix, sem):
+    slots, fields, levels, rows, cols = shape
+    high = x_ref.shape[2]
+    edge = 8
+    mid = high - 2 * edge
+    tile_at = place[0]
+    lev_at = place[1]
+    half = cols - LANES
+    lane = lax.broadcasted_iota(jnp.int32, (mid, LANES), 1)
+    row = lax.broadcasted_iota(jnp.int32, (mid, LANES), 0) + (tile_at * rows - HALO + edge)
+    near = jnp.where(
+        lev_at == 0, lane, jnp.where(lane < half, cols + LANES + lane, cols - LANES + lane)
+    )
+    far = jnp.where(lev_at == 0, LANES, cols) + lane
+    col_lane = jnp.where(lev_at == 0, 0, half - 1)
+    blocks = (HALO - edge, HALO - edge + rows - edge)
+
+    def mixing(r, c, down, right):
+        gap = jnp.minimum(jnp.minimum(r, SPAN - 1 - r), jnp.minimum(c, SPAN - 1 - c))
+        weight = jnp.maximum(BORDER - gap, 0).astype(jnp.float32) / jnp.float32(BORDER)
         keep = (r + down >= 0) & (r + down < SPAN) & (c + right >= 0) & (c + right < SPAN)
-        turn_r = lax.rem(high - down, high)
-        turn_c = lax.rem(wide - right, wide)
-        relaxed = []
-        for v in range(2):
-            k = 2 * step
-            along = jnp.where(second_row, sn_ref[0, 0, v, k + 1 : k + 2, :], sn_ref[0, 0, v, k : k + 1, :])
-            across = jnp.where(second_col, we_ref[0, 0, v, :, k + 1 : k + 2], we_ref[0, 0, v, :, k : k + 1])
-            driving = jnp.where(near_row, along, across)
-            moved = pltpu.roll(pltpu.roll(state[v], turn_r, 0), turn_c, 1)
-            retained = jnp.where(keep, moved, driving)
-            relaxed.append(retained + weight * (driving - retained))
-        for v in range(2):
-            here = relaxed[v]
-            around = (
-                pltpu.roll(here, 1, 0)
-                + pltpu.roll(here, high - 1, 0)
-                + pltpu.roll(here, 1, 1)
-                + pltpu.roll(here, wide - 1, 1)
-                - 4.0 * here
-            )
-            change = rate_l * around + rate_v * (relaxed[1 - v] - 2.0 * here)
-            state[v] = jnp.where(inside, here + change, here)
-    for v in range(2):
-        o_ref[0, 0, v] = state[v][HALO : HALO + rows, :cols]
-
-
-def advance_nests(wide_nests, along, across, offs, place, lateral, vertical, rows, cols, steps):
-    slots, fields, levels, high, wide = wide_nests.shape
-    spec = lambda *tail: pl.BlockSpec((1, 1) + tail, lambda n, f, *_: (n, f, 0, 0, 0))
+        return jnp.where(keep, weight, 1.0)
+
+    for n in range(slots):
+        shifts = []
+        for step in range(steps):
+            down = offs[(step * slots + n) * 2]
+            right = offs[(step * slots + n) * 2 + 1]
+            shifts.append((down, right))
+            weight = mixing(row, near, down, right)
+            side_row = (row < BORDER) | (row >= SPAN - BORDER)
+            gap_c = jnp.minimum(near, SPAN - 1 - near)
+            weight = jnp.where(side_row | (gap_c >= BORDER), 0.0, weight)
+            second = ((near >= 3) & (near < BORDER)) | (near >= SPAN - 3)
+            col_mix[step, 0] = 1.0 - weight
+            col_mix[step, 1] = jnp.where(second, 0.0, weight)
+            col_mix[step, 2] = jnp.where(second, weight, 0.0)
+            for side in range(2):
+                for at, start in enumerate(blocks):
+                    r = row[start : start + edge]
+                    c = (near, far)[side][start : start + edge]
+                    weight = mixing(r, c, down, right)
+                    weight = jnp.where((r < BORDER) | (r >= SPAN - BORDER), weight, 0.0)
+                    second = ((r >= 3) & (r < BORDER)) | (r >= SPAN - 3)
+                    row_mix[step, side, at, 0] = 1.0 - weight
+                    row_mix[step, side, at, 1] = jnp.where(second, 0.0, weight)
+                    row_mix[step, side, at, 2] = jnp.where(second, weight, 0.0)
+
+        def one_field(f, carry):
+            rate_l = lateral[f]
+            rate_v = vertical[f]
+            keep_rate = 1.0 - 4.0 * rate_l - 2.0 * rate_v
+            for step in range(steps):
+                down, right = shifts[step]
+                k = 2 * step
+                turn = lax.rem(LANES - right, LANES)
+                own = (lane + right >= 0) & (lane + right < LANES)
+                for v in range(levels):
+                    b = (n * fields + f) * levels + v
+                    if step == 0:
+                        source = [x_ref[b, side, pl.ds(edge + down, mid), :] for side in range(2)]
+                    else:
+                        source = [state[v, side, pl.ds(edge + down, mid), :] for side in range(2)]
+                    turned = [pltpu.roll(a, turn, 1) for a in source]
+                    first = jnp.where(own, turned[0], turned[1])
+                    first = (
+                        col_mix[step, 0] * first
+                        + col_mix[step, 1] * we_ref[b, edge : edge + mid, k : k + 1]
+                        + col_mix[step, 2] * we_ref[b, edge : edge + mid, k + 1 : k + 2]
+                    )
+                    relaxed[v, 0, edge : edge + mid] = first
+                    relaxed[v, 1, edge : edge + mid] = jnp.where(own, turned[1], turned[0])
+                    for side in range(2):
+                        wide = slice(side * LANES, (side + 1) * LANES)
+                        for at, start in enumerate(blocks):
+                            here = slice(edge + start, 2 * edge + start)
+                            relaxed[v, side, here] = (
+                                row_mix[step, side, at, 0] * relaxed[v, side, here]
+                                + row_mix[step, side, at, 1] * sn_ref[b, k : k + 1, wide]
+                                + row_mix[step, side, at, 2] * sn_ref[b, k + 1 : k + 2, wide]
+                            )
+                for v in range(levels):
+                    here = [relaxed[v, side, edge : edge + mid] for side in range(2)]
+                    west = [pltpu.roll(a, 1, 1) for a in here]
+                    east = [pltpu.roll(a, LANES - 1, 1) for a in here]
+                    results = []
+                    for side in range(2):
+                        around = (
+                            relaxed[v, side, edge - 1 : edge - 1 + mid]
+                            + relaxed[v, side, edge + 1 : edge + 1 + mid]
+                            + jnp.where(lane == 0, west[1 - side], west[side])
+                            + jnp.where(lane == LANES - 1, east[1 - side], east[side])
+                        )
+                        new = (
+                            keep_rate * here[side]
+                            + rate_l * around
+                            + rate_v * relaxed[1 - v, side, edge : edge + mid]
+                        )
+                        if side == 0:
+                            new = jnp.where(lane == col_lane, here[side], new)
+                        state[v, side, edge : edge + mid] = new
+                    for side in range(2):
+                        for at, start in enumerate(blocks):
+                            r = row[start : start + edge]
+                            spot = slice(edge + start, 2 * edge + start)
+                            state[v, side, spot] = jnp.where(
+                                (r == 0) | (r == SPAN - 1), relaxed[v, side, spot], state[v, side, spot]
+                            )
+            for v in range(levels):
+                near_part = state[v, 0, HALO : HALO + rows]
+                far_part = state[v, 1, HALO : HALO + rows]
+                done[n, f, v, :, :LANES] = jnp.where(lev_at == 0, near_part, far_part)
+                done[n, f, v, :, LANES:] = jnp.where(lev_at == 0, far_part, near_part)[:, :half]
+            return carry
+
+        lax.fori_loop(0, fields, one_field, 0)
+        pltpu.make_async_copy(done.at[n], o_hbm.at[n], sem.at[n]).start()
+    for n in range(slots):
+        pltpu.make_async_copy(done.at[n], o_hbm.at[n], sem.at[n]).wait()
+
+
+def advance_nests(wide_nests, along, across, offs, place, lateral, vertical, shape, steps):
+    slots, fields, levels, rows, cols = shape
+    high = wide_nests.shape[2]
+    vmem = pl.BlockSpec(memory_space=pltpu.VMEM)
+    smem = pl.BlockSpec(memory_space=pltpu.SMEM)
     return pl.pallas_call(
-        functools.partial(nest_kernel, rows, cols, steps),
-        out_shape=jax.ShapeDtypeStruct((slots, fields, levels, rows, cols), jnp.float32),
-        grid_spec=pltpu.PrefetchScalarGridSpec(
-            num_scalar_prefetch=4,
-            grid=(slots, fields),
-            in_specs=[
-                spec(levels, high, wide),
-                spec(levels, 2 * steps, wide),
-                spec(levels, high, 2 * steps),
-            ],
-            out_specs=spec(levels, rows, cols),
-        ),
-        compiler_params=pltpu.CompilerParams(vmem_limit_bytes=32 * 1024 * 1024),
+        functools.partial(nest_kernel, shape, steps),
+        out_shape=jax.ShapeDtypeStruct(shape, jnp.float32),
+        in_specs=[smem] * 4 + [vmem] * 3,
+        out_specs=pl.BlockSpec(memory_space=pl.ANY),
+        scratch_shapes=[
+            pltpu.VMEM((levels, 2, high, LANES), jnp.float32),
+            pltpu.VMEM((levels, 2, high, LANES), jnp.float32),
+            pltpu.VMEM(shape, jnp.float32),
+            pltpu.VMEM((steps, 3, high - 16, LANES), jnp.float32),
+            pltpu.VMEM((steps, 2, 2, 3, 8, LANES), jnp.float32),
+            pltpu.SemaphoreType.DMA((slots,)),
+        ],
+        compiler_params=pltpu.CompilerParams(vmem_limit_bytes=24 * 1024 * 1024),
     )(offs, place, lateral, vertical, wide_nests, along, across)
 
 
@@ -441,23 +524,22 @@
 
     counts = (tiles, groups, levs)
     planes = fields * levels
-    first, second, wide_nests = exchange_halos(
+    stages, wide_nests = exchange_halos(
         parent_field.reshape(planes, prow, pcol),
         nest_fields.reshape(slots * planes, rows, cols),
         lateral_rate,
         vertical_rate,
         counts,
     )
-    high, wide = wide_nests.shape[1:]
-    wide_nests = wide_nests.reshape(slots, fields, levels, high, wide)
-    stages = (first, second)
+    high = wide_nests.shape[2]
+    wide = 2 * LANES
     xg = tile_at * prow + jnp.arange(prow, dtype=jnp.int32)
     yg = (nest_at * levs + lev_at) * pcol + jnp.arange(pcol, dtype=jnp.int32)
 
     storm_ids = jnp.arange(storms, dtype=jnp.int32)
     pick = (slot_storm[:, None] == storm_ids[None, :]).astype(jnp.int32)
-    place_at = [select_rows(pick, centres[n]) for n in range(steps + 1)]
-    offs = jnp.stack([3 * (place_at[n + 1] - place_at[n]) for n in range(steps)])
+    place_at = jnp.sum(pick[None, :, :, None] * centres[:, None, :, :], axis=2)
+    offs = 3 * (place_at[1:] - place_at[:-1])
     offs = lax.dynamic_slice_in_dim(offs, nest_at * slots, slots, 1).reshape(-1)
 
     edges = jnp.array([0, 1, FP - 2, FP - 1], jnp.int32)
@@ -470,31 +552,29 @@
     along_at = starts[None, :, None] + lane - ALONG * jnp.arange(slots, dtype=jnp.int32)[:, None, None]
     own_lane = lane // ALONG == jnp.arange(slots, dtype=jnp.int32)[:, None, None]
     along_at = jnp.where(own_lane, along_at, -SPAN * SPAN)
-    sn_parts = []
-    we_parts = []
-    for n in range(steps):
-        now = stages[n]
-        corner = place_at[n + 1] - FP // 2
-        row_edge = (corner[:, 0, None, None] + edges[None, :, None] == xg).astype(jnp.float32)
-        col_edge = (corner[:, 1, None, None] + edges[None, :, None] == yg).astype(jnp.float32)
-        col_at = corner[:, 1].reshape(groups, slots, 1, 1, 1) + along_at[None, :, :, None, :]
-        col_pick = (col_at == yg[:, None]).astype(jnp.float32)
-        row_pick = (corner[:, 0, None, None, None] + rows_at[None, :, :, None] == xg).astype(jnp.float32)
-        sn = jnp.einsum("jrx,fxy->jrfy", row_edge, now, precision=EXACT)
-        sn = sn.reshape(groups, slots, 2, 2, planes, pcol)
-        sn_parts.append(jnp.einsum("gnhkfy,gnlyc->lhgkfc", sn, col_pick, precision=EXACT))
-        we = jnp.einsum("jky,fxy->jkfx", col_edge, now, precision=EXACT)
-        we = jnp.einsum("jtrx,jkfx->jtrkf", row_pick, we, precision=EXACT)
-        we_parts.append(we.reshape(groups, slots, tiles, deep, levs, 2, planes))
-    sn = jnp.stack(sn_parts, axis=3).reshape(levs, 2 * groups, steps * 2 * planes, lanes)
-    we = jnp.stack(we_parts, axis=0)
+    corner = place_at[1:] - FP // 2
+    corner_r, corner_c = corner[:, :, 0, None, None], corner[:, :, 1, None, None]
+    row_edge = (corner_r + edges[:, None] == xg).astype(jnp.float32)
+    col_edge = (corner_c + edges[:, None] == yg).astype(jnp.float32)
+    col_at = corner[:, :, 1].reshape(steps, groups, slots, 1, 1, 1) + along_at[:, :, None, :]
+    col_pick = (col_at == yg[:, None]).astype(jnp.float32)
+    row_pick = (corner_r[..., None] + rows_at[:, :, None] == xg).astype(jnp.float32)
+    sn = jnp.einsum("sjrx,sfxy->sjrfy", row_edge, stages, precision=EXACT)
+    sn = sn.reshape(steps, groups, slots, 2, 2, planes, pcol)
+    sn = jnp.einsum("sgnhkfy,sgnlyc->lhgskfc", sn, col_pick, precision=EXACT)
+    sn = sn.reshape(levs, 2 * groups, steps * 2 * planes, lanes)
+    we = jnp.einsum("sjky,sfxy->sjkfx", col_edge, stages, precision=EXACT)
+    we = jnp.einsum("sjtrx,sjkfx->sjtrkf", row_pick, we, precision=EXACT)
+    we = we.reshape(steps, groups, slots, tiles, deep, levs, 2, planes)
     we = jnp.transpose(we, (5, 3, 1, 4, 2, 6, 0, 7))
     we = we.reshape(levs, tiles * groups, deep, slots * 2 * steps * planes)
     we = jnp.pad(we, ((0, 0), (0, 0), (0, 0), (0, -we.shape[3] % LANES)))
     we, sn = sum_zones(we, sn, counts)
 
     jj = jnp.arange(wide, dtype=jnp.int32)
-    col_cell = jj + lev_at * jnp.where(jj >= cols, cols - wide, cols)
+    swapped = jnp.where(jj < cols - LANES, cols + LANES + jj, cols - LANES + jj)
+    swapped = jnp.where(jj < LANES, swapped, cols - LANES + jj)
+    col_cell = jnp.where(lev_at == 0, jj, swapped)
     row_cell = tile_at * rows - HALO + jnp.arange(high, dtype=jnp.int32)
     from_col = col_cell // 3 - lev_at * (FP - ALONG)
     spread_c = (own_lane[:, 0, :, None] & (from_col == (lane % ALONG)[:, None])).astype(jnp.float32)
@@ -502,15 +582,15 @@
     spread_r = (from_row[:, None] == jnp.arange(deep, dtype=jnp.int32)).astype(jnp.float32)
     along = jnp.einsum("ql,nlc->nqc", sn, spread_c, precision=EXACT)
     along = along.reshape(slots, 2 * steps, fields, levels, wide)
-    along = jnp.transpose(along, (0, 2, 3, 1, 4))
+    along = jnp.transpose(along, (0, 2, 3, 1, 4)).reshape(slots * planes, 2 * steps, wide)
     across = jnp.einsum("rq,qm->rm", spread_r, we, precision=EXACT)
     across = across[:, : slots * 2 * steps * planes].reshape(high, slots, 2, steps, fields, levels)
-    across = jnp.transpose(across, (1, 4, 5, 0, 3, 2)).reshape(slots, fields, levels, high, 2 * steps)
+    across = jnp.transpose(across, (1, 4, 5, 0, 3, 2)).reshape(slots * planes, high, 2 * steps)
     place = jnp.stack([tile_at, lev_at]).astype(jnp.int32)
     nests = advance_nests(
-        wide_nests, along, across, offs, place, lateral_rate, vertical_rate, rows, cols, steps
+        wide_nests, along, across, offs, place, lateral_rate, vertical_rate, nest_fields.shape, steps
     )
-    return (second.reshape(parent_field.shape), nests)
+    return (stages[1].reshape(parent_field.shape), nests)
 
 
 def solution(mesh):

time: 72.3 us -> 68.6 us (0.949)
  Pallas kernels: 51 us -> 48.9 us
  local copies, waits for them, and re-layouts: 10.7 us -> 9.6 us
    pallas_call x2, Pallas kernels: 36.7 us -> 34.6 us  [the longest x1 21.8 us: exchange_halos(): pl.pallas_call(functools.partial(halo_kernel, counts), out_shape=(shape(2...]
    another operation x3 -> x0, local copies, waits for them, and re-layouts: 1.02 us -> none  [the longest x2 0.76 us: per_device(): we = jnp.stack(we_parts, axis=0)]
    mul x3 -> x0, local copies, waits for them, and re-layouts: 0.9 us -> none  [the longest x1 0.72 us: select_rows(): return jnp.sum(picker[:, :, None] * table[None, :, :], axis=1)]
    reshape x1 -> x2, local copies, waits for them, and re-layouts: 0.02 us -> 0.78 us  [the longest x1 0.76 us: per_device(): we = we.reshape(steps, groups, slots, tiles, deep, levs, 2, planes)]
    slice x1 -> x2, local copies, waits for them, and re-layouts: 0.21 us -> 0.97 us  [the longest x1 0.75 us: per_device(): return (stages[1].reshape(parent_field.shape), nests)]
    unnamed x15 -> x16, local copies, waits for them, and re-layouts: 6.95 us -> 6.23 us
    dot_general x8 -> x4, matrix products: 5.42 us -> 4.91 us  [the longest x1 2.43 us: per_device(): we = jnp.einsum('sjtrx,sjkfx->sjtrkf', row_pick, we, precision=EXACT)]
where the time goes in v3:
time: 68.6 us; the launch traced here: 68.3 us
  Pallas kernels  48.9 us (71%)
  local copies, waits for them, and re-layouts  9.6 us (14%)
  matrix products  5.66 us (8%)
  other arithmetic  3.23 us (5%)
  between operations  0.9 us (1%)
    pallas_call x1, Pallas kernels, exchange_halos(): pl.pallas_call(functools.partial(halo_kernel, counts), out_shape=(shape(2...  21.8 us
    pallas_call x1, Pallas kernels, sum_zones(): pl.pallas_call(functools.partial(zone_kernel, counts), out_shape=(jax.Sha...  14.3 us
    pallas_call x1, Pallas kernels, advance_nests(): pl.pallas_call(functools.partial(nest_kernel, shape, steps), out_shape=ja...  12.9 us
    unnamed x16, local copies, waits for them, and re-layouts  6.23 us
    dot_general x1, matrix products, per_device(): we = jnp.einsum('sjtrx,sjkfx->sjtrkf', row_pick, we, precision=EXACT)  2.43 us

profile of v3, /device:TPU:0, one launch (start us, length us, event | category | flops | bytes accessed | tf_op | source)
XLA Modules:
  0.0 68.3 jit_solution(9376737161783727357)
XLA Ops:
  1.0 0.7 %fusion.31 = s32[6,6]{1,0:T(8,128)S(1)} fusion(s32[6]{0:T(128)} %param.13), kind=kLoop, calls=%fused_computation.44 | loop fusion | flops 72 | bytes 168 | tf_op jit(solution)/shard_map/convert_element_type | solution.py:540
  1.8 1.1 %multiply_reduce_fusion = s32[3,6,2]{2,1,0:T(8,128)S(1)} fusion(s32[3,6,2]{1,2,0:T(2,128)} %param.12, s32[6,6]{1,0:T(8,128)S(1)} %fusion.31), kind=kLoop, calls=%fused_computation.31 | loop fusion | flops 396 | bytes 432 | tf_op jit(solution)/shard_map/reduce_sum | solution.py:541
  2.9 0.2 slice_reduce_fusion
  3.3 0.7 %broadcast_add_fusion.3 = (s32[2,6,4]{1,2,0:T(4,128)S(1)}, s32[2,6,4]{1,2,0:T(4,128)S(1)}) fusion(s32[2,6]{1,0:T(2,128)S(1)} %get-tuple-element.11, s32[4]{0:T(128)} %constant.86.clone, s32[2,6]{1,0:T(2,128)S(1)} %get-tuple-element.10), kind=kLoop, calls=%fused_computation.49 | loop fusion | flops 96 | bytes 496 | tf_op jit(solution)/shard_map/add | solution.py:557
  4.3 0.1 broadcast_compare_fusion
  4.5 1.8 %copy-done.2 = f32[3,5,2,96,192]{4,3,2,1,0:T(8,128)S(1)} copy-done((f32[3,5,2,96,192]{4,3,2,1,0:T(8,128)S(1)}, f32[3,5,2,96,192]{4,3,2,1,0:T(8,128)}, u32[]{:S(2)}) %copy-start.2) | copy-done | bytes 2211864
  6.3 1.0 %copy-done.3 = f32[5,2,64,128]{3,2,1,0:T(8,128)S(1)} copy-done((f32[5,2,64,128]{3,2,1,0:T(8,128)S(1)}, f32[5,2,64,128]{3,2,1,0:T(8,128)}, u32[]{:S(2)}) %copy-start.3) | copy-done | bytes 327704
  7.3 0.7 copy-done.4
  7.9 0.7 copy-done.6
  8.6 21.8 %shard_map.95 = (f32[2,10,64,128]{3,2,1,0:T(8,128)S(1)}, f32[30,2,128,128]{3,2,1,0:T(8,128)S(1)}) custom-call(f32[10,64,128]{2,1,0:T(8,128)S(1)} %bitcast.60, f32[30,96,192]{2,1,0:T(8,128)S(1)} %bitcast.58, f32[5]{0:T(128)S(1)} %copy-done.4, f32[5]{0:T(128)S(1)} %copy-done.6), custom_call_target="tpu_custom_call" | custom-call | tf_op jit(solution)/shard_map/pallas_call | solution.py:206
  30.3 0.4 fusion.12
  30.7 0.9 %convolution_bitcast_fusion = f32[2,6,4,10,64,1]{4,2,3,1,0,5:T(4,128)S(1)} fusion(f32[2,10,64,128]{3,2,1,0:T(8,128)S(1)} %get-tuple-element.6, s32[128]{0:T(128)S(1)} %iota_add_fusion.4, s32[2,6,4]{2,1,0:T(8,128)S(1)} %copy.44), kind=kOutput, calls=%fused_computation.6 | convolution fusion | flops 47192064 | bytes 778944 | tf_op jit(solution)/shard_map/sjky,sfxy->sjkfx/dot_general | solution.py:566
  31.6 0.8 %slice.20 = f32[1,10,64,128]{3,2,1,0:T(8,128)} slice(f32[2,10,64,128]{3,2,1,0:T(8,128)S(1)} %get-tuple-element.6), slice={[1:2], [0:10], [0:64], [0:128]} | slice | bytes 655360 | tf_op jit(solution)/shard_map/slice | solution.py:593
  32.4 1.2 %fusion.5 = f32[2,2,2,2,2,10,256]{6,5,4,1,0,3,2:T(8,128)S(1)} fusion(s32[2,2,3,2,256]{4,2,3,0,1:T(4,128)S(1)} %broadcast_add_fusion, s32[128]{0:T(128)S(1)} %iota_add_fusion.4, f32[2,2,3,2,2,10,128,1]{6,4,3,5,2,1,0,7:T(2,128)S(1)} %bitcast.66), kind=kOutput, calls=%fused_computation.5 | convolution fusion | flops 378273792 | bytes 598528 | tf_op jit(solution)/shard_map/sgnhkfy,sgnlyc->lhgskfc/dot_general | solution.py:564
  33.6 0.3 copy.51
  33.9 2.4 %fusion.8 = f32[2,6,4,40,4,10]{3,5,4,2,1,0:T(8,128)S(1)} fusion(s32[64]{0:T(128)S(1)} %iota_add_fusion.5, s32[2,6,4,40]{3,2,1,0:T(4,128)S(1)} %broadcast_add_fusion.1, f32[2,6,4,10,64,1]{4,2,3,1,0,5:T(4,128)S(1)} %convolution_bitcast_fusion), kind=kOutput, calls=%fused_computation.8 | convolution fusion | flops 59105280 | bytes 438016 | tf_op jit(solution)/shard_map/sjtrx,sjkfx->sjtrkf/dot_general | solution.py:567
  36.3 0.8 %copy.46 = f32[2,2,3,4,40,2,2,10]{4,1,3,7,0,6,2,5:T(2,128)S(1)} copy(f32[2,2,3,4,40,2,2,10]{4,7,6,5,3,2,1,0:T(8,128)S(1)} %bitcast.61) | data formatting | bytes 614400 | tf_op jit(solution)/shard_map/reshape | solution.py:568
  37.1 0.3 copy.47
  37.5 14.3 %shard_map.96 = (f32[40,128]{1,0:T(8,128)S(1)}, f32[40,256]{1,0:T(8,128)S(1)}) custom-call(f32[2,8,40,128]{3,2,1,0:T(8,128)S(1)} %pad.4.we_ref, f32[2,4,40,256]{3,2,1,0:T(8,128)S(1)} %copy.52.sn_ref), custom_call_target="tpu_custom_call" | custom-call | tf_op jit(solution)/shard_map/pallas_call | solution.py:341
  51.8 0.5 convolution_bitcast_fusion.1
  52.4 0.3 fusion.21
  52.7 0.6 copy.55.we_ref
  53.4 2.1 %copy-done.1 = f32[30,2,128,128]{3,2,1,0:T(8,128)S(1)} copy-done((f32[30,2,128,128]{3,2,1,0:T(8,128)S(1)}, f32[30,2,128,128]{3,2,1,0:T(8,128)}, u32[]{:S(2)}) %copy-start.1) | copy-done | bytes 3932184
  55.5 12.9 %shard_map.97 = f32[3,5,2,96,192]{4,3,2,1,0:T(8,128)} custom-call(s32[12]{0:T(128)S(1)} %reshape.284.offs, s32[2]{0:T(128)S(1)} %pad_add_fusion.place, f32[5]{0:T(128)S(1)} %copy-done.5, f32[5]{0:T(128)S(1)} %copy-done.7, f32[30,2,128,128]{3,2,1,0:T(8,128)S(1)} %copy-done.1, f32[30,4,256]{2,1,0:T(4,128)S(1)} %bitcast.59, f32[30,128,4]{2,1,0:T(8,128)S(1)} %copy.55.we_ref), custom_call_target="tpu_custom_call" | custom-call | tf_op jit(solution)/shard_map/pallas_call | solution.py:494
  (38 shorter events, 1.1 us)
Async XLA Ops:
  4.4 1.8 %copy-start.2 = (f32[3,5,2,96,192]{4,3,2,1,0:T(8,128)S(1)}, f32[3,5,2,96,192]{4,3,2,1,0:T(8,128)}, u32[]{:S(2)}) copy-start(f32[3,5,2,96,192]{4,3,2,1,0:T(8,128)} %param.9) | copy-start | bytes 6635524
  6.3 1.0 %copy-start.3 = (f32[5,2,64,128]{3,2,1,0:T(8,128)S(1)}, f32[5,2,64,128]{3,2,1,0:T(8,128)}, u32[]{:S(2)}) copy-start(f32[5,2,64,128]{3,2,1,0:T(8,128)} %param.8) | copy-start | bytes 983044
  7.3 0.7 copy-start.4
  7.9 0.7 copy-start.6
  30.3 6.0 %copy-start = (f32[30,2,128,128]{3,2,1,0:T(8,128)}, f32[30,2,128,128]{3,2,1,0:T(8,128)S(1)}, u32[]{:S(2)}) copy-start(f32[30,2,128,128]{3,2,1,0:T(8,128)S(1)} %get-tuple-element.7.x_ref) | copy-start | bytes 11796484
  37.1 16.2 %copy-start.5 = (f32[5]{0:T(128)S(1)}, f32[5]{0:T(128)}, u32[]{:S(2)}) copy-start(f32[5]{0:T(128)} %lateral.1) | copy-start | bytes 64
  37.1 16.2 %copy-start.7 = (f32[5]{0:T(128)S(1)}, f32[5]{0:T(128)}, u32[]{:S(2)}) copy-start(f32[5]{0:T(128)} %vertical.1) | copy-start | bytes 64
  53.4 2.1 %copy-start.1 = (f32[30,2,128,128]{3,2,1,0:T(8,128)S(1)}, f32[30,2,128,128]{3,2,1,0:T(8,128)}, u32[]{:S(2)}) copy-start(f32[30,2,128,128]{3,2,1,0:T(8,128)} %copy-done) | copy-start | bytes 11796484

commit v4 on v3

--- a/solution.py
+++ b/solution.py
@@ -20,8 +20,8 @@
 MESH = pl.DeviceIdType.MESH
 
 
-def halo_kernel(counts, p_hbm, n_hbm, lat_ref, ver_ref, stage_ref, w_ref,
-                p_ref, n_ref, load, field, side, pack, held, cols_out, cols_in, send, recv):
+def halo_kernel(counts, p_hbm, n_hbm, lat_ref, ver_ref, stage_ref, w_hbm,
+                p_ref, n_ref, w_ref, load, field, side, pack, held, cols_out, cols_in, send, recv):
     tiles, groups, levs = counts
     tile_at = lax.axis_index("tile")
     nest_at = lax.axis_index("nest")
@@ -188,10 +188,24 @@
 
     lax.fori_loop(0, planes // 2, advance, 0)
 
+    def keep(at, start, size):
+        return pltpu.make_async_copy(
+            w_ref.at[:, :, pl.ds(start, size)], w_hbm.at[:, :, pl.ds(start, size)], load.at[at]
+        )
+
+    middle = keep(0, HALO, rows)
+    middle.start()
     pl.when(above)(nest_up.wait_send)
     pl.when(below)(nest_down.wait_send)
     pl.when(below)(nest_up.wait_recv)
     pl.when(above)(nest_down.wait_recv)
+    head = keep(1, 0, HALO)
+    tail = keep(2, HALO + rows, HALO)
+    head.start()
+    tail.start()
+    middle.wait()
+    head.wait()
+    tail.wait()
 
 
 def exchange_halos(parent, nests, lateral, vertical, counts):
@@ -210,11 +224,12 @@
             shape(blocks, 2, rows + 2 * HALO, LANES),
         ),
         in_specs=[anywhere, anywhere, smem, smem],
-        out_specs=(vmem, vmem),
+        out_specs=(vmem, anywhere),
         scratch_shapes=[
             pltpu.VMEM((planes, prow, pcol), jnp.float32),
             pltpu.VMEM((blocks, rows, cols), jnp.float32),
-            pltpu.SemaphoreType.DMA((2,)),
+            pltpu.VMEM((blocks, 2, rows + 2 * HALO, LANES), jnp.float32),
+            pltpu.SemaphoreType.DMA((3,)),
             pltpu.VMEM((planes, tall, LANES), jnp.float32),
             pltpu.VMEM((planes, tall, LANES), jnp.float32),
             pltpu.VMEM((blocks // 2, rows, LANES), jnp.float32),
@@ -225,7 +240,7 @@
             pltpu.SemaphoreType.DMA((7,)),
         ],
         compiler_params=pltpu.CompilerParams(
-            collective_id=1, has_side_effects=True, vmem_limit_bytes=24 * 1024 * 1024
+            collective_id=1, has_side_effects=True, vmem_limit_bytes=56 * 1024 * 1024
         ),
     )(parent, nests, lateral, vertical)
 
@@ -364,12 +379,20 @@
     )(we, sn)
 
 
-def nest_kernel(shape, steps, offs, place, lateral, vertical, x_ref, sn_ref, we_ref, o_hbm,
-                relaxed, state, done, col_mix, row_mix, sem):
+def nest_kernel(shape, steps, offs, place, lateral, vertical, x_hbm, sn_ref, we_ref, o_hbm,
+                x_ref, relaxed, state, done, col_mix, row_mix, load, sem):
     slots, fields, levels, rows, cols = shape
+    planes = fields * levels
     high = x_ref.shape[2]
     edge = 8
     mid = high - 2 * edge
+
+    def fetch(n):
+        part = pl.ds(n * planes, planes)
+        return pltpu.make_async_copy(x_hbm.at[part], x_ref.at[part], load.at[n])
+
+    for n in range(slots):
+        fetch(n).start()
     tile_at = place[0]
     lev_at = place[1]
     half = cols - LANES
@@ -388,7 +411,15 @@
         keep = (r + down >= 0) & (r + down < SPAN) & (c + right >= 0) & (c + right < SPAN)
         return jnp.where(keep, weight, 1.0)
 
-    for n in range(slots):
+    def patched(whole, blend):
+        parts = []
+        past = 0
+        for at, start in enumerate(blocks):
+            parts += [whole[past:start], blend(at, start, whole[start : start + edge])]
+            past = start + edge
+        return jnp.concatenate([a for a in parts + [whole[past:]] if a.shape[0]], axis=0)
+
+    def one_nest(n, carry):
         shifts = []
         for step in range(steps):
             down = offs[(step * slots + n) * 2]
@@ -413,75 +444,87 @@
                     row_mix[step, side, at, 1] = jnp.where(second, 0.0, weight)
                     row_mix[step, side, at, 2] = jnp.where(second, weight, 0.0)
 
-        def one_field(f, carry):
+        fetch(n).wait()
+
+        def relax(step, f, v):
+            down, right = shifts[step]
+            k = 2 * step
+            turn = lax.rem(LANES - right, LANES)
+            own = (lane + right >= 0) & (lane + right < LANES)
+            b = n * planes + f * levels + v
+            spot = pl.ds(edge + down, mid)
+            if step == 0:
+                turned = [pltpu.roll(x_ref[b, side, spot, :], turn, 1) for side in range(2)]
+            else:
+                turned = [
+                    pltpu.roll(state[f * levels + v, side, spot, :], turn, 1) for side in range(2)
+                ]
+            first = jnp.where(own, turned[0], turned[1])
+            first = (
+                col_mix[step, 0] * first
+                + col_mix[step, 1] * we_ref[b, edge : edge + mid, k : k + 1]
+                + col_mix[step, 2] * we_ref[b, edge : edge + mid, k + 1 : k + 2]
+            )
+            halves = (first, jnp.where(own, turned[1], turned[0]))
+            for side in range(2):
+                wide = slice(side * LANES, (side + 1) * LANES)
+
+                def blend(at, start, block):
+                    return (
+                        row_mix[step, side, at, 0] * block
+                        + row_mix[step, side, at, 1] * sn_ref[b, k : k + 1, wide]
+                        + row_mix[step, side, at, 2] * sn_ref[b, k + 1 : k + 2, wide]
+                    )
+
+                relaxed[f * levels + v, side, edge : edge + mid] = patched(halves[side], blend)
+
+        def diffuse(f, v):
             rate_l = lateral[f]
             rate_v = vertical[f]
             keep_rate = 1.0 - 4.0 * rate_l - 2.0 * rate_v
-            for step in range(steps):
-                down, right = shifts[step]
-                k = 2 * step
-                turn = lax.rem(LANES - right, LANES)
-                own = (lane + right >= 0) & (lane + right < LANES)
+            p = f * levels + v
+            here = [relaxed[p, side, edge : edge + mid] for side in range(2)]
+            west = [pltpu.roll(a, 1, 1) for a in here]
+            east = [pltpu.roll(a, LANES - 1, 1) for a in here]
+            for side in range(2):
+                around = (
+                    relaxed[p, side, edge - 1 : edge - 1 + mid]
+                    + relaxed[p, side, edge + 1 : edge + 1 + mid]
+                    + jnp.where(lane == 0, west[1 - side], west[side])
+                    + jnp.where(lane == LANES - 1, east[1 - side], east[side])
+                )
+                new = (
+                    keep_rate * here[side]
+                    + rate_l * around
+                    + rate_v * relaxed[f * levels + 1 - v, side, edge : edge + mid]
+                )
+                if side == 0:
+                    new = jnp.where(lane == col_lane, here[0], new)
+
+                def blend(at, start, block):
+                    r = row[start : start + edge]
+                    before = here[side][start : start + edge]
+                    return jnp.where((r == 0) | (r == SPAN - 1), before, block)
+
+                state[p, side, edge : edge + mid] = patched(new, blend)
+
+        for step in range(steps):
+            for f in range(fields):
                 for v in range(levels):
-                    b = (n * fields + f) * levels + v
-                    if step == 0:
-                        source = [x_ref[b, side, pl.ds(edge + down, mid), :] for side in range(2)]
-                    else:
-                        source = [state[v, side, pl.ds(edge + down, mid), :] for side in range(2)]
-                    turned = [pltpu.roll(a, turn, 1) for a in source]
-                    first = jnp.where(own, turned[0], turned[1])
-                    first = (
-                        col_mix[step, 0] * first
-                        + col_mix[step, 1] * we_ref[b, edge : edge + mid, k : k + 1]
-                        + col_mix[step, 2] * we_ref[b, edge : edge + mid, k + 1 : k + 2]
-                    )
-                    relaxed[v, 0, edge : edge + mid] = first
-                    relaxed[v, 1, edge : edge + mid] = jnp.where(own, turned[1], turned[0])
-                    for side in range(2):
-                        wide = slice(side * LANES, (side + 1) * LANES)
-                        for at, start in enumerate(blocks):
-                            here = slice(edge + start, 2 * edge + start)
-                            relaxed[v, side, here] = (
-                                row_mix[step, side, at, 0] * relaxed[v, side, here]
-                                + row_mix[step, side, at, 1] * sn_ref[b, k : k + 1, wide]
-                                + row_mix[step, side, at, 2] * sn_ref[b, k + 1 : k + 2, wide]
-                            )
+                    relax(step, f, v)
+            for f in range(fields):
                 for v in range(levels):
-                    here = [relaxed[v, side, edge : edge + mid] for side in range(2)]
-                    west = [pltpu.roll(a, 1, 1) for a in here]
-                    east = [pltpu.roll(a, LANES - 1, 1) for a in here]
-                    results = []
-                    for side in range(2):
-                        around = (
-                            relaxed[v, side, edge - 1 : edge - 1 + mid]
-                            + relaxed[v, side, edge + 1 : edge + 1 + mid]
-                            + jnp.where(lane == 0, west[1 - side], west[side])
-                            + jnp.where(lane == LANES - 1, east[1 - side], east[side])
-                        )
-                        new = (
-                            keep_rate * here[side]
-                            + rate_l * around
-                            + rate_v * relaxed[1 - v, side, edge : edge + mid]
-                        )
-                        if side == 0:
-                            new = jnp.where(lane == col_lane, here[side], new)
-                        state[v, side, edge : edge + mid] = new
-                    for side in range(2):
-                        for at, start in enumerate(blocks):
-                            r = row[start : start + edge]
-                            spot = slice(edge + start, 2 * edge + start)
-                            state[v, side, spot] = jnp.where(
-                                (r == 0) | (r == SPAN - 1), relaxed[v, side, spot], state[v, side, spot]
-                            )
+                    diffuse(f, v)
+        for f in range(fields):
             for v in range(levels):
-                near_part = state[v, 0, HALO : HALO + rows]
-                far_part = state[v, 1, HALO : HALO + rows]
+                near_part = state[f * levels + v, 0, HALO : HALO + rows]
+                far_part = state[f * levels + v, 1, HALO : HALO + rows]
                 done[n, f, v, :, :LANES] = jnp.where(lev_at == 0, near_part, far_part)
                 done[n, f, v, :, LANES:] = jnp.where(lev_at == 0, far_part, near_part)[:, :half]
-            return carry
-
-        lax.fori_loop(0, fields, one_field, 0)
         pltpu.make_async_copy(done.at[n], o_hbm.at[n], sem.at[n]).start()
+        return carry
+
+    lax.fori_loop(0, slots, one_nest, 0)
     for n in range(slots):
         pltpu.make_async_copy(done.at[n], o_hbm.at[n], sem.at[n]).wait()
 
@@ -494,17 +537,19 @@
     return pl.pallas_call(
         functools.partial(nest_kernel, shape, steps),
         out_shape=jax.ShapeDtypeStruct(shape, jnp.float32),
-        in_specs=[smem] * 4 + [vmem] * 3,
+        in_specs=[smem] * 4 + [pl.BlockSpec(memory_space=pl.ANY)] + [vmem] * 2,
         out_specs=pl.BlockSpec(memory_space=pl.ANY),
         scratch_shapes=[
-            pltpu.VMEM((levels, 2, high, LANES), jnp.float32),
-            pltpu.VMEM((levels, 2, high, LANES), jnp.float32),
+            pltpu.VMEM(wide_nests.shape, jnp.float32),
+            pltpu.VMEM((fields * levels, 2, high, LANES), jnp.float32),
+            pltpu.VMEM((fields * levels, 2, high, LANES), jnp.float32),
             pltpu.VMEM(shape, jnp.float32),
             pltpu.VMEM((steps, 3, high - 16, LANES), jnp.float32),
             pltpu.VMEM((steps, 2, 2, 3, 8, LANES), jnp.float32),
             pltpu.SemaphoreType.DMA((slots,)),
+            pltpu.SemaphoreType.DMA((slots,)),
         ],
-        compiler_params=pltpu.CompilerParams(vmem_limit_bytes=24 * 1024 * 1024),
+        compiler_params=pltpu.CompilerParams(vmem_limit_bytes=56 * 1024 * 1024),
     )(offs, place, lateral, vertical, wide_nests, along, across)
 
 

time: 68.6 us -> 70.5 us (1.028)
  local copies, waits for them, and re-layouts: 9.6 us -> 6.83 us
  matrix products: 5.66 us -> 7.88 us
  Pallas kernels: 48.9 us -> 50.9 us
    unnamed x16 -> x0, local copies, waits for them, and re-layouts: 6.23 us -> none
    pallas_call x1, Pallas kernels: 21.8 us -> 23.7 us  [exchange_halos(): pl.pallas_call(functools.partial(halo_kernel, counts), out_shape=(shape(2...]
    reshape x1, local copies, waits for them, and re-layouts: 0.6 us -> 1.9 us  [per_device(): jnp.transpose(across, (1, 4, 5, 0, 3, 2))]
    dot_general x1, matrix products: 0.91 us -> 2 us  [per_device(): we = jnp.einsum('sjky,sfxy->sjkfx', col_edge, stages, precision=EXACT)]
    dot_general x1, matrix products: 0.36 us -> 1.44 us  [per_device(): sn = jnp.einsum('sjrx,sfxy->sjrfy', row_edge, stages, precision=EXACT)]
    slice x1, local copies, waits for them, and re-layouts: 0.75 us -> 1.73 us  [per_device(): return (stages[1].reshape(parent_field.shape), nests)]
where the time goes in v4:
time: 70.5 us; the launch traced here: 70.2 us
  Pallas kernels  50.9 us (72%)
  matrix products  7.88 us (11%)
  local copies, waits for them, and re-layouts  6.83 us (10%)
  other arithmetic  3.75 us (5%)
  between operations  0.82 us (1%)
    pallas_call x1, Pallas kernels, exchange_halos(): pl.pallas_call(functools.partial(halo_kernel, counts), out_shape=(shape(2...  23.7 us
    pallas_call x1, Pallas kernels, sum_zones(): pl.pallas_call(functools.partial(zone_kernel, counts), out_shape=(jax.Sha...  14.4 us
    pallas_call x1, Pallas kernels, advance_nests(): pl.pallas_call(functools.partial(nest_kernel, shape, steps), out_shape=ja...  12.8 us
    dot_general x1, matrix products, per_device(): we = jnp.einsum('sjtrx,sjkfx->sjtrkf', row_pick, we, precision=EXACT)  2.44 us
    dot_general x1, matrix products, per_device(): we = jnp.einsum('sjky,sfxy->sjkfx', col_edge, stages, precision=EXACT)  2 us
    reshape x1, local copies, waits for them, and re-layouts, per_device(): jnp.transpose(across, (1, 4, 5, 0, 3, 2))  1.9 us
    slice x1, local copies, waits for them, and re-layouts, per_device(): return (stages[1].reshape(parent_field.shape), nests)  1.73 us
    dot_general x1, matrix products, per_device(): sn = jnp.einsum('sjrx,sfxy->sjrfy', row_edge, stages, precision=EXACT)  1.44 us

profile of v4, /device:TPU:0, one launch (start us, length us, event | category | flops | bytes accessed | tf_op | source)
XLA Modules:
  0.0 70.2 jit_solution(1930575183453620224)
XLA Ops:
  0.7 0.6 pad_add_fusion.place
  1.5 0.7 %fusion.31 = s32[6,6]{1,0:T(8,128)S(1)} fusion(s32[6]{0:T(128)} %param.13), kind=kLoop, calls=%fused_computation.44 | loop fusion | flops 72 | bytes 168 | tf_op jit(solution)/shard_map/convert_element_type | solution.py:585
  2.3 1.1 %multiply_reduce_fusion = s32[3,6,2]{2,1,0:T(8,128)S(1)} fusion(s32[3,6,2]{1,2,0:T(2,128)} %param.12, s32[6,6]{1,0:T(8,128)S(1)} %fusion.31), kind=kLoop, calls=%fused_computation.31 | loop fusion | flops 396 | bytes 432 | tf_op jit(solution)/shard_map/reduce_sum | solution.py:586
  3.4 0.2 slice_reduce_fusion
  3.6 0.1 add.229
  3.7 0.6 reshape.284.offs
  4.3 0.7 %broadcast_add_fusion.3 = (s32[2,6,4]{1,2,0:T(4,128)S(1)}, s32[2,6,4]{1,2,0:T(4,128)S(1)}) fusion(s32[2,6]{1,0:T(2,128)S(1)} %get-tuple-element.11, s32[4]{0:T(128)} %constant.86.clone, s32[2,6]{1,0:T(2,128)S(1)} %get-tuple-element.10), kind=kLoop, calls=%fused_computation.49 | loop fusion | flops 96 | bytes 496 | tf_op jit(solution)/shard_map/add | solution.py:602
  5.1 0.1 copy.44
  5.4 0.1 broadcast_compare_fusion
  5.5 23.7 %shard_map.95 = (f32[2,10,64,128]{3,2,1,0:T(8,128)}, f32[30,2,128,128]{3,2,1,0:T(8,128)}) custom-call(f32[10,64,128]{2,1,0:T(8,128)} %bitcast.63, f32[30,96,192]{2,1,0:T(8,128)} %bitcast.60, f32[5]{0:T(128)} %lateral.1, f32[5]{0:T(128)} %vertical.1), custom_call_target="tpu_custom_call" | custom-call | tf_op jit(solution)/shard_map/pallas_call | solution.py:220
  29.2 1.4 %fusion.12 = f32[2,6,4,10,128]{4,2,3,1,0:T(4,128)S(1)} fusion(f32[2,10,64,128]{3,2,1,0:T(8,128)} %get-tuple-element.6, pred[2,6,4,64,1]{3,1,2,0,4:T(8,128)(4,1)S(1)} %compare_bitcast_fusion), kind=kOutput, calls=%fused_computation.12 | convolution fusion | flops 47185920 | bytes 904192 | tf_op jit(solution)/shard_map/sjrx,sfxy->sjrfy/dot_general | solution.py:607
  30.6 2.0 %convolution_bitcast_fusion = f32[2,6,4,10,64,1]{4,2,3,1,0,5:T(4,128)S(1)} fusion(f32[2,10,64,128]{3,2,1,0:T(8,128)} %get-tuple-element.6, s32[128]{0:T(128)S(1)} %iota_add_fusion.4, s32[2,6,4]{2,1,0:T(8,128)S(1)} %copy.44), kind=kOutput, calls=%fused_computation.6 | convolution fusion | flops 47192064 | bytes 778944 | tf_op jit(solution)/shard_map/sjky,sfxy->sjkfx/dot_general | solution.py:611
  32.6 1.7 %slice.20 = f32[1,10,64,128]{3,2,1,0:T(8,128)} slice(f32[2,10,64,128]{3,2,1,0:T(8,128)} %get-tuple-element.6), slice={[1:2], [0:10], [0:64], [0:128]} | slice | bytes 655360 | tf_op jit(solution)/shard_map/slice | solution.py:638
  34.4 1.3 %fusion.5 = f32[2,2,2,2,2,10,256]{6,5,4,1,0,3,2:T(8,128)S(1)} fusion(s32[2,2,3,2,256]{4,2,3,0,1:T(4,128)S(1)} %broadcast_add_fusion, s32[128]{0:T(128)S(1)} %iota_add_fusion.4, f32[2,2,3,2,2,10,128,1]{6,4,3,5,2,1,0,7:T(2,128)S(1)} %bitcast.66), kind=kOutput, calls=%fused_computation.5 | convolution fusion | flops 378273792 | bytes 598528 | tf_op jit(solution)/shard_map/sgnhkfy,sgnlyc->lhgskfc/dot_general | solution.py:609
  35.6 0.3 copy.51
  35.9 2.4 %fusion.8 = f32[2,6,4,40,4,10]{3,5,4,2,1,0:T(8,128)S(1)} fusion(s32[64]{0:T(128)S(1)} %iota_add_fusion.5, s32[2,6,4,40]{3,2,1,0:T(4,128)S(1)} %broadcast_add_fusion.1, f32[2,6,4,10,64,1]{4,2,3,1,0,5:T(4,128)S(1)} %convolution_bitcast_fusion), kind=kOutput, calls=%fused_computation.8 | convolution fusion | flops 59105280 | bytes 438016 | tf_op jit(solution)/shard_map/sjtrx,sjkfx->sjtrkf/dot_general | solution.py:612
  38.4 0.8 %copy.46 = f32[2,2,3,4,40,2,2,10]{4,1,3,7,0,6,2,5:T(2,128)S(1)} copy(f32[2,2,3,4,40,2,2,10]{4,7,6,5,3,2,1,0:T(8,128)S(1)} %bitcast.58) | data formatting | bytes 614400 | tf_op jit(solution)/shard_map/reshape | solution.py:613
  39.1 0.3 copy.47
  39.5 14.4 %shard_map.96 = (f32[40,128]{1,0:T(8,128)S(1)}, f32[40,256]{1,0:T(8,128)S(1)}) custom-call(f32[2,8,40,128]{3,2,1,0:T(8,128)S(1)} %pad.4.we_ref, f32[2,4,40,256]{3,2,1,0:T(8,128)S(1)} %copy.52.sn_ref), custom_call_target="tpu_custom_call" | custom-call | tf_op jit(solution)/shard_map/pallas_call | solution.py:356
  54.0 0.5 convolution_bitcast_fusion.1
  54.5 0.7 copy.53
  55.2 0.3 fusion.21
  55.5 1.9 %copy.55.we_ref = f32[30,128,4]{2,1,0:T(8,128)} copy(f32[30,128,4]{1,2,0:T(4,128)S(1)} %bitcast.67) | data formatting | bytes 122880 | tf_op jit(solution)/shard_map/reshape | solution.py:633
  57.4 12.8 %shard_map.97 = f32[3,5,2,96,192]{4,3,2,1,0:T(8,128)} custom-call(s32[12]{0:T(128)} %reshape.284.offs, s32[2]{0:T(128)} %pad_add_fusion.place, f32[5]{0:T(128)} %lateral.1, f32[5]{0:T(128)} %vertical.1, f32[30,2,128,128]{3,2,1,0:T(8,128)} %get-tuple-element.7.x_hbm, f32[30,4,256]{2,1,0:T(4,128)} %bitcast.62, f32[30,128,4]{2,1,0:T(8,128)} %copy.55.we_ref), custom_call_target="tpu_custom_call" | custom-call | tf_op jit(solution)/shard_map/pallas_call | solution.py:537
  (22 shorter events, 0.7 us)

commit v5 on v4

--- a/solution.py
+++ b/solution.py
@@ -74,6 +74,18 @@
     pl.when(below)(rows_down.start)
 
     load_nests.wait()
+    own_up = remote(
+        n_ref.at[:, pl.ds(0, HALO), pl.ds(0, LANES)],
+        w_ref.at[:, lev_at, pl.ds(HALO + rows, HALO)],
+        7, 7, upper,
+    )
+    own_down = remote(
+        n_ref.at[:, pl.ds(rows - HALO, HALO), pl.ds(0, LANES)],
+        w_ref.at[:, lev_at, pl.ds(0, HALO)],
+        8, 8, lower,
+    )
+    pl.when(above)(own_up.start)
+    pl.when(below)(own_down.start)
 
     def gather(i, carry):
         def nearer(b):
@@ -134,10 +146,15 @@
         return carry
 
     lax.fori_loop(0, blocks // 2, widen, 0)
+    mixed_at = 1 - lev_at
     nest_up = remote(
-        w_ref.at[:, :, pl.ds(HALO, HALO)], w_ref.at[:, :, pl.ds(HALO + rows, HALO)], 5, 5, upper
-    )
-    nest_down = remote(w_ref.at[:, :, pl.ds(rows, HALO)], w_ref.at[:, :, pl.ds(0, HALO)], 6, 6, lower)
+        w_ref.at[:, mixed_at, pl.ds(HALO, HALO)],
+        w_ref.at[:, mixed_at, pl.ds(HALO + rows, HALO)],
+        5, 5, upper,
+    )
+    nest_down = remote(
+        w_ref.at[:, mixed_at, pl.ds(rows, HALO)], w_ref.at[:, mixed_at, pl.ds(0, HALO)], 6, 6, lower
+    )
     pl.when(above)(nest_up.start)
     pl.when(below)(nest_down.start)
 
@@ -195,10 +212,11 @@
 
     middle = keep(0, HALO, rows)
     middle.start()
-    pl.when(above)(nest_up.wait_send)
-    pl.when(below)(nest_down.wait_send)
-    pl.when(below)(nest_up.wait_recv)
-    pl.when(above)(nest_down.wait_recv)
+    for up, down in ((own_up, own_down), (nest_up, nest_down)):
+        pl.when(above)(up.wait_send)
+        pl.when(below)(down.wait_send)
+        pl.when(below)(up.wait_recv)
+        pl.when(above)(down.wait_recv)
     head = keep(1, 0, HALO)
     tail = keep(2, HALO + rows, HALO)
     head.start()
@@ -236,11 +254,11 @@
             pltpu.VMEM((blocks // 2, rows, LANES), jnp.float32),
             pltpu.VMEM((2, tall, LANES), jnp.float32),
             pltpu.VMEM((2, tall, LANES), jnp.float32),
-            pltpu.SemaphoreType.DMA((7,)),
-            pltpu.SemaphoreType.DMA((7,)),
+            pltpu.SemaphoreType.DMA((9,)),
+            pltpu.SemaphoreType.DMA((9,)),
         ],
         compiler_params=pltpu.CompilerParams(
-            collective_id=1, has_side_effects=True, vmem_limit_bytes=56 * 1024 * 1024
+            collective_id=1, has_side_effects=True, vmem_limit_bytes=52 * 1024 * 1024
         ),
     )(parent, nests, lateral, vertical)
 
@@ -379,7 +397,7 @@
     )(we, sn)
 
 
-def nest_kernel(shape, steps, offs, place, lateral, vertical, x_hbm, sn_ref, we_ref, o_hbm,
+def nest_kernel(shape, steps, centres, storms, lateral, vertical, x_hbm, sn_ref, we_ref, o_hbm,
                 x_ref, relaxed, state, done, col_mix, row_mix, load, sem):
     slots, fields, levels, rows, cols = shape
     planes = fields * levels
@@ -393,8 +411,9 @@
 
     for n in range(slots):
         fetch(n).start()
-    tile_at = place[0]
-    lev_at = place[1]
+    tile_at = lax.axis_index("tile")
+    nest_at = lax.axis_index("nest")
+    lev_at = lax.axis_index("lev")
     half = cols - LANES
     lane = lax.broadcasted_iota(jnp.int32, (mid, LANES), 1)
     row = lax.broadcasted_iota(jnp.int32, (mid, LANES), 0) + (tile_at * rows - HALO + edge)
@@ -421,9 +440,10 @@
 
     def one_nest(n, carry):
         shifts = []
+        storm = storms[nest_at * slots + n]
         for step in range(steps):
-            down = offs[(step * slots + n) * 2]
-            right = offs[(step * slots + n) * 2 + 1]
+            down = 3 * (centres[step + 1, storm, 0] - centres[step, storm, 0])
+            right = 3 * (centres[step + 1, storm, 1] - centres[step, storm, 1])
             shifts.append((down, right))
             weight = mixing(row, near, down, right)
             side_row = (row < BORDER) | (row >= SPAN - BORDER)
@@ -529,7 +549,7 @@
         pltpu.make_async_copy(done.at[n], o_hbm.at[n], sem.at[n]).wait()
 
 
-def advance_nests(wide_nests, along, across, offs, place, lateral, vertical, shape, steps):
+def advance_nests(wide_nests, along, across, centres, storms, lateral, vertical, shape, steps):
     slots, fields, levels, rows, cols = shape
     high = wide_nests.shape[2]
     vmem = pl.BlockSpec(memory_space=pltpu.VMEM)
@@ -549,8 +569,8 @@
             pltpu.SemaphoreType.DMA((slots,)),
             pltpu.SemaphoreType.DMA((slots,)),
         ],
-        compiler_params=pltpu.CompilerParams(vmem_limit_bytes=56 * 1024 * 1024),
-    )(offs, place, lateral, vertical, wide_nests, along, across)
+        compiler_params=pltpu.CompilerParams(vmem_limit_bytes=52 * 1024 * 1024),
+    )(centres, storms, lateral, vertical, wide_nests, along, across)
 
 
 def per_device(parent_field, nest_fields, lateral_rate, vertical_rate, centres, slot_storm):
@@ -584,8 +604,6 @@
     storm_ids = jnp.arange(storms, dtype=jnp.int32)
     pick = (slot_storm[:, None] == storm_ids[None, :]).astype(jnp.int32)
     place_at = jnp.sum(pick[None, :, :, None] * centres[:, None, :, :], axis=2)
-    offs = 3 * (place_at[1:] - place_at[:-1])
-    offs = lax.dynamic_slice_in_dim(offs, nest_at * slots, slots, 1).reshape(-1)
 
     edges = jnp.array([0, 1, FP - 2, FP - 1], jnp.int32)
     deep = coarse + 8
@@ -631,9 +649,16 @@
     across = jnp.einsum("rq,qm->rm", spread_r, we, precision=EXACT)
     across = across[:, : slots * 2 * steps * planes].reshape(high, slots, 2, steps, fields, levels)
     across = jnp.transpose(across, (1, 4, 5, 0, 3, 2)).reshape(slots * planes, high, 2 * steps)
-    place = jnp.stack([tile_at, lev_at]).astype(jnp.int32)
     nests = advance_nests(
-        wide_nests, along, across, offs, place, lateral_rate, vertical_rate, nest_fields.shape, steps
+        wide_nests,
+        along,
+        across,
+        centres,
+        slot_storm,
+        lateral_rate,
+        vertical_rate,
+        nest_fields.shape,
+        steps,
     )
     return (stages[1].reshape(parent_field.shape), nests)
 

time: 70.5 us -> 63.4 us (0.90)
  Pallas kernels: 50.9 us -> 45.7 us
  matrix products: 7.88 us -> 5.72 us
  local copies, waits for them, and re-layouts: 6.83 us -> 7.67 us
    pallas_call x1, Pallas kernels: 23.7 us -> 18.8 us  [exchange_halos(): pl.pallas_call(functools.partial(halo_kernel, counts), out_shape=(shape(2...]
    unnamed x0 -> x13, local copies, waits for them, and re-layouts: none -> 3.08 us
    dot_general x1, matrix products: 2 us -> 0.91 us  [per_device(): we = jnp.einsum('sjky,sfxy->sjkfx', col_edge, stages, precision=EXACT)]
    dot_general x1, matrix products: 1.44 us -> 0.36 us  [per_device(): sn = jnp.einsum('sjrx,sfxy->sjrfy', row_edge, stages, precision=EXACT)]
    slice x1, local copies, waits for them, and re-layouts: 1.73 us -> 0.75 us  [per_device(): return (stages[1].reshape(parent_field.shape), nests)]
where the time goes in v5:
time: 63.4 us; the launch traced here: 63.1 us
  Pallas kernels  45.7 us (72%)
  local copies, waits for them, and re-layouts  7.67 us (12%)
  matrix products  5.72 us (9%)
  other arithmetic  3.15 us (5%)
  between operations  0.87 us (1%)
    pallas_call x1, Pallas kernels, exchange_halos(): pl.pallas_call(functools.partial(halo_kernel, counts), out_shape=(shape(2...  18.8 us
    pallas_call x1, Pallas kernels, sum_zones(): pl.pallas_call(functools.partial(zone_kernel, counts), out_shape=(jax.Sha...  14.3 us
    pallas_call x1, Pallas kernels, advance_nests(): pl.pallas_call(functools.partial(nest_kernel, shape, steps), out_shape=ja...  12.6 us
    unnamed x13, local copies, waits for them, and re-layouts  3.08 us
    dot_general x1, matrix products, per_device(): we = jnp.einsum('sjtrx,sjkfx->sjtrkf', row_pick, we, precision=EXACT)  2.44 us
    reshape x1, local copies, waits for them, and re-layouts, per_device(): jnp.transpose(across, (1, 4, 5, 0, 3, 2))  1.91 us

profile of v5, /device:TPU:0, one launch (start us, length us, event | category | flops | bytes accessed | tf_op | source)
XLA Modules:
  0.0 63.1 jit_solution(4622943398653043318)
XLA Ops:
  0.9 0.7 %fusion.30 = s32[6,6]{1,0:T(8,128)S(1)} fusion(s32[6]{0:T(128)} %storms.1), kind=kLoop, calls=%fused_computation.42 | loop fusion | flops 72 | bytes 168 | tf_op jit(solution)/shard_map/convert_element_type | solution.py:605
  1.7 1.1 %multiply_reduce_fusion = s32[3,6,2]{2,1,0:T(8,128)S(1)} fusion(s32[3,6,2]{1,2,0:T(2,128)} %param.12, s32[6,6]{1,0:T(8,128)S(1)} %fusion.30), kind=kLoop, calls=%fused_computation.31 | loop fusion | flops 396 | bytes 432 | tf_op jit(solution)/shard_map/reduce_sum | solution.py:606
  2.8 0.2 slice_reduce_fusion
  3.1 0.7 %broadcast_add_fusion.2 = (s32[2,6,4]{1,2,0:T(4,128)S(1)}, s32[2,6,4]{1,2,0:T(4,128)S(1)}) fusion(s32[2,6]{1,0:T(2,128)S(1)} %get-tuple-element.11, s32[4]{0:T(128)} %constant.83.clone, s32[2,6]{1,0:T(2,128)S(1)} %get-tuple-element.10), kind=kLoop, calls=%fused_computation.47 | loop fusion | flops 96 | bytes 496 | tf_op jit(solution)/shard_map/add | solution.py:620
  3.9 0.1 copy.45
  4.0 0.8 %copy.56.centres = s32[3,6,2]{2,1,0:T(8,128)S(1)} copy(s32[3,6,2]{1,2,0:T(2,128)} %param.12) | data formatting | bytes 288 | tf_op args[4]
  4.9 0.1 broadcast_compare_fusion
  5.1 1.0 %copy-done = f32[5,2,64,128]{3,2,1,0:T(8,128)S(1)} copy-done((f32[5,2,64,128]{3,2,1,0:T(8,128)S(1)}, f32[5,2,64,128]{3,2,1,0:T(8,128)}, u32[]{:S(2)}) %copy-start) | copy-done | bytes 327704
  6.0 0.7 %copy-done.1 = f32[5]{0:T(128)S(1)} copy-done((f32[5]{0:T(128)S(1)}, f32[5]{0:T(128)}, u32[]{:S(2)}) %copy-start.1) | copy-done | bytes 44
  6.7 0.7 %copy-done.3 = f32[5]{0:T(128)S(1)} copy-done((f32[5]{0:T(128)S(1)}, f32[5]{0:T(128)}, u32[]{:S(2)}) %copy-start.3) | copy-done | bytes 44
  7.4 18.8 %shard_map.95 = (f32[2,10,64,128]{3,2,1,0:T(8,128)S(1)}, f32[30,2,128,128]{3,2,1,0:T(8,128)}) custom-call(f32[10,64,128]{2,1,0:T(8,128)S(1)} %bitcast.57, f32[30,96,192]{2,1,0:T(8,128)} %bitcast.60, f32[5]{0:T(128)S(1)} %copy-done.1, f32[5]{0:T(128)S(1)} %copy-done.3), custom_call_target="tpu_custom_call" | custom-call | tf_op jit(solution)/shard_map/pallas_call | solution.py:238
  26.1 0.4 fusion.12
  26.5 0.9 %convolution_bitcast_fusion = f32[2,6,4,10,64,1]{4,2,3,1,0,5:T(4,128)S(1)} fusion(f32[2,10,64,128]{3,2,1,0:T(8,128)S(1)} %get-tuple-element.6, s32[128]{0:T(128)S(1)} %iota_add_fusion.4, s32[2,6,4]{2,1,0:T(8,128)S(1)} %copy.45), kind=kOutput, calls=%fused_computation.6 | convolution fusion | flops 47192064 | bytes 778944 | tf_op jit(solution)/shard_map/sjky,sfxy->sjkfx/dot_general | solution.py:629
  27.4 0.8 %slice.16 = f32[1,10,64,128]{3,2,1,0:T(8,128)} slice(f32[2,10,64,128]{3,2,1,0:T(8,128)S(1)} %get-tuple-element.6), slice={[1:2], [0:10], [0:64], [0:128]} | slice | bytes 655360 | tf_op jit(solution)/shard_map/slice | solution.py:663
  28.2 1.3 %fusion.5 = f32[2,2,2,2,2,10,256]{6,5,4,1,0,3,2:T(8,128)S(1)} fusion(s32[2,2,3,2,256]{4,2,3,0,1:T(4,128)S(1)} %broadcast_add_fusion, s32[128]{0:T(128)S(1)} %iota_add_fusion.4, f32[2,2,3,2,2,10,128,1]{6,4,3,5,2,1,0,7:T(2,128)S(1)} %bitcast.64), kind=kOutput, calls=%fused_computation.5 | convolution fusion | flops 378273792 | bytes 598528 | tf_op jit(solution)/shard_map/sgnhkfy,sgnlyc->lhgskfc/dot_general | solution.py:627
  29.4 0.3 copy.52
  29.7 2.4 %fusion.8 = f32[2,6,4,40,4,10]{3,5,4,2,1,0:T(8,128)S(1)} fusion(s32[64]{0:T(128)S(1)} %iota_add_fusion.5, s32[2,6,4,40]{3,2,1,0:T(4,128)S(1)} %broadcast_add_fusion.1, f32[2,6,4,10,64,1]{4,2,3,1,0,5:T(4,128)S(1)} %convolution_bitcast_fusion), kind=kOutput, calls=%fused_computation.8 | convolution fusion | flops 59105280 | bytes 438016 | tf_op jit(solution)/shard_map/sjtrx,sjkfx->sjtrkf/dot_general | solution.py:630
  32.2 0.8 %copy.47 = f32[2,2,3,4,40,2,2,10]{4,1,3,7,0,6,2,5:T(2,128)S(1)} copy(f32[2,2,3,4,40,2,2,10]{4,7,6,5,3,2,1,0:T(8,128)S(1)} %bitcast.58) | data formatting | bytes 614400 | tf_op jit(solution)/shard_map/reshape | solution.py:631
  33.0 0.3 copy.48
  33.3 14.3 %shard_map.96 = (f32[40,128]{1,0:T(8,128)S(1)}, f32[40,256]{1,0:T(8,128)S(1)}) custom-call(f32[2,8,40,128]{3,2,1,0:T(8,128)S(1)} %pad.4.we_ref, f32[2,4,40,256]{3,2,1,0:T(8,128)S(1)} %copy.53.sn_ref), custom_call_target="tpu_custom_call" | custom-call | tf_op jit(solution)/shard_map/pallas_call | solution.py:374
  47.7 0.5 convolution_bitcast_fusion.1
  48.2 0.3 fusion.21
  48.6 1.9 %copy.57.we_ref = f32[30,128,4]{2,1,0:T(8,128)} copy(f32[30,128,4]{1,2,0:T(4,128)S(1)} %bitcast.65) | data formatting | bytes 122880 | tf_op jit(solution)/shard_map/reshape | solution.py:651
  50.5 12.6 %shard_map.97 = f32[3,5,2,96,192]{4,3,2,1,0:T(8,128)} custom-call(s32[3,6,2]{2,1,0:T(8,128)S(1)} %copy.56.centres, s32[6]{0:T(128)S(1)} %copy-done.5, f32[5]{0:T(128)S(1)} %copy-done.2, f32[5]{0:T(128)S(1)} %copy-done.4, f32[30,2,128,128]{3,2,1,0:T(8,128)} %get-tuple-element.7.x_hbm, f32[30,4,256]{2,1,0:T(4,128)S(1)} %bitcast.56, f32[30,128,4]{2,1,0:T(8,128)} %copy.57.we_ref), custom_call_target="tpu_custom_call" | custom-call | tf_op jit(solution)/shard_map/pallas_call | solution.py:557
  (32 shorter events, 0.8 us)
Async XLA Ops:
  5.1 1.0 %copy-start = (f32[5,2,64,128]{3,2,1,0:T(8,128)S(1)}, f32[5,2,64,128]{3,2,1,0:T(8,128)}, u32[]{:S(2)}) copy-start(f32[5,2,64,128]{3,2,1,0:T(8,128)} %param.8) | copy-start | bytes 983044
  6.0 0.7 %copy-start.1 = (f32[5]{0:T(128)S(1)}, f32[5]{0:T(128)}, u32[]{:S(2)}) copy-start(f32[5]{0:T(128)} %lateral.1) | copy-start | bytes 64
  6.7 0.7 %copy-start.3 = (f32[5]{0:T(128)S(1)}, f32[5]{0:T(128)}, u32[]{:S(2)}) copy-start(f32[5]{0:T(128)} %vertical.1) | copy-start | bytes 64
  33.0 17.5 %copy-start.2 = (f32[5]{0:T(128)S(1)}, f32[5]{0:T(128)}, u32[]{:S(2)}) copy-start(f32[5]{0:T(128)} %lateral.1) | copy-start | bytes 64
  33.0 17.5 %copy-start.4 = (f32[5]{0:T(128)S(1)}, f32[5]{0:T(128)}, u32[]{:S(2)}) copy-start(f32[5]{0:T(128)} %vertical.1) | copy-start | bytes 64
  33.0 17.5 %copy-start.5 = (s32[6]{0:T(128)S(1)}, s32[6]{0:T(128)}, u32[]{:S(2)}) copy-start(s32[6]{0:T(128)} %storms.1) | copy-start | bytes 76

commit v6 on v5

--- a/solution.py
+++ b/solution.py
@@ -20,7 +20,7 @@
 MESH = pl.DeviceIdType.MESH
 
 
-def halo_kernel(counts, p_hbm, n_hbm, lat_ref, ver_ref, stage_ref, w_hbm,
+def halo_kernel(counts, p_hbm, n_hbm, rates, stage_ref, w_hbm,
                 p_ref, n_ref, w_ref, load, field, side, pack, held, cols_out, cols_in, send, recv):
     tiles, groups, levs = counts
     tile_at = lax.axis_index("tile")
@@ -182,8 +182,8 @@
     domain = (x >= 0) & (x < prow * tiles) & (y >= 0) & (y < pcol * groups * levs)
 
     def advance(i, carry):
-        rate_l = lat_ref[i]
-        rate_v = ver_ref[i]
+        rate_l = rates[0, i]
+        rate_v = rates[1, i]
         now = [jnp.concatenate([field[2 * i + v], side[2 * i + v]], axis=1) for v in range(2)]
         for step in range(2):
             later = []
@@ -226,7 +226,7 @@
     tail.wait()
 
 
-def exchange_halos(parent, nests, lateral, vertical, counts):
+def exchange_halos(parent, nests, rates, counts):
     planes, prow, pcol = parent.shape
     blocks, rows, cols = nests.shape
     assert pcol == LANES and planes % 2 == 0 and blocks % 2 == 0 and 2 * (cols - LANES) == LANES
@@ -241,7 +241,7 @@
             shape(2, planes, prow, pcol),
             shape(blocks, 2, rows + 2 * HALO, LANES),
         ),
-        in_specs=[anywhere, anywhere, smem, smem],
+        in_specs=[anywhere, anywhere, smem],
         out_specs=(vmem, anywhere),
         scratch_shapes=[
             pltpu.VMEM((planes, prow, pcol), jnp.float32),
@@ -260,7 +260,7 @@
         compiler_params=pltpu.CompilerParams(
             collective_id=1, has_side_effects=True, vmem_limit_bytes=52 * 1024 * 1024
         ),
-    )(parent, nests, lateral, vertical)
+    )(parent, nests, rates)
 
 
 def zone_kernel(counts, we_ref, sn_ref, we_out, sn_out, we_sum, sn_sum, we_in, sn_in,
@@ -397,7 +397,7 @@
     )(we, sn)
 
 
-def nest_kernel(shape, steps, centres, storms, lateral, vertical, x_hbm, sn_ref, we_ref, o_hbm,
+def nest_kernel(shape, steps, centres, storms, rates, x_hbm, sn_ref, we_ref, o_hbm,
                 x_ref, relaxed, state, done, col_mix, row_mix, load, sem):
     slots, fields, levels, rows, cols = shape
     planes = fields * levels
@@ -499,8 +499,8 @@
                 relaxed[f * levels + v, side, edge : edge + mid] = patched(halves[side], blend)
 
         def diffuse(f, v):
-            rate_l = lateral[f]
-            rate_v = vertical[f]
+            rate_l = rates[0, f]
+            rate_v = rates[1, f]
             keep_rate = 1.0 - 4.0 * rate_l - 2.0 * rate_v
             p = f * levels + v
             here = [relaxed[p, side, edge : edge + mid] for side in range(2)]
@@ -549,7 +549,7 @@
         pltpu.make_async_copy(done.at[n], o_hbm.at[n], sem.at[n]).wait()
 
 
-def advance_nests(wide_nests, along, across, centres, storms, lateral, vertical, shape, steps):
+def advance_nests(wide_nests, along, across, centres, storms, rates, shape, steps):
     slots, fields, levels, rows, cols = shape
     high = wide_nests.shape[2]
     vmem = pl.BlockSpec(memory_space=pltpu.VMEM)
@@ -557,7 +557,7 @@
     return pl.pallas_call(
         functools.partial(nest_kernel, shape, steps),
         out_shape=jax.ShapeDtypeStruct(shape, jnp.float32),
-        in_specs=[smem] * 4 + [pl.BlockSpec(memory_space=pl.ANY)] + [vmem] * 2,
+        in_specs=[smem] * 3 + [pl.BlockSpec(memory_space=pl.ANY)] + [vmem] * 2,
         out_specs=pl.BlockSpec(memory_space=pl.ANY),
         scratch_shapes=[
             pltpu.VMEM(wide_nests.shape, jnp.float32),
@@ -569,8 +569,8 @@
             pltpu.SemaphoreType.DMA((slots,)),
             pltpu.SemaphoreType.DMA((slots,)),
         ],
-        compiler_params=pltpu.CompilerParams(vmem_limit_bytes=52 * 1024 * 1024),
-    )(centres, storms, lateral, vertical, wide_nests, along, across)
+        compiler_params=pltpu.CompilerParams(vmem_limit_bytes=50 * 1024 * 1024),
+    )(centres, storms, rates, wide_nests, along, across)
 
 
 def per_device(parent_field, nest_fields, lateral_rate, vertical_rate, centres, slot_storm):
@@ -589,11 +589,11 @@
 
     counts = (tiles, groups, levs)
     planes = fields * levels
+    rates = jnp.stack([lateral_rate, vertical_rate])
     stages, wide_nests = exchange_halos(
         parent_field.reshape(planes, prow, pcol),
         nest_fields.reshape(slots * planes, rows, cols),
-        lateral_rate,
-        vertical_rate,
+        rates,
         counts,
     )
     high = wide_nests.shape[2]
@@ -655,8 +655,7 @@
         across,
         centres,
         slot_storm,
-        lateral_rate,
-        vertical_rate,
+        rates,
         nest_fields.shape,
         steps,
     )

time: 63.4 us -> 60.6 us (0.956)
  local copies, waits for them, and re-layouts: 7.67 us -> 5.04 us
  Pallas kernels: 45.7 us -> 44.9 us
  other arithmetic: 3.15 us -> 3.83 us
    unnamed x13 -> x5, local copies, waits for them, and re-layouts: 3.08 us -> 1.76 us
    reshape x1, local copies, waits for them, and re-layouts: 1.91 us -> 0.6 us  [per_device(): jnp.transpose(across, (1, 4, 5, 0, 3, 2))]
    pallas_call x1, Pallas kernels: 12.6 us -> 11.8 us  [advance_nests(): pl.pallas_call(functools.partial(nest_kernel, shape, steps), out_shape=ja...]
    another operation x1 -> x2, other arithmetic: 0.01 us -> 0.69 us  [the longest x1 0.68 us: per_device(): rates = jnp.stack([lateral_rate, vertical_rate])]
where the time goes in v6:
time: 60.6 us; the launch traced here: 60.3 us
  Pallas kernels  44.9 us (74%)
  matrix products  5.71 us (9%)
  local copies, waits for them, and re-layouts  5.04 us (8%)
  other arithmetic  3.83 us (6%)
  between operations  0.86 us (1%)
    pallas_call x1, Pallas kernels, exchange_halos(): pl.pallas_call(functools.partial(halo_kernel, counts), out_shape=(shape(2...  18.8 us
    pallas_call x1, Pallas kernels, sum_zones(): pl.pallas_call(functools.partial(zone_kernel, counts), out_shape=(jax.Sha...  14.3 us
    pallas_call x1, Pallas kernels, advance_nests(): pl.pallas_call(functools.partial(nest_kernel, shape, steps), out_shape=ja...  11.8 us
    dot_general x1, matrix products, per_device(): we = jnp.einsum('sjtrx,sjkfx->sjtrkf', row_pick, we, precision=EXACT)  2.43 us
    unnamed x5, local copies, waits for them, and re-layouts  1.76 us
    dot_general x1, matrix products, per_device(): sn = jnp.einsum('sgnhkfy,sgnlyc->lhgskfc', sn, col_pick, precision=EXACT)  1.26 us

profile of v6, /device:TPU:0, one launch (start us, length us, event | category | flops | bytes accessed | tf_op | source)
XLA Modules:
  0.0 60.3 jit_solution(11353287904781974741)
XLA Ops:
  0.7 0.7 %pad_maximum_fusion.rates = f32[2,5]{1,0:T(2,128)S(1)} fusion(f32[1,5]{1,0:T(1,128)} %bitcast.68, f32[1,5]{1,0:T(1,128)} %bitcast.69), kind=kLoop, calls=%fused_computation.67 | loop fusion | flops 10 | bytes 80 | tf_op jit(solution)/shard_map/stack | solution.py:592
  1.6 0.7 %fusion.30 = s32[6,6]{1,0:T(8,128)S(1)} fusion(s32[6]{0:T(128)} %storms.1), kind=kLoop, calls=%fused_computation.42 | loop fusion | flops 72 | bytes 168 | tf_op jit(solution)/shard_map/convert_element_type | solution.py:605
  2.4 1.1 %multiply_reduce_fusion = s32[3,6,2]{2,1,0:T(8,128)S(1)} fusion(s32[3,6,2]{1,2,0:T(2,128)} %param.12, s32[6,6]{1,0:T(8,128)S(1)} %fusion.30), kind=kLoop, calls=%fused_computation.31 | loop fusion | flops 396 | bytes 432 | tf_op jit(solution)/shard_map/reduce_sum | solution.py:606
  3.5 0.2 slice_reduce_fusion
  3.7 0.1 add.225
  3.8 0.7 %broadcast_add_fusion.2 = (s32[2,6,4]{1,2,0:T(4,128)S(1)}, s32[2,6,4]{1,2,0:T(4,128)S(1)}) fusion(s32[2,6]{1,0:T(2,128)S(1)} %get-tuple-element.11, s32[4]{0:T(128)} %constant.83.clone, s32[2,6]{1,0:T(2,128)S(1)} %get-tuple-element.10), kind=kLoop, calls=%fused_computation.47 | loop fusion | flops 96 | bytes 496 | tf_op jit(solution)/shard_map/add | solution.py:620
  4.6 0.1 copy.45
  4.7 0.8 %copy.56.centres = s32[3,6,2]{2,1,0:T(8,128)S(1)} copy(s32[3,6,2]{1,2,0:T(2,128)} %param.12) | data formatting | bytes 288 | tf_op args[4]
  5.6 0.1 broadcast_compare_fusion
  5.8 1.0 %copy-done = f32[5,2,64,128]{3,2,1,0:T(8,128)S(1)} copy-done((f32[5,2,64,128]{3,2,1,0:T(8,128)S(1)}, f32[5,2,64,128]{3,2,1,0:T(8,128)}, u32[]{:S(2)}) %copy-start) | copy-done | bytes 327704
  6.7 18.8 %shard_map.95 = (f32[2,10,64,128]{3,2,1,0:T(8,128)S(1)}, f32[30,2,128,128]{3,2,1,0:T(8,128)}) custom-call(f32[10,64,128]{2,1,0:T(8,128)S(1)} %bitcast.59, f32[30,96,192]{2,1,0:T(8,128)} %bitcast.62, f32[2,5]{1,0:T(2,128)S(1)} %pad_maximum_fusion.rates), custom_call_target="tpu_custom_call" | custom-call | tf_op jit(solution)/shard_map/pallas_call | solution.py:238
  25.5 0.4 fusion.12
  25.9 0.9 %convolution_bitcast_fusion = f32[2,6,4,10,64,1]{4,2,3,1,0,5:T(4,128)S(1)} fusion(f32[2,10,64,128]{3,2,1,0:T(8,128)S(1)} %get-tuple-element.6, s32[128]{0:T(128)S(1)} %iota_add_fusion.4, s32[2,6,4]{2,1,0:T(8,128)S(1)} %copy.45), kind=kOutput, calls=%fused_computation.6 | convolution fusion | flops 47192064 | bytes 778944 | tf_op jit(solution)/shard_map/sjky,sfxy->sjkfx/dot_general | solution.py:629
  26.8 0.8 %slice.16 = f32[1,10,64,128]{3,2,1,0:T(8,128)} slice(f32[2,10,64,128]{3,2,1,0:T(8,128)S(1)} %get-tuple-element.6), slice={[1:2], [0:10], [0:64], [0:128]} | slice | bytes 655360 | tf_op jit(solution)/shard_map/slice | solution.py:662
  27.5 1.3 %fusion.5 = f32[2,2,2,2,2,10,256]{6,5,4,1,0,3,2:T(8,128)S(1)} fusion(s32[2,2,3,2,256]{4,2,3,0,1:T(4,128)S(1)} %broadcast_add_fusion, s32[128]{0:T(128)S(1)} %iota_add_fusion.4, f32[2,2,3,2,2,10,128,1]{6,4,3,5,2,1,0,7:T(2,128)S(1)} %bitcast.66), kind=kOutput, calls=%fused_computation.5 | convolution fusion | flops 378273792 | bytes 598528 | tf_op jit(solution)/shard_map/sgnhkfy,sgnlyc->lhgskfc/dot_general | solution.py:627
  28.8 0.3 copy.52
  29.1 2.4 %fusion.8 = f32[2,6,4,40,4,10]{3,5,4,2,1,0:T(8,128)S(1)} fusion(s32[64]{0:T(128)S(1)} %iota_add_fusion.5, s32[2,6,4,40]{3,2,1,0:T(4,128)S(1)} %broadcast_add_fusion.1, f32[2,6,4,10,64,1]{4,2,3,1,0,5:T(4,128)S(1)} %convolution_bitcast_fusion), kind=kOutput, calls=%fused_computation.8 | convolution fusion | flops 59105280 | bytes 438016 | tf_op jit(solution)/shard_map/sjtrx,sjkfx->sjtrkf/dot_general | solution.py:630
  31.5 0.8 %copy.47 = f32[2,2,3,4,40,2,2,10]{4,1,3,7,0,6,2,5:T(2,128)S(1)} copy(f32[2,2,3,4,40,2,2,10]{4,7,6,5,3,2,1,0:T(8,128)S(1)} %bitcast.60) | data formatting | bytes 614400 | tf_op jit(solution)/shard_map/reshape | solution.py:631
  32.3 0.3 copy.48
  32.7 14.3 %shard_map.96 = (f32[40,128]{1,0:T(8,128)S(1)}, f32[40,256]{1,0:T(8,128)S(1)}) custom-call(f32[2,8,40,128]{3,2,1,0:T(8,128)S(1)} %pad.4.we_ref, f32[2,4,40,256]{3,2,1,0:T(8,128)S(1)} %copy.53.sn_ref), custom_call_target="tpu_custom_call" | custom-call | tf_op jit(solution)/shard_map/pallas_call | solution.py:374
  47.0 0.5 convolution_bitcast_fusion.1
  47.6 0.3 fusion.21
  47.9 0.6 copy.57.we_ref
  48.5 11.8 %shard_map.97 = f32[3,5,2,96,192]{4,3,2,1,0:T(8,128)} custom-call(s32[3,6,2]{2,1,0:T(8,128)S(1)} %copy.56.centres, s32[6]{0:T(128)S(1)} %copy-done.1, f32[2,5]{1,0:T(2,128)S(1)} %pad_maximum_fusion.rates, f32[30,2,128,128]{3,2,1,0:T(8,128)} %get-tuple-element.7.x_hbm, f32[30,4,256]{2,1,0:T(4,128)S(1)} %bitcast.58, f32[30,128,4]{2,1,0:T(8,128)S(1)} %copy.57.we_ref), custom_call_target="tpu_custom_call" | custom-call | tf_op jit(solution)/shard_map/pallas_call | solution.py:557
  (25 shorter events, 0.7 us)
Async XLA Ops:
  5.7 1.0 %copy-start = (f32[5,2,64,128]{3,2,1,0:T(8,128)S(1)}, f32[5,2,64,128]{3,2,1,0:T(8,128)}, u32[]{:S(2)}) copy-start(f32[5,2,64,128]{3,2,1,0:T(8,128)} %param.8) | copy-start | bytes 983044
  32.3 16.2 %copy-start.1 = (s32[6]{0:T(128)S(1)}, s32[6]{0:T(128)}, u32[]{:S(2)}) copy-start(s32[6]{0:T(128)} %storms.1) | copy-start | bytes 76
